TPU v7x, 32 devices: a whole 2x2x4 slice. The times are simulated.
32 devices in a mesh: gx: 8 (over z, y), gy: 4 (over x, core).
Axes of the slice: x: 2, y: 2, z: 4, core: 2. Of those that a mesh axis runs over, the one named last changes fastest.
Arguments:
- features: bfloat16 [256, 64, 512], P(('gx', 'gy')), may hold values from -6 to 6
- neighbours: int32 [256, 6], P(('gx', 'gy')), may hold values from 0 to 16, as said below
- counts: int32 [32], P(('gx', 'gy')), may hold values from 1 to 8, as said below
- conv_weight: bfloat16 [64, 448], replicated, may hold values from -0.25 to 0.25
- down_weight: bfloat16 [128, 512], replicated, may hold values from -0.25 to 0.25
- head_weight: bfloat16 [128, 128], replicated, may hold values from -0.5 to 0.5
- coarse_map: int32 [32, 8], P(('gx', 'gy')), may hold values from 0 to 32, as said below
- latent_grad: bfloat16 [32, 512, 128], P(('gx', 'gy')), may hold values from -6 to 6
Outputs:
- latent: bfloat16 [32, 512, 128], P(('gx', 'gy'))
- features_grad: bfloat16 [256, 64, 512], P(('gx', 'gy'))
- conv_grad: float32 [64, 448], replicated
- down_grad: float32 [128, 512], replicated
- head_grad: float32 [128, 128], replicated
Inputs may be any that keep to these rules, and one draw needn't show every extreme that they name: `counts`: in every draw, max(1, (devices along gx times devices along gy) // 8) columns have exactly 8 active blocks; each other column has between 1 and 4. 16 means no neighbour; a value below 8 is an active slot of the same column; a value v of 8 or more is the active slot v - 8 of the adjacent column in that direction; the z directions never name another column; inactive slots have no neighbours. `coarse_map`: 32 marks an empty octant; every other entry names an active block's octant, and each such octant is named at most once among the four columns that share a merged list.
All inputs are finite; a program needn't handle non-finite values.
Results may differ from a plain program's by a relative error of at most 0.013.
Values may be sent and summed in bfloat16 or wider, within the bound.
No kernel may reach another device: no remote copies, remote signals or barrier semaphores. Data moves between devices by JAX's collectives and lax.ppermute only.
A program may use at most 128 MiB of HBM per device.

v0:
```python
import jax
import jax.numpy as jnp
from jax import lax
from jax.sharding import PartitionSpec as P


def from_partner(block, axis, distance):
    count = lax.axis_size(axis)
    route = []
    for low in range(count):
        high = low | 1 << distance
        if high != low and high < count:
            route += [(low, high), (high, low)]
    return lax.ppermute(block, axis, route)


def padded(block, sides, width):
    for axis, dim in sides:
        count = lax.axis_size(axis)
        forward = [(i, i + 1) for i in range(count - 1)]
        backward = [(target, source) for source, target in forward]
        low = lax.ppermute(
            lax.slice_in_dim(block, block.shape[dim] - width, None, axis=dim), axis, forward
        )
        high = lax.ppermute(lax.slice_in_dim(block, 0, width, axis=dim), axis, backward)
        block = jnp.concatenate([low, block, high], axis=dim)
    return block


def silu_grad(values):
    sigmoid_value = jax.nn.sigmoid(values)
    return sigmoid_value * (1.0 + values * (1.0 - sigmoid_value))


def octet(volume):
    return volume.reshape(volume.shape[0], volume.shape[1], 2, 2, 2, 4, 4, 4)


def face_of(cube, axis_number, upper):
    number, channels = (cube.shape[0], cube.shape[1])
    plane = lax.index_in_dim(cube, 3 if upper else 0, 5 + axis_number, keepdims=False)
    plane = lax.index_in_dim(plane, 1 if upper else 0, 2 + axis_number, keepdims=False)
    return plane.reshape(number, channels * 64)


def face_index(axis_number, upper):
    index = [slice(None)] * 8
    index[2 + axis_number] = 1 if upper else 0
    index[5 + axis_number] = 3 if upper else 0
    return tuple(index)


def expand_plane(rows, cube, axis_number):
    number, channels = (cube.shape[0], cube.shape[1])
    return jnp.expand_dims(
        rows.reshape(number, channels, 2, 2, 4, 4), (2 + axis_number, 5 + axis_number)
    )


def shift_minus(cube, rows, axis_number):
    parity, place = (2 + axis_number, 5 + axis_number)
    plane = expand_plane(rows, cube, axis_number)
    lower = lax.slice_in_dim(cube, 0, 1, axis=parity)
    upper = lax.slice_in_dim(cube, 1, 2, axis=parity)
    out_low = jnp.concatenate([plane, lax.slice_in_dim(upper, 0, 3, axis=place)], axis=place)
    return jnp.concatenate([out_low, lower], axis=parity)


def shift_plus(cube, rows, axis_number):
    parity, place = (2 + axis_number, 5 + axis_number)
    plane = expand_plane(rows, cube, axis_number)
    lower = lax.slice_in_dim(cube, 0, 1, axis=parity)
    upper = lax.slice_in_dim(cube, 1, 2, axis=parity)
    out_high = jnp.concatenate([lax.slice_in_dim(lower, 1, 4, axis=place), plane], axis=place)
    return jnp.concatenate([upper, out_high], axis=parity)


def minus_back(grad_out, axis_number):
    parity, place = (2 + axis_number, 5 + axis_number)
    grad_low = lax.slice_in_dim(grad_out, 0, 1, axis=parity)
    grad_high = lax.slice_in_dim(grad_out, 1, 2, axis=parity)
    moved = jnp.concatenate(
        [
            lax.slice_in_dim(grad_low, 1, 4, axis=place),
            jnp.zeros_like(lax.slice_in_dim(grad_low, 0, 1, axis=place)),
        ],
        axis=place,
    )
    plane = lax.index_in_dim(
        lax.index_in_dim(grad_low, 0, place, keepdims=False), 0, parity, keepdims=False
    )
    return (jnp.concatenate([grad_high, moved], axis=parity), plane)


def plus_back(grad_out, axis_number):
    parity, place = (2 + axis_number, 5 + axis_number)
    grad_low = lax.slice_in_dim(grad_out, 0, 1, axis=parity)
    grad_high = lax.slice_in_dim(grad_out, 1, 2, axis=parity)
    moved = jnp.concatenate(
        [
            jnp.zeros_like(lax.slice_in_dim(grad_high, 0, 1, axis=place)),
            lax.slice_in_dim(grad_high, 0, 3, axis=place),
        ],
        axis=place,
    )
    plane = lax.index_in_dim(
        lax.index_in_dim(grad_high, 3, place, keepdims=False), 0, parity, keepdims=False
    )
    return (jnp.concatenate([moved, grad_low], axis=parity), plane)


def face_layers(cube):
    return (
        face_of(cube, 0, True),
        face_of(cube, 0, False),
        face_of(cube, 1, True),
        face_of(cube, 1, False),
        face_of(cube, 2, True),
        face_of(cube, 2, False),
    )


def pick_rows(local_rows, remote_rows, index):
    width = local_rows.shape[1]
    pooled = jnp.concatenate(
        [local_rows, remote_rows, jnp.zeros((1, width), local_rows.dtype)], axis=0
    )
    return pooled[index]


def neighbour_stack(cube, faces, remotes, links):
    number, channels = (cube.shape[0], cube.shape[1])
    blank = jnp.zeros_like(faces[4])
    sources = (remotes[0], remotes[1], remotes[2], remotes[3], blank, blank)
    picked = [
        pick_rows(faces[direction], sources[direction], links[:, direction])
        for direction in range(6)
    ]
    fields = [
        cube,
        shift_minus(cube, picked[0], 0),
        shift_plus(cube, picked[1], 0),
        shift_minus(cube, picked[2], 1),
        shift_plus(cube, picked[3], 1),
        shift_minus(cube, picked[4], 2),
        shift_plus(cube, picked[5], 2),
    ]
    return jnp.stack(fields, axis=1).reshape(number, 7 * channels, 512)


def stack_grad(taps_grad, links):
    number, channels = (taps_grad.shape[0], taps_grad.shape[1] // 7)
    parts = taps_grad.reshape(number, 7, channels, 2, 2, 2, 4, 4, 4)
    grad_cube = parts[:, 0]
    face_grads = []
    for direction in range(6):
        axis_number = direction // 2
        if direction % 2 == 0:
            moved, plane = minus_back(parts[:, direction + 1], axis_number)
        else:
            moved, plane = plus_back(parts[:, direction + 1], axis_number)
        grad_cube = grad_cube + moved
        face_grads.append(plane.reshape(number, channels * 64))
    pools = [
        jnp.zeros((2 * number + 1, channels * 64), jnp.float32)
        .at[links[:, direction]]
        .add(face_grads[direction])
        for direction in range(6)
    ]
    for direction in range(6):
        shaped = pools[direction][:number].reshape(number, channels, 2, 2, 4, 4)
        grad_cube = grad_cube.at[face_index(direction // 2, direction % 2 == 0)].add(shaped)
    far_rows = [
        pools[direction][number : 2 * number].astype(jnp.bfloat16) for direction in range(4)
    ]
    return (grad_cube, far_rows)


def add_faces(grad_cube, into_xhigh, into_xlow, into_yhigh, into_ylow):
    number, channels = (grad_cube.shape[0], grad_cube.shape[1])

    def planes(rows):
        return rows.astype(jnp.float32).reshape(number, channels, 2, 2, 4, 4)

    grad_cube = grad_cube.at[face_index(0, True)].add(planes(into_xhigh))
    grad_cube = grad_cube.at[face_index(0, False)].add(planes(into_xlow))
    grad_cube = grad_cube.at[face_index(1, True)].add(planes(into_yhigh))
    grad_cube = grad_cube.at[face_index(1, False)].add(planes(into_ylow))
    return grad_cube


def merge_pool(own_rows):
    beside_y = from_partner(own_rows, "gy", 0)
    received = from_partner(jnp.concatenate([own_rows, beside_y], axis=0), "gx", 0)
    half = own_rows.shape[0]
    return jnp.concatenate([own_rows, received[:half], beside_y, received[half:]], axis=0)


def split_pool(back_rows):
    half = back_rows.shape[0] // 4
    own_part = back_rows[:half].astype(jnp.float32)
    along_x = back_rows[half : 2 * half]
    along_y = back_rows[2 * half : 3 * half]
    diagonal = back_rows[3 * half :]
    returned = from_partner(jnp.concatenate([along_x, diagonal], axis=0), "gx", 0)
    kept = own_part + returned[:half].astype(jnp.float32)
    beside = (along_y.astype(jnp.float32) + returned[half:].astype(jnp.float32)).astype(
        jnp.bfloat16
    )
    final_rows = kept + from_partner(beside, "gy", 0).astype(jnp.float32)
    return final_rows.astype(jnp.bfloat16)


def scatter_rows(volume, links, number):
    width = volume.shape[1] * volume.shape[2] // 8
    rows = volume.reshape(volume.shape[0] * 8, width)
    total = (
        jnp.zeros((4 * number + 1, width), jnp.float32)
        .at[links.reshape(-1)]
        .add(rows.astype(jnp.float32))
    )
    return total[: 4 * number].astype(jnp.bfloat16)


def body(
    features, neighbours, counts, conv_weight, down_weight, head_weight, coarse_map, latent_grad
):
    number, channels = (features.shape[0], features.shape[1])
    wide = down_weight.shape[0]
    coarse_count = coarse_map.shape[0]
    active = jnp.arange(number) < counts[0]
    masked = jnp.where(active[:, None, None], features, jnp.zeros((), jnp.bfloat16))
    cube = octet(masked)
    faces = face_layers(cube)
    rim_x = padded(jnp.stack([faces[1], faces[0]]), (("gx", 0),), 1)
    rim_y = padded(jnp.stack([faces[3], faces[2]]), (("gy", 0),), 1)
    taps = neighbour_stack(cube, faces, (rim_x[0], rim_x[3], rim_y[0], rim_y[3]), neighbours)
    hidden = jnp.einsum("ok,bkv->bov", conv_weight, taps, preferred_element_type=jnp.float32)
    act = jax.nn.silu(hidden).astype(jnp.bfloat16)
    patches = act.reshape(number, channels * 8, 64)
    octants = jnp.einsum(
        "ok,bkv->bvo", down_weight, patches, preferred_element_type=jnp.float32
    ).astype(jnp.bfloat16)
    empty_row = jnp.zeros((1, 64 * wide), jnp.bfloat16)
    octant_act = jax.nn.silu(octants.astype(jnp.float32)).astype(jnp.bfloat16)
    projected = jnp.einsum(
        "oi,bvi->bvo", head_weight, octant_act, preferred_element_type=jnp.float32
    ).astype(jnp.bfloat16)
    merged = merge_pool(projected.reshape(number, 64 * wide))
    latent = jnp.concatenate([merged, empty_row], axis=0)[coarse_map].reshape(
        coarse_count, 512, wide
    )
    routed_grad = split_pool(scatter_rows(latent_grad, coarse_map, number)).reshape(
        number, 64, wide
    )
    act_grad = jnp.einsum(
        "oi,bvo->bvi", head_weight, routed_grad, preferred_element_type=jnp.float32
    )
    octant_grad = (act_grad * silu_grad(octants.astype(jnp.float32))).astype(jnp.bfloat16)
    head_part = jnp.einsum(
        "bvo,bvi->oi", routed_grad, octant_act, preferred_element_type=jnp.float32
    )
    down_part = jnp.einsum("bvo,bkv->ok", octant_grad, patches, preferred_element_type=jnp.float32)
    patch_grad = jnp.einsum(
        "ok,bvo->bkv", down_weight, octant_grad, preferred_element_type=jnp.float32
    )
    hidden_grad = (patch_grad.reshape(number, channels, 512) * silu_grad(hidden)).astype(
        jnp.bfloat16
    )
    conv_part = jnp.einsum("bov,bkv->ok", hidden_grad, taps, preferred_element_type=jnp.float32)
    taps_grad = jnp.einsum(
        "ok,bov->bkv", conv_weight, hidden_grad, preferred_element_type=jnp.float32
    )
    near_grad, far_rows = stack_grad(taps_grad, neighbours)
    return_x = padded(jnp.stack([far_rows[0], far_rows[1]]), (("gx", 0),), 1)
    return_y = padded(jnp.stack([far_rows[2], far_rows[3]]), (("gy", 0),), 1)
    total_grad = add_faces(near_grad, return_x[3], return_x[0], return_y[3], return_y[0]).reshape(
        number, channels, 512
    )
    features_grad = jnp.where(active[:, None, None], total_grad, 0.0).astype(jnp.bfloat16)
    summed = lax.psum((conv_part, down_part, head_part), ("gx", "gy"))
    scale = float(number * lax.axis_size("gx") * lax.axis_size("gy")) ** (-0.5)
    return (latent, features_grad, summed[0] * scale, summed[1] * scale, summed[2] * scale)


def solution(mesh):
    placed = (
        P(("gx", "gy"), None, None),
        P(("gx", "gy"), None),
        P(("gx", "gy")),
        P(),
        P(),
        P(),
        P(("gx", "gy"), None),
        P(("gx", "gy"), None, None),
    )
    return jax.shard_map(
        body,
        mesh=mesh,
        in_specs=placed,
        out_specs=(P(("gx", "gy"), None, None), P(("gx", "gy"), None, None), P(), P(), P()),
        check_vma=False,
    )
```

profile of v0, /device:TPU:0, one launch (start us, length us, event | category | flops | bytes accessed | tf_op | source)
XLA Modules:
  0.0 462.5 jit_solution(12513185669417528039)
XLA Ops:
  11.0 3.0 collective-permute-start.6
  18.2 2.5 collective-permute-start
  25.3 3.1 copy.125
  33.4 3.1 copy.132
  92.6 11.2 %copy.149 = bf16[8,7,64,2,2,2,4,4,4]{2,1,8,7,6,5,4,3,0:T(8,128)(2,1)} copy(bf16[8,7,64,2,2,2,4,4,4]{2,0,8,7,6,5,4,3,1:T(8,128)(2,1)} %fusion.15) | data formatting | bytes 7340032 | tf_op jit(solution)/shard_map/stack | solution.py:148
  103.8 11.7 %reshape.689 = bf16[8,448,512]{1,2,0:T(8,128)(2,1)} reshape(bf16[8,7,64,2,2,2,4,4,4]{2,1,8,7,6,5,4,3,0:T(8,128)(2,1)} %copy.149) | data formatting | bytes 7340032 | tf_op jit(solution)/shard_map/reshape | solution.py:148
  115.6 4.6 multiply_convert_fusion.1
  122.2 2.6 collective-permute-start.4
  127.3 2.6 collective-permute-start.5
  136.0 3.7 convolution_bitcast_fusion.4
  139.7 4.1 convolution_bitcast_fusion
  143.8 8.8 %copy.153 = f32[8,448,512]{1,2,0:T(8,128)} copy(f32[8,448,512]{2,1,0:T(8,128)} %convolution_bitcast_fusion) | data formatting | bytes 14680064 | tf_op jit(solution)/shard_map/ok,bov->bkv/transpose | solution.py:271
  152.6 13.1 %reshape.696 = f32[8,7,64,2,2,2,4,4,4]{2,1,8,7,6,5,4,3,0:T(8,128)} reshape(f32[8,448,512]{1,2,0:T(8,128)} %copy.153) | data formatting | bytes 14680064 | tf_op jit(solution)/shard_map/reshape | solution.py:153
  165.8 53.3 %fusion.61 = (f32[8,1,64,2,2,2,4,4,4]{2,1,8,7,6,5,4,3,0:T(1,128)S(1)}, f32[8,1,64,2,2,2,4,4,4]{2,1,8,7,6,5,4,3,0:T(1,128)S(1)}, f32[8,1,64,2,2,2,4,4,4]{2,1,8,7,...) fusion(f32[8,7,64,2,2,2,4,4,4]{2,1,8,7,6,5,4,3,0:T(8,128)} %res, ...), kind=kLoop, calls=%fused_computation.165 | loop fusion | bytes 14680064 | tf_op jit(solution)/shard_map/slice | solution.py:159
  235.2 3.1 copy.164
  240.6 3.6 copy.168
  247.9 3.1 copy.160
  254.9 3.1 copy.172
  261.8 3.1 copy.176
  272.6 2.5 collective-permute-start.9
  277.7 3.7 collective-permute-start.11
  299.1 6.2 %fusion = f32[8,64,2,2,2,4,4,4]{1,7,6,5,4,3,2,0:T(4,128)S(1)} fusion(f32[8,64,2,2,1,4,4,3]{1,7,6,5,4,3,2,0:T(4,128)} %slice.902, f32[8,64,2,2,1,4,4,3]{1,7,6,5,4,3,2,0:T(4,128)} %slice.900, f32[8,64,2,1,2,4,3,4]{1,7,6,5,4,3,2,0:T(4,128)} %slice.896, f32[8,64,2,1,2,4,3,4]{1,7,6,5,4,3,2,0:T(4,128)} %slice.894, f32[8,64,1,2,2,3,4,4]{1,7,6,5,4,3,2,0:T(4,128)} %slice.890, ...), kind=kLoop, calls=%fused_computation.16 | loop fusion | flops 6291456 | bytes 7602176 | tf_op jit(solution)/shard_map/add | solution.py:162
  306.6 5.5 %scatter-add.109 = f32[8,64,2,2,2,4,4,4]{1,7,6,5,4,3,2,0:T(4,128)S(1)} dynamic-update-slice(f32[8,64,2,2,2,4,4,4]{1,7,6,5,4,3,2,0:T(4,128)S(1)} %fusion.22, f32[8,64,2,2,1,4,4,1]{1,7,6,5,4,3,2,0:T(1,128)S(1)} %slice_add_fusion.5, s32[]{:T(128)} %constant.277.clone.1, s32[]{:T(128)} %constant.277.clone.1, s32[]{:T(128)} %constant.277.clone.1, s32[]{:T(128)} %constant.277.clone.1, ...) | dynamic-update-slice | bytes 262148 | tf_op jit(solution)/shard_map/scatter-add | solution.py:172
  312.5 5.5 %scatter-add.111 = f32[8,64,2,2,2,4,4,4]{1,7,6,5,4,3,2,0:T(4,128)S(1)} dynamic-update-slice(f32[8,64,2,2,2,4,4,4]{1,7,6,5,4,3,2,0:T(4,128)S(1)} %scatter-add.109, f32[8,64,2,2,1,4,4,1]{1,7,6,5,4,3,2,0:T(1,128)S(1)} %slice_add_fusion.4, s32[]{:T(128)} %constant.277.clone.1, s32[]{:T(128)} %constant.277.clone.1, s32[]{:T(128)} %constant.277.clone.1, s32[]{:T(128)} %constant.277.clone.1, ...) | dynamic-update-slice | bytes 262148 | tf_op jit(solution)/shard_map/scatter-add | solution.py:172
  319.0 2.5 copy.190
  321.5 2.4 copy.191
  323.9 2.5 copy.184
  328.9 2.5 copy.188
  331.4 2.6 copy.189
  334.0 2.5 copy.186
  336.6 2.4 copy.187
  346.0 104.7 %all-reduce.9.cloned.1.call-done = (f32[64,448]{1,0:T(8,128)}, f32[128,512]{1,0:T(8,128)}, f32[128,128]{1,0:T(8,128)}) async-done(((f32[64,448]{1,0:T(8,128)}, f32[128,512]{1,0:T(8,128)}, f32[128,128]{1,0:T(8,128)}), (f32[64,448]{1,0:T(8,128)}, f32[128,512]{1,0:T(8,128)}, f32[128,128]{1,0:T(8,128)})) %all-reduce.9.cloned.1.call-update) | async-done | bytes 442384 | tf_op jit(solution)/shard_map/psum | solution.py:281
  (294 shorter events, 156.9 us)
Async XLA Ops:
  7.2 113.5 %copy-start = (bf16[128,512]{1,0:T(8,128)(2,1)S(1)}, bf16[128,512]{1,0:T(8,128)(2,1)}, u32[]{:S(2)}) copy-start(bf16[128,512]{1,0:T(8,128)(2,1)} %param.32) | copy-start | bytes 393220
  7.2 443.5 %all-reduce.9.cloned.1.call-start = ((), (), s32[]{:S(2)}) async-start(), calls=%async_computation | async-start | bytes 917504 | tf_op jit(solution)/shard_map/psum | solution.py:281
  8.9 5.8 %copy-start.22 = (bf16[8,64,512]{2,1,0:T(8,128)(2,1)S(1)}, bf16[8,64,512]{2,1,0:T(8,128)(2,1)}, u32[]{:S(2)}) copy-start(bf16[8,64,512]{2,1,0:T(8,128)(2,1)} %param.28) | copy-start | bytes 1572868
  10.2 4.4 copy-start.4
  11.0 113.9 %collective-permute-start.6 = (bf16[16,8192]{1,0:T(8,128)(2,1)}, bf16[16,8192]{1,0:T(8,128)(2,1)}, u32[]{:S(2)}, u32[]{:S(2)}) collective-permute-start(bf16[16,8192]{1,0:T(8,128)(2,1)} %pad_maximum_fusion.1), channel_id=1, source_target_pairs={{0,4},{4,0},{8,12},{12,8},{16,20},{20,16},{24,28},{28,24},{1,5},{5... | collective-permute-start | bytes 786440 | tf_op jit(solution)/shard_map/ppermute | solution.py:14
  18.2 48.9 %collective-permute-start = (bf16[1,8,4096]{2,1,0:T(8,128)(2,1)}, bf16[1,8,4096]{2,1,0:T(8,128)(2,1)}, u32[]{:S(2)}, u32[]{:S(2)}) collective-permute-start(bf16[1,8,4096]{2,1,0:T(8,128)(2,1)} %copy.113), channel_id=1, source_target_pairs={{0,4},{4,8},{8,12},{12,16},{16,20},{20,24},{24,28},{1,5},{5,9},{9,... | collective-permute-start | bytes 196616 | tf_op jit(solution)/shard_map/ppermute | solution.py:22
  23.3 43.8 %collective-permute-start.1 = (bf16[1,8,4096]{2,1,0:T(8,128)(2,1)}, bf16[1,8,4096]{2,1,0:T(8,128)(2,1)}, u32[]{:S(2)}, u32[]{:S(2)}) collective-permute-start(bf16[1,8,4096]{2,1,0:T(8,128)(2,1)} %copy.120), channel_id=1, source_target_pairs={{4,0},{8,4},{12,8},{16,12},{20,16},{24,20},{28,24},{5,1},{9,5},{13... | collective-permute-start | bytes 196616 | tf_op jit(solution)/shard_map/ppermute | solution.py:25
  28.5 12.0 %copy-start.48 = (s32[1,8]{1,0:T(1,128)S(1)}, s32[1,8]{1,0:T(1,128)}, u32[]{:S(2)}) copy-start(s32[1,8]{1,0:T(1,128)} %param.34) | copy-start | bytes 100
  30.6 36.6 %collective-permute-start.2 = (bf16[1,8,4096]{2,1,0:T(8,128)(2,1)}, bf16[1,8,4096]{2,1,0:T(8,128)(2,1)}, u32[]{:S(2)}, u32[]{:S(2)}) collective-permute-start(bf16[1,8,4096]{2,1,0:T(8,128)(2,1)} %copy.127), channel_id=1, source_target_pairs={{0,1},{1,2},{2,3},{4,5},{5,6},{6,7},{8,9},{9,10},{10,11},{12,13},{... | collective-permute-start | bytes 196616 | tf_op jit(solution)/shard_map/ppermute | solution.py:22
  38.6 28.6 %collective-permute-start.3 = (bf16[1,8,4096]{2,1,0:T(8,128)(2,1)}, bf16[1,8,4096]{2,1,0:T(8,128)(2,1)}, u32[]{:S(2)}, u32[]{:S(2)}) collective-permute-start(bf16[1,8,4096]{2,1,0:T(8,128)(2,1)} %copy.134), channel_id=1, source_target_pairs={{1,0},{2,1},{3,2},{5,4},{6,5},{7,6},{9,8},{10,9},{11,10},{13,12},{... | collective-permute-start | bytes 196616 | tf_op jit(solution)/shard_map/ppermute | solution.py:25
  45.3 4.0 copy-start.35
  60.3 3.8 copy-start.27
  79.0 5.7 %copy-start.10 = (bf16[8,64,1,2,2,4,4,4]{1,0,7,6,5,4,3,2:T(8,128)(2,1)S(1)}, bf16[8,64,1,2,2,4,4,4]{1,0,7,6,5,4,3,2:T(8,128)(2,1)}, u32[]{:S(2)}) copy-start(bf16[8,64,1,2,2,4,4,4]{1,0,7,6,5,4,3,2:T(8,128)(2,1)} %get-tuple-element.158) | copy-start | bytes 786436
  79.0 5.7 %copy-start.16 = (bf16[8,64,1,2,2,3,4,4]{1,0,7,6,5,4,3,2:T(8,128)(2,1)S(1)}, bf16[8,64,1,2,2,3,4,4]{1,0,7,6,5,4,3,2:T(8,128)(2,1)}, u32[]{:S(2)}) copy-start(bf16[8,64,1,2,2,3,4,4]{1,0,7,6,5,4,3,2:T(8,128)(2,1)} %get-tuple-element.160) | copy-start | bytes 589828
  81.4 4.6 %copy-start.9 = (bf16[8,64,1,2,2,4,4,4]{1,0,7,6,5,4,3,2:T(8,128)(2,1)S(1)}, bf16[8,64,1,2,2,4,4,4]{1,0,7,6,5,4,3,2:T(8,128)(2,1)}, u32[]{:S(2)}) copy-start(bf16[8,64,1,2,2,4,4,4]{1,0,7,6,5,4,3,2:T(8,128)(2,1)} %get-tuple-element.157) | copy-start | bytes 786436
  81.4 4.6 %copy-start.15 = (bf16[8,64,1,2,2,3,4,4]{1,0,7,6,5,4,3,2:T(8,128)(2,1)S(1)}, bf16[8,64,1,2,2,3,4,4]{1,0,7,6,5,4,3,2:T(8,128)(2,1)}, u32[]{:S(2)}) copy-start(bf16[8,64,1,2,2,3,4,4]{1,0,7,6,5,4,3,2:T(8,128)(2,1)} %get-tuple-element.159) | copy-start | bytes 589828
  103.8 11.7 %copy-start.36 = (bf16[64,448]{1,0:T(8,128)(2,1)S(1)}, bf16[64,448]{1,0:T(8,128)(2,1)}, u32[]{:S(2)}) copy-start(bf16[64,448]{1,0:T(8,128)(2,1)} %param.31) | copy-start | bytes 172036
  122.2 3.7 collective-permute-start.4
  125.9 4.1 collective-permute-start.7
  127.3 215.3 %collective-permute-start.5 = (bf16[16,8192]{1,0:T(8,128)(2,1)}, bf16[16,8192]{1,0:T(8,128)(2,1)}, u32[]{:S(2)}, u32[]{:S(2)}) collective-permute-start(bf16[16,8192]{1,0:T(8,128)(2,1)} %pad_maximum_fusion), channel_id=1, source_target_pairs={{0,4},{4,0},{8,12},{12,8},{16,20},{20,16},{24,28},{28,24},{1,5},{5... | collective-permute-start | bytes 786440 | tf_op jit(solution)/shard_map/ppermute | solution.py:14
  270.3 11.0 %copy-start.26 = (f32[8,4096]{1,0:T(8,128)S(1)}, f32[8,4096]{1,0:T(8,128)}, u32[]{:S(2)}) copy-start(f32[8,4096]{1,0:T(8,128)} %slice.915) | copy-start | bytes 393220
  272.6 61.4 %collective-permute-start.9 = (bf16[1,8,4096]{2,1,0:T(8,128)(2,1)}, bf16[1,8,4096]{2,1,0:T(8,128)(2,1)}, u32[]{:S(2)}, u32[]{:S(2)}) collective-permute-start(bf16[1,8,4096]{2,1,0:T(8,128)(2,1)} %fusion.46), channel_id=1, source_target_pairs={{0,4},{4,8},{8,12},{12,16},{16,20},{20,24},{24,28},{1,5},{5,9},{9,... | collective-permute-start | bytes 196616 | tf_op jit(solution)/shard_map/ppermute | solution.py:22
  275.1 53.8 %collective-permute-start.10 = (bf16[1,8,4096]{2,1,0:T(8,128)(2,1)}, bf16[1,8,4096]{2,1,0:T(8,128)(2,1)}, u32[]{:S(2)}, u32[]{:S(2)}) collective-permute-start(bf16[1,8,4096]{2,1,0:T(8,128)(2,1)} %fusion.47), channel_id=1, source_target_pairs={{1,0},{2,1},{3,2},{5,4},{6,5},{7,6},{9,8},{10,9},{11,10},{13,12},{... | collective-permute-start | bytes 196616 | tf_op jit(solution)/shard_map/ppermute | solution.py:25
  276.4 47.5 %collective-permute-start.8 = (bf16[1,8,4096]{2,1,0:T(8,128)(2,1)}, bf16[1,8,4096]{2,1,0:T(8,128)(2,1)}, u32[]{:S(2)}, u32[]{:S(2)}) collective-permute-start(bf16[1,8,4096]{2,1,0:T(8,128)(2,1)} %fusion.45), channel_id=1, source_target_pairs={{4,0},{8,4},{12,8},{16,12},{20,16},{24,20},{28,24},{5,1},{9,5},{13... | collective-permute-start | bytes 196616 | tf_op jit(solution)/shard_map/ppermute | solution.py:25
  277.7 41.3 %collective-permute-start.11 = (bf16[1,8,4096]{2,1,0:T(8,128)(2,1)}, bf16[1,8,4096]{2,1,0:T(8,128)(2,1)}, u32[]{:S(2)}, u32[]{:S(2)}) collective-permute-start(bf16[1,8,4096]{2,1,0:T(8,128)(2,1)} %fusion.48), channel_id=1, source_target_pairs={{0,1},{1,2},{2,3},{4,5},{5,6},{6,7},{8,9},{9,10},{10,11},{12,13},{... | collective-permute-start | bytes 196616 | tf_op jit(solution)/shard_map/ppermute | solution.py:22
  299.0 6.2 %copy-start.19 = (f32[8,64,1,2,2,1,4,4]{1,7,6,5,4,3,2,0:T(4,128)S(1)}, f32[8,64,1,2,2,1,4,4]{1,7,6,5,4,3,2,0:T(4,128)}, u32[]{:S(2)}) copy-start(f32[8,64,1,2,2,1,4,4]{1,7,6,5,4,3,2,0:T(4,128)} %copy.163) | copy-start | bytes 393220
  299.1 6.3 %copy-start.21 = (f32[8,64,1,2,2,1,4,4]{1,7,6,5,4,3,2,0:T(4,128)S(1)}, f32[8,64,1,2,2,1,4,4]{1,7,6,5,4,3,2,0:T(4,128)}, u32[]{:S(2)}) copy-start(f32[8,64,1,2,2,1,4,4]{1,7,6,5,4,3,2,0:T(4,128)} %copy.167) | copy-start | bytes 393220
  299.1 6.5 %copy-start.18 = (f32[8,64,2,1,2,4,1,4]{1,7,6,5,4,3,2,0:T(4,128)S(1)}, f32[8,64,2,1,2,4,1,4]{1,7,6,5,4,3,2,0:T(4,128)}, u32[]{:S(2)}) copy-start(f32[8,64,2,1,2,4,1,4]{1,7,6,5,4,3,2,0:T(4,128)} %copy.171) | copy-start | bytes 393220
  305.3 6.9 %copy-start.17 = (f32[8,64,2,2,1,4,4,1]{1,7,6,5,4,3,2,0:T(1,128)S(1)}, f32[8,64,2,2,1,4,4,1]{1,7,6,5,4,3,2,0:T(1,128)}, u32[]{:S(2)}) copy-start(f32[8,64,2,2,1,4,4,1]{1,7,6,5,4,3,2,0:T(1,128)} %copy.183) | copy-start | bytes 393220
  305.5 12.5 %copy-start.30 = (bf16[8,64,128]{2,1,0:T(8,128)(2,1)S(1)}, bf16[8,64,128]{2,1,0:T(8,128)(2,1)}, u32[]{:S(2)}) copy-start(bf16[8,64,128]{2,1,0:T(8,128)(2,1)} %copy-done.29) | copy-start | bytes 393220
  305.5 12.5 %copy-start.34 = (bf16[1,8,64,128]{3,1,2,0:T(8,128)(2,1)S(1)}, bf16[1,8,64,128]{3,1,2,0:T(8,128)(2,1)}, u32[]{:S(2)}) copy-start(bf16[1,8,64,128]{3,1,2,0:T(8,128)(2,1)} %copy-done.33) | copy-start | bytes 393220
  340.7 114.7 %copy-start.1 = (bf16[128,512]{1,0:T(8,128)(2,1)S(1)}, bf16[128,512]{1,0:T(8,128)(2,1)}, u32[]{:S(2)}) copy-start(bf16[128,512]{1,0:T(8,128)(2,1)} %param.32) | copy-start | bytes 393220
  (30 other events, 59.5 us)
Sparse Core Ops, SparseCore 0:
  319.1 131.5 all-reduce.8
where the time goes:
time: 470 us; the launch traced here: 463 us
  local copies, waits for them, and re-layouts  262 us (56%)
  waiting for transfers between devices  105 us (22%)
  other arithmetic  38.9 us (8%)
  starting transfers between devices  24.8 us (5%)
  between operations  16.1 us (3%)
  matrix products  15.5 us (3%)
    psum x1, waiting for transfers between devices, body(): summed = lax.psum((conv_part, down_part, head_part), ('gx', 'gy'))  105 us
    slice x1, local copies, waits for them, and re-layouts, stack_grad(): moved, plane = minus_back(parts[:, direction + 1], axis_number)  53.3 us
    convert_element_type x8, local copies, waits for them, and re-layouts, planes(): return rows.astype(jnp.float32).reshape(number, channels, 2, 2, 4, 4)  19.9 us
    slice x12, local copies, waits for them, and re-layouts, face_of(): lax.index_in_dim(plane, 1 if upper else 0, 2 + axis_number, keepdims=False)  16.3 us
    reshape x1, local copies, waits for them, and re-layouts, stack_grad(): parts = taps_grad.reshape(number, 7, channels, 2, 2, 2, 4, 4, 4)  13.1 us
    unnamed x112, local copies, waits for them, and re-layouts  12.9 us
    slice x6, local copies, waits for them, and re-layouts, minus_back(): lax.index_in_dim(grad_low, 0, place, keepdims=False)  12.2 us
    reshape x1, local copies, waits for them, and re-layouts, neighbour_stack(): return jnp.stack(fields, axis=1).reshape(number, 7 * channels, 512)  11.7 us
  transfers between devices with their start and end apart: 13, of which 1 were waited for; matrix products, arithmetic and copies ran while one was open for 66% of the time, Pallas kernels for 0%

commit v1 on v0

v1 whole, which is shorter than its diff:
```python
import jax
import jax.numpy as jnp
import numpy as np
from jax import lax
from jax.experimental import pallas as pl
from jax.experimental.pallas import tpu as pltpu
from jax.sharding import PartitionSpec as P

BF = jnp.bfloat16
F32 = jnp.float32
C = 64
SLOTS = 8
LIMIT = 48 * 1024 * 1024
NT = (((1,), (1,)), ((), ()))


def tables():
    lane = np.arange(128)
    r, a, b, c = lane // 64, lane // 16 % 4, lane // 4 % 4, lane % 4

    def one_hot(source, count):
        out = np.zeros((count, source.size), np.float32)
        out[source, np.arange(source.size)] = 1
        return out

    def at(r, a, b, c):
        return r * 64 + a % 4 * 16 + b % 4 * 4 + c % 4

    x_minus = one_hot(at(r, a - 1, b, c), 128)
    x_plus = one_hot(at(r, a + 1, b, c), 128)
    y_minus = one_hot(at(r, a, b - 1, c), 128)
    y_plus = one_hot(at(r, a, b + 1, c), 128)
    z_minus = one_hot(at(1 - r, a, b, c - (r == 0)), 128)
    z_plus = one_hot(at(1 - r, a, b, c + (r == 1)), 128)
    turn_z = np.concatenate([z_minus, z_plus], 1)
    turn_xy = np.stack(
        [
            np.concatenate([(x_plus, x_minus)[k // 2], (y_plus, y_minus)[k % 2]], 1)
            for k in range(4)
        ]
    )
    wide = np.arange(256)
    half = wide // 128
    r, a, b, c = wide // 64 % 2, wide // 16 % 4, wide // 4 % 4, wide % 4
    spread_x = one_hot(half * 32 + r * 16 + b * 4 + c, 64)
    spread_y = one_hot(half * 32 + r * 16 + a * 4 + c, 64)

    def folded(spread):
        zero = np.zeros_like(spread)
        return np.concatenate(
            [np.concatenate([spread, zero], 0), np.concatenate([zero, spread], 0)], 1
        )

    packs = []
    for spread, place, want in ((spread_x, a, 3), (spread_x, a, 0), (spread_y, b, 3), (spread_y, b, 0)):
        pack = (spread * (place == want)).T
        packs.append(np.concatenate([pack, pack], 1))
    index = np.arange(512)
    regroup = np.zeros((512, 512), np.float32)
    regroup[index, index % 64 * 8 + index // 64] = 1
    return [
        np.asarray(t, BF)
        for t in (
            turn_z,
            turn_xy,
            np.stack([folded(spread_x), folded(spread_y)]),
            np.stack(packs),
            regroup,
        )
    ]


def dot(left, right, dims=None):
    if dims is None:
        return jnp.dot(left, right, preferred_element_type=F32)
    return lax.dot_general(left, right, dims, preferred_element_type=F32)


def lane_of(shape):
    return lax.broadcasted_iota(jnp.int32, shape, len(shape) - 1)


def parts(block, direction):
    if direction == 0:
        return block[:, 256:512]
    if direction == 1:
        return block[:, 0:256]
    first = 128 if direction == 2 else 0
    return jnp.concatenate([block[:, first : first + 128], block[:, first + 256 : first + 384]], 1)


def roll_blocks(source, turn_z, turn_xy, pool, pool_z):
    for k in range(4):
        chunk = source[:, k * 128 : (k + 1) * 128]
        moved = dot(chunk, turn_xy[k]).astype(BF).reshape(SLOTS, C, 256)
        x_dir, y_dir = 1 - k // 2, 3 - k % 2
        x_at, y_at = k % 2 * 128, k // 2 * 128
        pool[x_dir, 0:SLOTS, :, x_at : x_at + 128] = moved[:, :, 0:128]
        pool[y_dir, 0:SLOTS, :, y_at : y_at + 128] = moved[:, :, 128:256]
        moved = dot(chunk, turn_z[...]).astype(BF).reshape(SLOTS, C, 256)
        pool_z[0, 0:SLOTS, :, k * 128 : (k + 1) * 128] = moved[:, :, 0:128]
        pool_z[1, 0:SLOTS, :, k * 128 : (k + 1) * 128] = moved[:, :, 128:256]


def rim_masks():
    lane = lane_of((C, 256))
    a, b = lane // 16 % 4, lane // 4 % 4
    masks = [a == 0, a == 3, b == 0, b == 3]
    lane = lane_of((C, 512))
    r, c = lane // 64 % 2, lane % 4
    return masks, [(r == 0) & (c == 0), (r == 1) & (c == 3)]


def weave(direction, moved, block):
    if direction == 0:
        return [moved[:, 0:128], moved[:, 128:256], block[:, 0:128], block[:, 128:256]]
    if direction == 1:
        return [block[:, 256:384], block[:, 384:512], moved[:, 0:128], moved[:, 128:256]]
    if direction == 2:
        return [moved[:, 0:128], block[:, 0:128], moved[:, 128:256], block[:, 256:384]]
    return [block[:, 128:256], moved[:, 0:128], block[:, 384:512], moved[:, 128:256]]


def parities():
    return lax.rem(lax.axis_index("gx"), 2), lax.rem(lax.axis_index("gy"), 2)


def pack_kernel(counts, cmap, x_ref, lat_ref, pack_ref, send_xa, send_xb, send_ya, send_yb):
    px, py = parities()
    masked = jnp.concatenate(
        [
            jnp.where(b < counts[0], x_ref[b * C : (b + 1) * C, :], jnp.zeros((C, 512), BF))
            for b in range(SLOTS)
        ],
        0,
    )
    low = lane_of((256, 128)) < 64
    faces = []
    for d in range(4):
        packed = dot(parts(masked, d), pack_ref[d])
        faces.append(jnp.where(low, packed[0:256], packed[256:512]))
    even = px == 0
    send_xa[0:256, :] = jnp.where(even, faces[0], faces[1]).astype(BF)
    send_xb[...] = jnp.where(even, faces[1], faces[0]).astype(BF)
    even = py == 0
    send_ya[0:256, :] = jnp.where(even, faces[2], faces[3]).astype(BF)
    send_yb[...] = jnp.where(even, faces[3], faces[2]).astype(BF)
    row = lax.broadcasted_iota(jnp.int32, (16, 128), 0)
    named = jnp.zeros((16, 128), jnp.int32)
    for k in range(8):
        named = jnp.where(row == k, cmap[0, k], named)
    named = named.astype(F32).astype(BF)
    lat = lat_ref[...]
    send_xa[256:768, :] = lat
    send_ya[256:768, :] = lat
    send_xa[768:784, :] = named
    send_ya[768:784, :] = named


def main_kernel(
    counts, nb, cmap,
    x_ref, lat_ref, got_xa, got_xb, got_ya, got_yb, got_xy,
    conv_ref, down_ref, head_ref, turn_z, turn_xy, spread, pack, regroup,
    hg_ref, sums_ref, send_xa, send_xb, send_ya, send_yb,
    xm, pool, pool_z, taps, slope, act2, routed, far, maps_v, maps_s, sem,
):
    px, py = parities()
    for j, got in enumerate((got_xa, got_ya)):
        maps_v[j] = got[768:784, :].astype(F32).astype(jnp.int32)
    maps_v[2] = got_xy[512:528, :].astype(F32).astype(jnp.int32)
    copy = pltpu.make_async_copy(maps_v, maps_s, sem)
    copy.start()

    for b in range(SLOTS):
        rows = slice(b * C, (b + 1) * C)
        xm[rows, :] = jnp.where(b < counts[0], x_ref[rows, :], jnp.zeros((C, 512), BF))
    roll_blocks(xm, turn_z, turn_xy, pool, pool_z)
    for got, axis, direction in (
        (got_xa, 0, 1 - px), (got_xb, 0, px), (got_ya, 1, 3 - py), (got_yb, 1, 2 + py),
    ):
        wide = dot(got[0:256, :], spread[axis]).astype(BF).reshape(4, C, 512)
        pool[direction, 8:12] = wide[:, :, 0:256]
        pool[direction, 12:16] = wide[:, :, 256:512]
    for d in range(4):
        pool[d, 16] = jnp.zeros((C, 256), BF)
    for d in range(2):
        pool_z[d, 8] = jnp.zeros((C, 512), BF)

    masks, masks_z = rim_masks()
    low = lane_of((C, 128)) < 64
    conv = conv_ref[...]
    for pair in range(SLOTS // 2):
        acts = []
        for b in (2 * pair, 2 * pair + 1):
            block = xm[b * C : (b + 1) * C, :]
            taps[b, 0:C, :] = block
            for d in range(4):
                moved = jnp.where(masks[d], pool[d, nb[b, d]], pool[d, b])
                for k, piece in enumerate(weave(d, moved, block)):
                    taps[b, (d + 1) * C : (d + 2) * C, k * 128 : (k + 1) * 128] = piece
            for d in range(2):
                near = jnp.minimum(nb[b, d + 4], SLOTS)
                taps[b, (d + 5) * C : (d + 6) * C, :] = jnp.where(
                    masks_z[d], pool_z[d, near], pool_z[d, b]
                )
            hidden = dot(conv, taps[b])
            gate = 0.5 * jnp.tanh(0.5 * hidden) + 0.5
            slope[b] = gate * (1.0 + hidden * (1.0 - gate))
            acts.append(hidden * gate)
        lanes = slice(pair * 128, (pair + 1) * 128)
        for k in range(4):
            one, two = (v[:, k * 128 : (k + 1) * 128] for v in acts)
            first = jnp.where(low, one, pltpu.roll(two, 64, 1))
            second = jnp.where(low, pltpu.roll(one, 64, 1), two)
            act2[2 * k * C : (2 * k + 1) * C, lanes] = first.astype(BF)
            act2[(2 * k + 1) * C : (2 * k + 2) * C, lanes] = second.astype(BF)

    down = dot(down_ref[...], regroup[...], NT).astype(BF)
    down_back = dot(regroup[...], down_ref[...], NT).astype(BF)
    octants = dot(down, act2[...]).astype(BF).astype(F32)
    gate = 0.5 * jnp.tanh(0.5 * octants) + 0.5
    oct_act = (octants * gate).astype(BF)
    oct_slope = gate * (1.0 + octants * (1.0 - gate))
    projected = dot(head_ref[...], oct_act).T.astype(BF)
    send_xa[256:768, :] = projected
    send_ya[256:768, :] = projected

    copy.wait()
    for s in range(SLOTS):
        routed[s] = jnp.zeros((C, 128), BF)
    for j, (got, start) in enumerate(((lat_ref, 0), (got_xa, 256), (got_ya, 256), (got_xy, 0))):
        for k in range(8):
            name = cmap[0, k] if j == 0 else maps_s[j - 1, k, 0]
            name = name - j * SLOTS
            name = jnp.where((name >= 0) & (name < SLOTS), name, SLOTS)
            routed[name] = got[start + k * C : start + (k + 1) * C, :]
    grad = routed[0:SLOTS].reshape(SLOTS * C, 128)
    head_back = head_ref[...].astype(F32).T.astype(BF)
    oct_grad = (dot(head_back, grad, NT) * oct_slope).astype(BF)
    sums_ref[768:896, :] = dot(oct_act, grad).T
    down_sum = dot(oct_grad, act2[...], NT)
    for k in range(4):
        sums_ref[256 + k * 128 : 256 + (k + 1) * 128, :] = down_sum[:, k * 128 : (k + 1) * 128]
    conv_sum = jnp.zeros((C, 448), F32)
    for pair in range(SLOTS // 2):
        patch = dot(down_back, oct_grad[:, pair * 128 : (pair + 1) * 128])
        for side in range(2):
            b = 2 * pair + side
            for k in range(4):
                first = patch[2 * k * C : (2 * k + 1) * C]
                second = patch[(2 * k + 1) * C : (2 * k + 2) * C]
                if side == 0:
                    both = jnp.where(low, first, pltpu.roll(second, 64, 1))
                else:
                    both = jnp.where(low, pltpu.roll(first, 64, 1), second)
                lanes = slice(k * 128, (k + 1) * 128)
                hg_ref[b * C : (b + 1) * C, lanes] = (both * slope[b, :, lanes]).astype(BF)
            conv_sum = conv_sum + dot(hg_ref[b * C : (b + 1) * C, :], taps[b], NT)
    for k in range(3):
        sums_ref[k * C : (k + 1) * C, :] = conv_sum[:, k * 128 : (k + 1) * 128]
    sums_ref[3 * C : 4 * C, 0:C] = conv_sum[:, 384:448]
    sums_ref[3 * C : 4 * C, C:128] = jnp.zeros((C, C), F32)

    for d in range(4):
        for s in range(5):
            far[d, s] = jnp.zeros((C, 128), F32)
    high = lane_of((C, 128)) // 64
    for d in range(4):
        face = dot(parts(hg_ref[...], d ^ 1), pack[d ^ 1])
        for b in range(SLOTS):
            name = nb[b, d] - SLOTS
            away = (name >= 0) & (name < SLOTS)
            row = jnp.where(away, lax.rem(name, 4), 4)
            side = jnp.where(name >= 4, 1, 0)
            far[d, row] += jnp.where(high == side, face[b * C : (b + 1) * C, :], 0.0)
    send_xa[0:256, :] = far[1 - px, 0:4].reshape(256, 128).astype(BF)
    send_xb[...] = far[px, 0:4].reshape(256, 128).astype(BF)
    send_ya[0:256, :] = far[3 - py, 0:4].reshape(256, 128).astype(BF)
    send_yb[...] = far[2 + py, 0:4].reshape(256, 128).astype(BF)


def last_kernel(
    counts, nb,
    hg_ref, got_xa, got_xb, got_ya, got_yb, conv_ref, turn_z, turn_xy, spread,
    out_ref,
    pool, pool_z, total, total_z, fields,
):
    px, py = parities()
    roll_blocks(hg_ref, turn_z, turn_xy, pool, pool_z)
    for got, axis, direction in (
        (got_xa, 0, px), (got_xb, 0, 1 - px), (got_ya, 1, 2 + py), (got_yb, 1, 3 - py),
    ):
        wide = dot(got[0:256, :], spread[axis]).reshape(4, C, 512)
        total[direction, 0:4] = wide[:, :, 0:256]
        total[direction, 4:8] = wide[:, :, 256:512]
    for d in range(2):
        for s in range(SLOTS):
            total_z[d, s] = jnp.zeros((C, 512), F32)
    for b in range(SLOTS):
        for d in range(4):
            near = jnp.minimum(nb[b, d], SLOTS)
            total[d, near] += pool[d ^ 1, b].astype(F32)
        for d in range(2):
            near = jnp.minimum(nb[b, d + 4], SLOTS)
            total_z[d, near] += pool_z[1 - d, b].astype(F32)
    masks, masks_z = rim_masks()
    conv = conv_ref[...]
    for b in range(SLOTS):
        block = hg_ref[b * C : (b + 1) * C, :]
        fields[0:C, :] = block
        for d in range(4):
            moved = jnp.where(masks[d ^ 1], total[d, b].astype(BF), pool[d ^ 1, b])
            for k, piece in enumerate(weave(d ^ 1, moved, block)):
                fields[(d + 1) * C : (d + 2) * C, k * 128 : (k + 1) * 128] = piece
        for d in range(2):
            fields[(d + 5) * C : (d + 6) * C, :] = jnp.where(
                masks_z[1 - d], total_z[d, b].astype(BF), pool_z[1 - d, b]
            )
        near = dot(conv, fields[...])
        out_ref[b * C : (b + 1) * C, :] = jnp.where(b < counts[0], near, 0.0).astype(BF)


def latent_kernel(cmap, own, got_xa, got_ya, got_xy, out_ref, rows):
    rows[0:8] = own[256:768, :].reshape(8, C, 128)
    rows[8:16] = got_xa[256:768, :].reshape(8, C, 128)
    rows[16:24] = got_ya[256:768, :].reshape(8, C, 128)
    rows[24:32] = got_xy[...].reshape(8, C, 128)
    rows[32] = jnp.zeros((C, 128), BF)
    for k in range(8):
        out_ref[k * C : (k + 1) * C, :] = rows[cmap[0, k]]


def scale_kernel(scale, conv_in, regroup, conv_out, down_out, head_out):
    for k in range(3):
        conv_out[:, k * 128 : (k + 1) * 128] = conv_in[k * C : (k + 1) * C, :].astype(F32) * scale
    conv_out[:, 384:448] = conv_in[3 * C : 4 * C, 0:C].astype(F32) * scale
    down = jnp.concatenate([conv_in[256 + k * 128 : 384 + k * 128, :] for k in range(4)], 1)
    down_out[...] = dot(down, regroup[...]) * scale
    head_out[...] = conv_in[768:896, :].astype(F32) * scale


def swap(value, axis, bit):
    count = lax.axis_size(axis)
    return lax.ppermute(value, axis, [(i, i ^ bit) for i in range(count)])


def swap_odd(value, axis):
    count = lax.axis_size(axis)
    route = []
    for low in range(1, count - 1, 2):
        route += [(low, low + 1), (low + 1, low)]
    return lax.ppermute(value, axis, route)


def total_of(sums):
    rows = sums.shape[0] // 2
    bit = lax.rem(lax.axis_index("gy"), 2)
    mine = lax.dynamic_slice_in_dim(sums, bit * rows, rows)
    other = lax.dynamic_slice_in_dim(sums, (1 - bit) * rows, rows)
    mine = mine + swap(other.astype(BF), "gy", 1).astype(F32)
    for axis, first in (("gy", 2), ("gx", 1)):
        step = first
        while step < lax.axis_size(axis):
            mine = mine + swap(mine.astype(BF), axis, step).astype(F32)
            step *= 2
    mine = mine.astype(BF)
    theirs = swap(mine, "gy", 1)
    return jnp.where(
        bit == 0, jnp.concatenate([mine, theirs]), jnp.concatenate([theirs, mine])
    )


def call(kernel, outs, ins, scalars=0, scratch=()):
    smem = pl.BlockSpec(memory_space=pltpu.SMEM)
    vmem = pl.BlockSpec(memory_space=pltpu.VMEM)
    return pl.pallas_call(
        kernel,
        out_shape=[jax.ShapeDtypeStruct(shape, kind) for shape, kind in outs],
        in_specs=[smem] * scalars + [vmem] * (len(ins) - scalars),
        out_specs=[vmem] * len(outs),
        scratch_shapes=list(scratch),
        compiler_params=pltpu.CompilerParams(vmem_limit_bytes=LIMIT),
    )(*ins)


def body(
    features, neighbours, counts, conv_weight, down_weight, head_weight, coarse_map, latent_grad
):
    turn_z, turn_xy, spread, pack, regroup = (jnp.asarray(t) for t in tables())
    flat = features.reshape(SLOTS * C, 512)
    lat = latent_grad.reshape(512, 128)
    send_xa, send_xb, send_ya, send_yb = call(
        pack_kernel,
        [((784, 128), BF), ((256, 128), BF), ((784, 128), BF), ((256, 128), BF)],
        (counts, coarse_map, flat, lat, pack),
        2,
    )
    got_xa = swap(send_xa, "gx", 1)
    got_xb = swap_odd(send_xb, "gx")
    got_yb = swap_odd(send_yb, "gy")
    got_ya = swap(send_ya, "gy", 1)
    got_xy = swap(got_xa[256:784], "gy", 1)
    hg, sums, send_xa, send_xb, send_ya, send_yb = call(
        main_kernel,
        [
            ((512, 512), BF), ((896, 128), F32),
            ((768, 128), BF), ((256, 128), BF), ((768, 128), BF), ((256, 128), BF),
        ],
        (
            counts, neighbours, coarse_map, flat, lat, got_xa, got_xb, got_ya, got_yb, got_xy,
            conv_weight, down_weight, head_weight, turn_z, turn_xy, spread, pack, regroup,
        ),
        3,
        [
            pltpu.VMEM((512, 512), BF),
            pltpu.VMEM((4, 17, C, 256), BF),
            pltpu.VMEM((2, 9, C, 512), BF),
            pltpu.VMEM((SLOTS, 448, 512), BF),
            pltpu.VMEM((SLOTS, C, 512), F32),
            pltpu.VMEM((512, 512), BF),
            pltpu.VMEM((SLOTS + 1, C, 128), BF),
            pltpu.VMEM((4, 5, C, 128), F32),
            pltpu.VMEM((3, 16, 128), jnp.int32),
            pltpu.SMEM((3, 16, 128), jnp.int32),
            pltpu.SemaphoreType.DMA,
        ],
    )
    own = send_xa
    got_xa = swap(send_xa, "gx", 1)
    got_xb = swap_odd(send_xb, "gx")
    got_yb = swap_odd(send_yb, "gy")
    got_ya = swap(send_ya, "gy", 1)
    got_xy = swap(got_xa[256:768], "gy", 1)
    summed = total_of(sums)
    conv_back = conv_weight.reshape(C, 7, C).transpose(2, 1, 0).reshape(C, 448)
    (grad,) = call(
        last_kernel,
        [((512, 512), BF)],
        (counts, neighbours, hg, got_xa, got_xb, got_ya, got_yb, conv_back, turn_z, turn_xy, spread),
        2,
        [
            pltpu.VMEM((4, 8, C, 256), BF),
            pltpu.VMEM((2, 8, C, 512), BF),
            pltpu.VMEM((4, 9, C, 256), F32),
            pltpu.VMEM((2, 9, C, 512), F32),
            pltpu.VMEM((448, 512), BF),
        ],
    )
    (latent,) = call(
        latent_kernel,
        [((512, 128), BF)],
        (coarse_map, own, got_xa, got_ya, got_xy),
        1,
        [pltpu.VMEM((33, C, 128), BF)],
    )
    scale = float(SLOTS * lax.axis_size("gx") * lax.axis_size("gy")) ** (-0.5)
    conv_grad, down_grad, head_grad = call(
        lambda *refs: scale_kernel(scale, *refs),
        [((C, 448), F32), ((128, 512), F32), ((128, 128), F32)],
        (summed, regroup),
    )
    return (
        latent.reshape(1, 512, 128), grad.reshape(SLOTS, C, 512), conv_grad, down_grad, head_grad,
    )


def solution(mesh):
    both = ("gx", "gy")
    placed = (
        P(both, None, None), P(both, None), P(both), P(), P(), P(), P(both, None),
        P(both, None, None),
    )
    return jax.shard_map(
        body,
        mesh=mesh,
        in_specs=placed,
        out_specs=(P(both, None, None), P(both, None, None), P(), P(), P()),
        check_vma=False,
    )
```

time: 470 us -> 74.2 us (0.16)
  the two profiles are of different devices: /device:TPU:0 before, /device:TPU:9 now
where the time goes in v1:
time: 74.2 us; the launch traced here: 73.7 us
  starting transfers between devices  30.6 us (41%)
  waiting for transfers between devices  16.8 us (23%)
  Pallas kernels  14.3 us (19%)
  local copies, waits for them, and re-layouts  10.2 us (14%)
  between operations  1.53 us (2%)
    ppermute x12, starting transfers between devices, swap(): return lax.ppermute(value, axis, [(i, i ^ bit) for i in range(count)])  17 us
    pallas_call x5, Pallas kernels, call(): pl.pallas_call(kernel, out_shape=[jax.ShapeDtypeStruct(shape, kind) for s...  14.3 us
    ppermute x4, starting transfers between devices, swap_odd(): return lax.ppermute(value, axis, route)  13.6 us
    ppermute x12, waiting for transfers between devices, swap(): return lax.ppermute(value, axis, [(i, i ^ bit) for i in range(count)])  12.8 us
    unnamed x38, local copies, waits for them, and re-layouts  9.01 us
    ppermute x4, waiting for transfers between devices, swap_odd(): return lax.ppermute(value, axis, route)  3.97 us
  transfers between devices with their start and end apart: 16, of which 8 were waited for; matrix products, arithmetic and copies ran while one was open for 2% of the time, Pallas kernels for 8%

profile of v1, /device:TPU:9, one launch (start us, length us, event | category | flops | bytes accessed | tf_op | source)
XLA Modules:
  0.0 73.7 jit_solution(16395020022348231137)
XLA Ops:
  1.9 1.0 %copy-done = bf16[8,64,512]{2,1,0:T(8,128)(2,1)S(1)} copy-done((bf16[8,64,512]{2,1,0:T(8,128)(2,1)S(1)}, bf16[8,64,512]{2,1,0:T(8,128)(2,1)}, u32[]{:S(2)}) %copy-start) | copy-done | bytes 524312
  3.0 0.9 %copy-done.7 = bf16[4,256,128]{2,1,0:T(8,128)(2,1)S(1)} copy-done((bf16[4,256,128]{2,1,0:T(8,128)(2,1)S(1)}, bf16[4,256,128]{2,1,0:T(8,128)(2,1)}, u32[]{:S(2)}) %copy-start.7) | copy-done | bytes 262168
  3.9 0.9 %copy-done.9 = bf16[1,512,128]{2,1,0:T(8,128)(2,1)S(1)} copy-done((bf16[1,512,128]{2,1,0:T(8,128)(2,1)S(1)}, bf16[1,512,128]{2,1,0:T(8,128)(2,1)}, u32[]{:S(2)}) %copy-start.9) | copy-done | bytes 131096
  4.8 1.0 %shard_map.164 = (bf16[784,128]{1,0:T(8,128)(2,1)S(1)}, bf16[256,128]{1,0:T(8,128)(2,1)S(1)}, bf16[784,128]{1,0:T(8,128)(2,1)S(1)}, bf16[256,128]{1,0:T(8,128)(2,1)S(1)}) custom-call(s32[1]{0:T(128)S(6)} %copy.20.counts, s32[1,8]{1,0:T(1,128)S(1)} %copy-done.18, bf16[512,512]{1,0:T(8,128)(2,1)S(1)} %bitcast.5, bf16[512,128]{1,0:T(8,128)(2,1)S(1)} %bitcast.7, ...), custom_call_target="tpu_custom_call" | custom-call | tf_op jit(solution)/shard_map/pallas_call | solution.py:376
  5.9 1.3 %collective-permute-start = (bf16[784,128]{1,0:T(8,128)(2,1)S(1)}, bf16[784,128]{1,0:T(8,128)(2,1)S(1)}, u32[]{:S(2)}, u32[]{:S(2)}) collective-permute-start(bf16[784,128]{1,0:T(8,128)(2,1)S(1)} %get-tuple-element.18), channel_id=1, source_target_pairs={{0,4},{4,0},{8,12},{12,8},{16,20},{20,16},{24,28},{28,24},{1,5},{5... | collective-permute-start | bytes 602120 | tf_op jit(solution)/shard_map/ppermute | solution.py:344
  7.2 0.9 %collective-permute-start.2 = (bf16[784,128]{1,0:T(8,128)(2,1)S(1)}, bf16[784,128]{1,0:T(8,128)(2,1)S(1)}, u32[]{:S(2)}, u32[]{:S(2)}) collective-permute-start(bf16[784,128]{1,0:T(8,128)(2,1)S(1)} %get-tuple-element.20), channel_id=1, source_target_pairs={{0,1},{1,0},{2,3},{3,2},{4,5},{5,4},{6,7},{7,6},{8,9},{9,8},{10,11... | collective-permute-start | bytes 602120 | tf_op jit(solution)/shard_map/ppermute | solution.py:344
  8.1 3.6 %collective-permute-done.got_xa = bf16[784,128]{1,0:T(8,128)(2,1)S(1)} collective-permute-done((bf16[784,128]{1,0:T(8,128)(2,1)S(1)}, bf16[784,128]{1,0:T(8,128)(2,1)S(1)}, u32[]{:S(2)}, u32[]{:S(2)}) %collective-permute-start) | collective-permute-done | bytes 200736 | tf_op jit(solution)/shard_map/ppermute | solution.py:344
  11.8 1.6 %collective-permute-start.4 = (bf16[528,128]{1,0:T(8,128)(2,1)S(1)}, bf16[528,128]{1,0:T(8,128)(2,1)S(1)}, u32[]{:S(2)}, u32[]{:S(2)}) collective-permute-start(bf16[528,128]{1,0:T(8,128)(2,1)S(1)} %slice.8), channel_id=1, source_target_pairs={{0,1},{1,0},{2,3},{3,2},{4,5},{5,4},{6,7},{7,6},{8,9},{9,8},{10,11... | collective-permute-start | bytes 405512 | tf_op jit(solution)/shard_map/ppermute | solution.py:344
  13.4 3.0 %collective-permute-start.1 = (bf16[256,128]{1,0:T(8,128)(2,1)S(1)}, bf16[256,128]{1,0:T(8,128)(2,1)S(1)}, u32[]{:S(2)}, u32[]{:S(2)}) collective-permute-start(bf16[256,128]{1,0:T(8,128)(2,1)S(1)} %get-tuple-element.19), channel_id=1, source_target_pairs={{4,8},{8,4},{12,16},{16,12},{20,24},{24,20},{5,9},{9,5},{13,17},{1... | collective-permute-start | bytes 196616 | tf_op jit(solution)/shard_map/ppermute | solution.py:352
  16.4 3.3 %collective-permute-start.3 = (bf16[256,128]{1,0:T(8,128)(2,1)S(1)}, bf16[256,128]{1,0:T(8,128)(2,1)S(1)}, u32[]{:S(2)}, u32[]{:S(2)}) collective-permute-start(bf16[256,128]{1,0:T(8,128)(2,1)S(1)} %get-tuple-element.21), channel_id=1, source_target_pairs={{1,2},{2,1},{5,6},{6,5},{9,10},{10,9},{13,14},{14,13},{17,18},{18,... | collective-permute-start | bytes 196616 | tf_op jit(solution)/shard_map/ppermute | solution.py:352
  19.9 2.1 %collective-permute-done.3.got_yb = bf16[256,128]{1,0:T(8,128)(2,1)S(1)} collective-permute-done((bf16[256,128]{1,0:T(8,128)(2,1)S(1)}, bf16[256,128]{1,0:T(8,128)(2,1)S(1)}, u32[]{:S(2)}, u32[]{:S(2)}) %collective-permute-start.3) | collective-permute-done | bytes 65568 | tf_op jit(solution)/shard_map/ppermute | solution.py:352
  22.1 0.9 %copy-done.3 = bf16[4,128,256]{2,1,0:T(8,128)(2,1)S(1)} copy-done((bf16[4,128,256]{2,1,0:T(8,128)(2,1)S(1)}, bf16[4,128,256]{2,1,0:T(8,128)(2,1)}, u32[]{:S(2)}) %copy-start.3) | copy-done | bytes 262168
  23.0 0.9 %copy-done.5 = bf16[2,128,512]{2,1,0:T(8,128)(2,1)S(1)} copy-done((bf16[2,128,512]{2,1,0:T(8,128)(2,1)S(1)}, bf16[2,128,512]{2,1,0:T(8,128)(2,1)}, u32[]{:S(2)}) %copy-start.5) | copy-done | bytes 262168
  24.0 0.9 %copy-done.8 = bf16[4,256,128]{2,1,0:T(8,128)(2,1)S(1)} copy-done((bf16[4,256,128]{2,1,0:T(8,128)(2,1)S(1)}, bf16[4,256,128]{2,1,0:T(8,128)(2,1)}, u32[]{:S(2)}) %copy-start.8) | copy-done | bytes 262168
  26.6 0.9 %copy-done.15 = bf16[128,512]{1,0:T(8,128)(2,1)S(1)} copy-done((bf16[128,512]{1,0:T(8,128)(2,1)S(1)}, bf16[128,512]{1,0:T(8,128)(2,1)}, u32[]{:S(2)}) %copy-start.15) | copy-done | bytes 131096
  27.5 6.8 %shard_map.165 = (bf16[512,512]{1,0:T(8,128)(2,1)S(1)}, f32[896,128]{1,0:T(8,128)S(1)}, bf16[768,128]{1,0:T(8,128)(2,1)S(1)}, bf16[256,128]{1,0:T(8,128)(2,1)S(1...) custom-call(s32[1]{0:T(128)S(6)} %copy.20.counts, s32[8,6]{1,0:T(8,128)S(1)} %copy-done.17, ...), custom_call_target="tpu_custom_call" | custom-call | tf_op jit(solution)/shard_map/pallas_call | solution.py:376
  34.4 1.3 %collective-permute-done.10 = bf16[448,128]{1,0:T(8,128)(2,1)S(1)} collective-permute-done((bf16[448,128]{1,0:T(8,128)(2,1)S(1)}, bf16[448,128]{1,0:T(8,128)(2,1)S(1)}, u32[]{:S(2)}, u32[]{:S(2)}) %collective-permute-start.10) | collective-permute-done | bytes 114720 | tf_op jit(solution)/shard_map/ppermute | solution.py:344
  35.7 1.2 %collective-permute-start.11 = (bf16[448,128]{1,0:T(8,128)(2,1)S(1)}, bf16[448,128]{1,0:T(8,128)(2,1)S(1)}, u32[]{:S(2)}, u32[]{:S(2)}) collective-permute-start(bf16[448,128]{1,0:T(8,128)(2,1)S(1)} %fusion.2), channel_id=1, source_target_pairs={{0,2},{1,3},{2,0},{3,1},{4,6},{5,7},{6,4},{7,5},{8,10},{9,11},{10,... | collective-permute-start | bytes 344072 | tf_op jit(solution)/shard_map/ppermute | solution.py:344
  37.0 3.4 %collective-permute-done.11 = bf16[448,128]{1,0:T(8,128)(2,1)S(1)} collective-permute-done((bf16[448,128]{1,0:T(8,128)(2,1)S(1)}, bf16[448,128]{1,0:T(8,128)(2,1)S(1)}, u32[]{:S(2)}, u32[]{:S(2)}) %collective-permute-start.11) | collective-permute-done | bytes 114720 | tf_op jit(solution)/shard_map/ppermute | solution.py:344
  40.4 1.4 %collective-permute-start.12 = (bf16[448,128]{1,0:T(8,128)(2,1)S(1)}, bf16[448,128]{1,0:T(8,128)(2,1)S(1)}, u32[]{:S(2)}, u32[]{:S(2)}) collective-permute-start(bf16[448,128]{1,0:T(8,128)(2,1)S(1)} %fusion), channel_id=1, source_target_pairs={{0,4},{4,0},{8,12},{12,8},{16,20},{20,16},{24,28},{28,24},{1,5},{5... | collective-permute-start | bytes 344072 | tf_op jit(solution)/shard_map/ppermute | solution.py:344
  41.9 2.3 %collective-permute-done.12 = bf16[448,128]{1,0:T(8,128)(2,1)S(1)} collective-permute-done((bf16[448,128]{1,0:T(8,128)(2,1)S(1)}, bf16[448,128]{1,0:T(8,128)(2,1)S(1)}, u32[]{:S(2)}, u32[]{:S(2)}) %collective-permute-start.12) | collective-permute-done | bytes 114720 | tf_op jit(solution)/shard_map/ppermute | solution.py:344
  44.7 1.1 %collective-permute-start.5 = (bf16[768,128]{1,0:T(8,128)(2,1)S(1)}, bf16[768,128]{1,0:T(8,128)(2,1)S(1)}, u32[]{:S(2)}, u32[]{:S(2)}) collective-permute-start(bf16[768,128]{1,0:T(8,128)(2,1)S(1)} %get-tuple-element.22.own), channel_id=1, source_target_pairs={{0,4},{4,0},{8,12},{12,8},{16,20},{20,16},{24,28},{28,24},{1,5},{5... | collective-permute-start | bytes 589832 | tf_op jit(solution)/shard_map/ppermute | solution.py:344
  45.8 2.1 %collective-permute-done.13 = bf16[448,128]{1,0:T(8,128)(2,1)S(1)} collective-permute-done((bf16[448,128]{1,0:T(8,128)(2,1)S(1)}, bf16[448,128]{1,0:T(8,128)(2,1)S(1)}, u32[]{:S(2)}, u32[]{:S(2)}) %collective-permute-start.13) | collective-permute-done | bytes 114720 | tf_op jit(solution)/shard_map/ppermute | solution.py:344
  48.0 2.4 %collective-permute-start.14 = (bf16[448,128]{1,0:T(8,128)(2,1)S(1)}, bf16[448,128]{1,0:T(8,128)(2,1)S(1)}, u32[]{:S(2)}, u32[]{:S(2)}) collective-permute-start(bf16[448,128]{1,0:T(8,128)(2,1)S(1)} %fusion.1), channel_id=1, source_target_pairs={{0,16},{4,20},{8,24},{12,28},{16,0},{20,4},{24,8},{28,12},{1,17},{... | collective-permute-start | bytes 344072 | tf_op jit(solution)/shard_map/ppermute | solution.py:344
  50.3 3.5 %collective-permute-start.6 = (bf16[768,128]{1,0:T(8,128)(2,1)S(1)}, bf16[768,128]{1,0:T(8,128)(2,1)S(1)}, u32[]{:S(2)}, u32[]{:S(2)}) collective-permute-start(bf16[768,128]{1,0:T(8,128)(2,1)S(1)} %get-tuple-element.23), channel_id=1, source_target_pairs={{0,1},{1,0},{2,3},{3,2},{4,5},{5,4},{6,7},{7,6},{8,9},{9,8},{10,11... | collective-permute-start | bytes 589832 | tf_op jit(solution)/shard_map/ppermute | solution.py:344
  54.6 2.9 %collective-permute-start.15 = (bf16[448,128]{1,0:T(8,128)(2,1)S(1)}, bf16[448,128]{1,0:T(8,128)(2,1)S(1)}, u32[]{:S(2)}, u32[]{:S(2)}) collective-permute-start(bf16[448,128]{1,0:T(8,128)(2,1)S(1)} %add_convert_fusion), channel_id=1, source_target_pairs={{0,1},{1,0},{2,3},{3,2},{4,5},{5,4},{6,7},{7,6},{8,9},{9,8},{10,11... | collective-permute-start | bytes 344072 | tf_op jit(solution)/shard_map/ppermute | solution.py:344
  57.5 3.9 %collective-permute-start.8 = (bf16[256,128]{1,0:T(8,128)(2,1)S(1)}, bf16[256,128]{1,0:T(8,128)(2,1)S(1)}, u32[]{:S(2)}, u32[]{:S(2)}) collective-permute-start(bf16[256,128]{1,0:T(8,128)(2,1)S(1)} %get-tuple-element.25), channel_id=1, source_target_pairs={{4,8},{8,4},{12,16},{16,12},{20,24},{24,20},{5,9},{9,5},{13,17},{1... | collective-permute-start | bytes 196616 | tf_op jit(solution)/shard_map/ppermute | solution.py:352
  61.5 3.3 %collective-permute-start.9 = (bf16[256,128]{1,0:T(8,128)(2,1)S(1)}, bf16[256,128]{1,0:T(8,128)(2,1)S(1)}, u32[]{:S(2)}, u32[]{:S(2)}) collective-permute-start(bf16[256,128]{1,0:T(8,128)(2,1)S(1)} %get-tuple-element.26), channel_id=1, source_target_pairs={{1,2},{2,1},{5,6},{6,5},{9,10},{10,9},{13,14},{14,13},{17,18},{18,... | collective-permute-start | bytes 196616 | tf_op jit(solution)/shard_map/ppermute | solution.py:352
  65.3 1.7 %collective-permute-done.9.got_yb = bf16[256,128]{1,0:T(8,128)(2,1)S(1)} collective-permute-done((bf16[256,128]{1,0:T(8,128)(2,1)S(1)}, bf16[256,128]{1,0:T(8,128)(2,1)S(1)}, u32[]{:S(2)}, u32[]{:S(2)}) %collective-permute-start.9) | collective-permute-done | bytes 65568 | tf_op jit(solution)/shard_map/ppermute | solution.py:352
  67.1 4.3 %shard_map.167 = bf16[512,512]{1,0:T(8,128)(2,1)} custom-call(s32[1]{0:T(128)S(6)} %copy.20.counts, s32[8,6]{1,0:T(8,128)S(1)} %copy-done.17, bf16[512,512]{1,0:T(8,128)(2,1)S(1)} %get-tuple-element.24.hg_ref, bf16[768,128]{1,0:T(8,128)(2,1)S(1)} %collective-permute-done.5.got_xa, bf16[256,128]{1,0:T(8,128)(2,1)S(1)} %collective-permute-done.8.got_xb, ...), custom_call_target="tpu_custom_call" | custom-call | tf_op jit(solution)/shard_map/pallas_call | solution.py:376
  71.4 1.2 %shard_map.166 = bf16[512,128]{1,0:T(8,128)(2,1)} custom-call(s32[1,8]{1,0:T(1,128)S(1)} %copy-done.18, bf16[768,128]{1,0:T(8,128)(2,1)S(1)} %get-tuple-element.22.own, bf16[768,128]{1,0:T(8,128)(2,1)S(1)} %collective-permute-done.5.got_xa, bf16[768,128]{1,0:T(8,128)(2,1)S(1)} %collective-permute-done.6.got_ya, ...), custom_call_target="tpu_custom_call" | custom-call | tf_op jit(solution)/shard_map/pallas_call | solution.py:376
  72.7 1.0 %shard_map.168 = (f32[64,448]{1,0:T(8,128)}, f32[128,512]{1,0:T(8,128)}, f32[128,128]{1,0:T(8,128)}) custom-call(bf16[896,128]{1,0:T(8,128)(2,1)S(1)} %maximum_select_fusion.refs_0_, bf16[512,512]{1,0:T(8,128)(2,1)S(1)} %copy-done.2), custom_call_target="tpu_custom_call" | custom-call | tf_op jit(solution)/shard_map/pallas_call | solution.py:376
  (55 shorter events, 4.5 us)
Async XLA Ops:
  1.9 1.0 %copy-start = (bf16[8,64,512]{2,1,0:T(8,128)(2,1)S(1)}, bf16[8,64,512]{2,1,0:T(8,128)(2,1)}, u32[]{:S(2)}) copy-start(bf16[8,64,512]{2,1,0:T(8,128)(2,1)} %param.13) | copy-start | bytes 1572868
  3.0 0.9 %copy-start.7 = (bf16[4,256,128]{2,1,0:T(8,128)(2,1)S(1)}, bf16[4,256,128]{2,1,0:T(8,128)(2,1)}, u32[]{:S(2)}) copy-start(bf16[4,256,128]{2,1,0:T(8,128)(2,1)} %constant.28.clone.pack_ref.pack) | copy-start | bytes 786436
  3.9 0.9 %copy-start.9 = (bf16[1,512,128]{2,1,0:T(8,128)(2,1)S(1)}, bf16[1,512,128]{2,1,0:T(8,128)(2,1)}, u32[]{:S(2)}) copy-start(bf16[1,512,128]{2,1,0:T(8,128)(2,1)} %param.20) | copy-start | bytes 393220
  4.8 17.2 %copy-start.1 = (bf16[8,64,512]{2,1,0:T(8,128)(2,1)S(1)}, bf16[8,64,512]{2,1,0:T(8,128)(2,1)}, u32[]{:S(2)}) copy-start(bf16[8,64,512]{2,1,0:T(8,128)(2,1)} %param.13) | copy-start | bytes 1572868
  4.8 17.2 %copy-start.2 = (bf16[512,512]{1,0:T(8,128)(2,1)S(1)}, bf16[512,512]{1,0:T(8,128)(2,1)}, u32[]{:S(2)}) copy-start(bf16[512,512]{1,0:T(8,128)(2,1)} %constant.29.clone.regroup.refs_1_) | copy-start | bytes 1572868
  5.9 5.9 %collective-permute-start = (bf16[784,128]{1,0:T(8,128)(2,1)S(1)}, bf16[784,128]{1,0:T(8,128)(2,1)S(1)}, u32[]{:S(2)}, u32[]{:S(2)}) collective-permute-start(bf16[784,128]{1,0:T(8,128)(2,1)S(1)} %get-tuple-element.18), channel_id=1, source_target_pairs={{0,4},{4,0},{8,12},{12,8},{16,20},{20,16},{24,28},{28,24},{1,5},{5... | collective-permute-start | bytes 602120 | tf_op jit(solution)/shard_map/ppermute | solution.py:344
  7.2 14.9 %copy-start.10 = (bf16[1,512,128]{2,1,0:T(8,128)(2,1)S(1)}, bf16[1,512,128]{2,1,0:T(8,128)(2,1)}, u32[]{:S(2)}) copy-start(bf16[1,512,128]{2,1,0:T(8,128)(2,1)} %param.20) | copy-start | bytes 393220
  7.2 14.9 %collective-permute-start.2 = (bf16[784,128]{1,0:T(8,128)(2,1)S(1)}, bf16[784,128]{1,0:T(8,128)(2,1)S(1)}, u32[]{:S(2)}, u32[]{:S(2)}) collective-permute-start(bf16[784,128]{1,0:T(8,128)(2,1)S(1)} %get-tuple-element.20), channel_id=1, source_target_pairs={{0,1},{1,0},{2,3},{3,2},{4,5},{5,4},{6,7},{7,6},{8,9},{9,8},{10,11... | collective-permute-start | bytes 602120 | tf_op jit(solution)/shard_map/ppermute | solution.py:344
  11.8 10.3 %copy-start.16 = (bf16[128,128]{1,0:T(8,128)(2,1)S(1)}, bf16[128,128]{1,0:T(8,128)(2,1)}, u32[]{:S(2)}) copy-start(bf16[128,128]{1,0:T(8,128)(2,1)} %head_ref.1) | copy-start | bytes 98308
  11.8 10.2 %collective-permute-start.4 = (bf16[528,128]{1,0:T(8,128)(2,1)S(1)}, bf16[528,128]{1,0:T(8,128)(2,1)S(1)}, u32[]{:S(2)}, u32[]{:S(2)}) collective-permute-start(bf16[528,128]{1,0:T(8,128)(2,1)S(1)} %slice.8), channel_id=1, source_target_pairs={{0,1},{1,0},{2,3},{3,2},{4,5},{5,4},{6,7},{7,6},{8,9},{9,8},{10,11... | collective-permute-start | bytes 405512 | tf_op jit(solution)/shard_map/ppermute | solution.py:344
  13.4 6.5 %collective-permute-start.1 = (bf16[256,128]{1,0:T(8,128)(2,1)S(1)}, bf16[256,128]{1,0:T(8,128)(2,1)S(1)}, u32[]{:S(2)}, u32[]{:S(2)}) collective-permute-start(bf16[256,128]{1,0:T(8,128)(2,1)S(1)} %get-tuple-element.19), channel_id=1, source_target_pairs={{4,8},{8,4},{12,16},{16,12},{20,24},{24,20},{5,9},{9,5},{13,17},{1... | collective-permute-start | bytes 196616 | tf_op jit(solution)/shard_map/ppermute | solution.py:352
  16.4 5.6 %collective-permute-start.3 = (bf16[256,128]{1,0:T(8,128)(2,1)S(1)}, bf16[256,128]{1,0:T(8,128)(2,1)S(1)}, u32[]{:S(2)}, u32[]{:S(2)}) collective-permute-start(bf16[256,128]{1,0:T(8,128)(2,1)S(1)} %get-tuple-element.21), channel_id=1, source_target_pairs={{1,2},{2,1},{5,6},{6,5},{9,10},{10,9},{13,14},{14,13},{17,18},{18,... | collective-permute-start | bytes 196616 | tf_op jit(solution)/shard_map/ppermute | solution.py:352
  19.8 2.3 %copy-start.17 = (s32[8,6]{1,0:T(8,128)S(1)}, s32[8,6]{1,0:T(8,128)}, u32[]{:S(2)}) copy-start(s32[8,6]{1,0:T(8,128)} %nb.3) | copy-start | bytes 580
  22.1 1.0 %copy-start.3 = (bf16[4,128,256]{2,1,0:T(8,128)(2,1)S(1)}, bf16[4,128,256]{2,1,0:T(8,128)(2,1)}, u32[]{:S(2)}) copy-start(bf16[4,128,256]{2,1,0:T(8,128)(2,1)} %constant.26.clone.turn_xy) | copy-start | bytes 786436
  23.0 0.9 %copy-start.5 = (bf16[2,128,512]{2,1,0:T(8,128)(2,1)S(1)}, bf16[2,128,512]{2,1,0:T(8,128)(2,1)}, u32[]{:S(2)}) copy-start(bf16[2,128,512]{2,1,0:T(8,128)(2,1)} %constant.27.clone.spread) | copy-start | bytes 786436
  24.0 0.9 %copy-start.8 = (bf16[4,256,128]{2,1,0:T(8,128)(2,1)S(1)}, bf16[4,256,128]{2,1,0:T(8,128)(2,1)}, u32[]{:S(2)}) copy-start(bf16[4,256,128]{2,1,0:T(8,128)(2,1)} %constant.28.clone.pack_ref.pack) | copy-start | bytes 786436
  26.6 0.9 %copy-start.15 = (bf16[128,512]{1,0:T(8,128)(2,1)S(1)}, bf16[128,512]{1,0:T(8,128)(2,1)}, u32[]{:S(2)}) copy-start(bf16[128,512]{1,0:T(8,128)(2,1)} %down_ref.1) | copy-start | bytes 393220
  34.3 1.4 %collective-permute-start.10 = (bf16[448,128]{1,0:T(8,128)(2,1)S(1)}, bf16[448,128]{1,0:T(8,128)(2,1)S(1)}, u32[]{:S(2)}, u32[]{:S(2)}) collective-permute-start(bf16[448,128]{1,0:T(8,128)(2,1)S(1)} %dynamic-slice_convert_fusion), channel_id=1, source_target_pairs={{0,1},{1,0},{2,3},{3,2},{4,5},{5,4},{6,7},{7,6},{8,9},{9,8},{10,11... | collective-permute-start | bytes 344072 | tf_op jit(solution)/shard_map/ppermute | solution.py:344
  35.7 4.7 %collective-permute-start.11 = (bf16[448,128]{1,0:T(8,128)(2,1)S(1)}, bf16[448,128]{1,0:T(8,128)(2,1)S(1)}, u32[]{:S(2)}, u32[]{:S(2)}) collective-permute-start(bf16[448,128]{1,0:T(8,128)(2,1)S(1)} %fusion.2), channel_id=1, source_target_pairs={{0,2},{1,3},{2,0},{3,1},{4,6},{5,7},{6,4},{7,5},{8,10},{9,11},{10,... | collective-permute-start | bytes 344072 | tf_op jit(solution)/shard_map/ppermute | solution.py:344
  40.4 3.7 %collective-permute-start.12 = (bf16[448,128]{1,0:T(8,128)(2,1)S(1)}, bf16[448,128]{1,0:T(8,128)(2,1)S(1)}, u32[]{:S(2)}, u32[]{:S(2)}) collective-permute-start(bf16[448,128]{1,0:T(8,128)(2,1)S(1)} %fusion), channel_id=1, source_target_pairs={{0,4},{4,0},{8,12},{12,8},{16,20},{20,16},{24,28},{28,24},{1,5},{5... | collective-permute-start | bytes 344072 | tf_op jit(solution)/shard_map/ppermute | solution.py:344
  44.2 3.7 %collective-permute-start.13 = (bf16[448,128]{1,0:T(8,128)(2,1)S(1)}, bf16[448,128]{1,0:T(8,128)(2,1)S(1)}, u32[]{:S(2)}, u32[]{:S(2)}) collective-permute-start(bf16[448,128]{1,0:T(8,128)(2,1)S(1)} %get-tuple-element.31), channel_id=1, source_target_pairs={{0,8},{4,12},{8,0},{12,4},{16,24},{20,28},{24,16},{28,20},{1,9},{5... | collective-permute-start | bytes 344072 | tf_op jit(solution)/shard_map/ppermute | solution.py:344
  44.7 9.2 %collective-permute-start.5 = (bf16[768,128]{1,0:T(8,128)(2,1)S(1)}, bf16[768,128]{1,0:T(8,128)(2,1)S(1)}, u32[]{:S(2)}, u32[]{:S(2)}) collective-permute-start(bf16[768,128]{1,0:T(8,128)(2,1)S(1)} %get-tuple-element.22.own), channel_id=1, source_target_pairs={{0,4},{4,0},{8,12},{12,8},{16,20},{20,16},{24,28},{28,24},{1,5},{5... | collective-permute-start | bytes 589832 | tf_op jit(solution)/shard_map/ppermute | solution.py:344
  48.0 6.6 %collective-permute-start.14 = (bf16[448,128]{1,0:T(8,128)(2,1)S(1)}, bf16[448,128]{1,0:T(8,128)(2,1)S(1)}, u32[]{:S(2)}, u32[]{:S(2)}) collective-permute-start(bf16[448,128]{1,0:T(8,128)(2,1)S(1)} %fusion.1), channel_id=1, source_target_pairs={{0,16},{4,20},{8,24},{12,28},{16,0},{20,4},{24,8},{28,12},{1,17},{... | collective-permute-start | bytes 344072 | tf_op jit(solution)/shard_map/ppermute | solution.py:344
  50.3 16.7 %collective-permute-start.6 = (bf16[768,128]{1,0:T(8,128)(2,1)S(1)}, bf16[768,128]{1,0:T(8,128)(2,1)S(1)}, u32[]{:S(2)}, u32[]{:S(2)}) collective-permute-start(bf16[768,128]{1,0:T(8,128)(2,1)S(1)} %get-tuple-element.23), channel_id=1, source_target_pairs={{0,1},{1,0},{2,3},{3,2},{4,5},{5,4},{6,7},{7,6},{8,9},{9,8},{10,11... | collective-permute-start | bytes 589832 | tf_op jit(solution)/shard_map/ppermute | solution.py:344
  54.6 10.3 %copy-start.12 = (bf16[64,448]{1,0:T(8,128)(2,1)S(1)}, bf16[64,448]{1,0:T(8,128)(2,1)}, u32[]{:S(2)}) copy-start(bf16[64,448]{1,0:T(8,128)(2,1)} %conv_ref.1) | copy-start | bytes 172036
  54.6 16.8 %collective-permute-start.7 = (bf16[512,128]{1,0:T(8,128)(2,1)}, bf16[512,128]{1,0:T(8,128)(2,1)S(1)}, u32[]{:S(2)}, u32[]{:S(2)}) collective-permute-start(bf16[512,128]{1,0:T(8,128)(2,1)} %slice.9), channel_id=1, source_target_pairs={{0,1},{1,0},{2,3},{3,2},{4,5},{5,4},{6,7},{7,6},{8,9},{9,8},{10,11... | collective-permute-start | bytes 393224 | tf_op jit(solution)/shard_map/ppermute | solution.py:344
  54.6 18.0 %collective-permute-start.15 = (bf16[448,128]{1,0:T(8,128)(2,1)S(1)}, bf16[448,128]{1,0:T(8,128)(2,1)S(1)}, u32[]{:S(2)}, u32[]{:S(2)}) collective-permute-start(bf16[448,128]{1,0:T(8,128)(2,1)S(1)} %add_convert_fusion), channel_id=1, source_target_pairs={{0,1},{1,0},{2,3},{3,2},{4,5},{5,4},{6,7},{7,6},{8,9},{9,8},{10,11... | collective-permute-start | bytes 344072 | tf_op jit(solution)/shard_map/ppermute | solution.py:344
  57.5 7.8 %collective-permute-start.8 = (bf16[256,128]{1,0:T(8,128)(2,1)S(1)}, bf16[256,128]{1,0:T(8,128)(2,1)S(1)}, u32[]{:S(2)}, u32[]{:S(2)}) collective-permute-start(bf16[256,128]{1,0:T(8,128)(2,1)S(1)} %get-tuple-element.25), channel_id=1, source_target_pairs={{4,8},{8,4},{12,16},{16,12},{20,24},{24,20},{5,9},{9,5},{13,17},{1... | collective-permute-start | bytes 196616 | tf_op jit(solution)/shard_map/ppermute | solution.py:352
  61.5 5.6 %collective-permute-start.9 = (bf16[256,128]{1,0:T(8,128)(2,1)S(1)}, bf16[256,128]{1,0:T(8,128)(2,1)S(1)}, u32[]{:S(2)}, u32[]{:S(2)}) collective-permute-start(bf16[256,128]{1,0:T(8,128)(2,1)S(1)} %get-tuple-element.26), channel_id=1, source_target_pairs={{1,2},{2,1},{5,6},{6,5},{9,10},{10,9},{13,14},{14,13},{17,18},{18,... | collective-permute-start | bytes 196616 | tf_op jit(solution)/shard_map/ppermute | solution.py:352
  64.8 2.2 %copy-start.6 = (bf16[2,128,512]{2,1,0:T(8,128)(2,1)S(1)}, bf16[2,128,512]{2,1,0:T(8,128)(2,1)}, u32[]{:S(2)}) copy-start(bf16[2,128,512]{2,1,0:T(8,128)(2,1)} %constant.27.clone.spread) | copy-start | bytes 786436
  65.0 2.1 %copy-start.4 = (bf16[4,128,256]{2,1,0:T(8,128)(2,1)S(1)}, bf16[4,128,256]{2,1,0:T(8,128)(2,1)}, u32[]{:S(2)}) copy-start(bf16[4,128,256]{2,1,0:T(8,128)(2,1)} %constant.26.clone.turn_xy) | copy-start | bytes 786436
  65.2 1.9 %copy-start.14 = (bf16[128,256]{1,0:T(8,128)(2,1)S(1)}, bf16[128,256]{1,0:T(8,128)(2,1)}, u32[]{:S(2)}) copy-start(bf16[128,256]{1,0:T(8,128)(2,1)} %constant.25.clone.turn_z) | copy-start | bytes 196612
  (3 other events, 2.3 us)

commit v2 on v1

v2 whole, which is shorter than its diff:
```python
import jax
import jax.numpy as jnp
from jax import lax
from jax.experimental import pallas as pl
from jax.experimental.pallas import tpu as pltpu
from jax.sharding import PartitionSpec as P

BF = jnp.bfloat16
F32 = jnp.float32
C = 64
SLOTS = 8
NT = (((1,), (1,)), ((), ()))
TN = (((0,), (0,)), ((), ()))


def one_hot(source, rows):
    row = lax.broadcasted_iota(jnp.int32, (rows, source.shape[1]), 0)
    return jnp.where(row == source, 1.0, 0.0).astype(BF)


def lanes_of(count):
    lane = lax.broadcasted_iota(jnp.int32, (1, count), 1)
    return lane, lane // 64 % 2, lane // 16 % 4, lane // 4 % 4, lane % 4


def cell(r, a, b, c):
    return r * 64 + (a + 4) % 4 * 16 + (b + 4) % 4 * 4 + (c + 4) % 4


def turn_z():
    lane, r, a, b, c = lanes_of(256)
    step = jnp.where(lane < 128, jnp.where(r == 0, -1, 0), jnp.where(r == 1, 1, 0))
    return one_hot(cell(1 - r, a, b, c + step), 128)


def turn_xy(k):
    lane, r, a, b, c = lanes_of(256)
    x = 1 - 2 * (k // 2)
    y = 1 - 2 * (k % 2)
    first = lane < 128
    return one_hot(cell(r, a + jnp.where(first, x, 0), b + jnp.where(first, 0, y), c), 128)


def spread(axis, want=None):
    lane, r, a, b, c = lanes_of(512)
    place, other = (a, b) if axis == 0 else (b, a)
    source = lane // 256 * 64 + lane // 128 % 2 * 32 + r * 16 + other * 4 + c
    if want is not None:
        source = jnp.where(place == want, source, -1)
    return one_hot(source, 128)


def pack(direction):
    lane = lanes_of(128)[0] % 64
    want = 3 * (1 - direction % 2)
    half, r, other, c = lane // 32, lane // 16 % 2, lane // 4 % 4, lane % 4
    a, b = (want, other) if direction < 2 else (other, want)
    return one_hot(half * 128 + cell(r, a, b, c), 256)


def regroup():
    lane = lanes_of(512)[0]
    return one_hot(lane % 8 * 64 + lane // 8, 512)


CONV, DOWN, DOWN_BACK, POOL, POOL_Z, STORE = 0, 64, 192, 704, 1728, 2880


def pool_at(store, d, slot):
    rows = pl.ds(pl.multiple_of(POOL + (d // 2 * SLOTS + slot) * C, C), C)
    return store[rows, d % 2 * 256 : d % 2 * 256 + 256]


def pool_z_at(store, d, slot):
    return store[pl.ds(pl.multiple_of(POOL_Z + (d * 9 + slot) * C, C), C), :]


def dot(left, right, dims=None):
    if dims is None:
        return jnp.dot(left, right, preferred_element_type=F32)
    return lax.dot_general(left, right, dims, preferred_element_type=F32)


def lane_of(shape):
    return lax.broadcasted_iota(jnp.int32, shape, len(shape) - 1)


def parts(block, direction):
    if direction == 0:
        return block[:, 256:512]
    if direction == 1:
        return block[:, 0:256]
    first = 128 if direction == 2 else 0
    return jnp.concatenate([block[:, first : first + 128], block[:, first + 256 : first + 384]], 1)


def roll_blocks(source, put, put_z):
    up = turn_z()
    for k in range(4):
        chunk = source[:, k * 128 : (k + 1) * 128]
        moved = dot(chunk, turn_xy(k)).astype(BF)
        x_dir, y_dir = 1 - k // 2, 3 - k % 2
        put(x_dir, k % 2 * 128, moved[:, 0:128])
        put(y_dir, k // 2 * 128, moved[:, 128:256])
        moved = dot(chunk, up).astype(BF)
        put_z(0, k * 128, moved[:, 0:128])
        put_z(1, k * 128, moved[:, 128:256])


def rim_masks():
    lane = lane_of((C, 256))
    a, b = lane // 16 % 4, lane // 4 % 4
    masks = [a == 0, a == 3, b == 0, b == 3]
    lane = lane_of((C, 512))
    r, c = lane // 64 % 2, lane % 4
    return masks, [(r == 0) & (c == 0), (r == 1) & (c == 3)]


def weave(direction, moved, block):
    if direction == 0:
        return [moved[:, 0:128], moved[:, 128:256], block[:, 0:128], block[:, 128:256]]
    if direction == 1:
        return [block[:, 256:384], block[:, 384:512], moved[:, 0:128], moved[:, 128:256]]
    if direction == 2:
        return [moved[:, 0:128], block[:, 0:128], moved[:, 128:256], block[:, 256:384]]
    return [block[:, 128:256], moved[:, 0:128], block[:, 384:512], moved[:, 128:256]]


def parities():
    return lax.rem(lax.axis_index("gx"), 2), lax.rem(lax.axis_index("gy"), 2)


def load(pairs, sems):
    copies = [pltpu.make_async_copy(src, dst, sems.at[i]) for i, (src, dst) in enumerate(pairs)]
    for copy in copies:
        copy.start()
    return copies


def pack_kernel(
    counts, cmap_hbm, x_hbm, lat_hbm,
    xm, send_xa, send_xb, send_ya, send_yb,
    cmap, sems,
):
    copies = load(
        [
            (cmap_hbm, cmap), (x_hbm, xm),
            (lat_hbm, send_xa.at[256:768]), (lat_hbm, send_ya.at[256:768]),
        ],
        sems,
    )
    px, py = parities()
    packs = [pack(d) for d in range(4)]
    for copy in copies[:2]:
        copy.wait()
    for b in range(1, SLOTS):
        @pl.when(b >= counts[0])
        def _():
            xm[b * C : (b + 1) * C, :] = jnp.zeros((C, 512), BF)
    masked = xm[...]
    low = lane_of((256, 128)) < 64
    faces = []
    for d in range(4):
        packed = dot(parts(masked, d), packs[d])
        faces.append(jnp.where(low, packed[0:256], packed[256:512]))
    even = px == 0
    send_xa[0:256, :] = jnp.where(even, faces[0], faces[1]).astype(BF)
    send_xb[...] = jnp.where(even, faces[1], faces[0]).astype(BF)
    even = py == 0
    send_ya[0:256, :] = jnp.where(even, faces[2], faces[3]).astype(BF)
    send_yb[...] = jnp.where(even, faces[3], faces[2]).astype(BF)
    row = lax.broadcasted_iota(jnp.int32, (16, 128), 0)
    named = jnp.zeros((16, 128), jnp.int32)
    for k in range(8):
        named = jnp.where(row == k, cmap[0, k], named)
    named = named.astype(F32).astype(BF)
    send_xa[768:784, :] = named
    send_ya[768:784, :] = named
    for copy in copies[2:]:
        copy.wait()


def prep_kernel(xm, conv_hbm, down_hbm, head_hbm, store, conv, sems):
    copies = load(
        [
            (down_hbm, store.at[DOWN : DOWN + 128]),
            (conv_hbm, conv),
            (head_hbm, store.at[DOWN_BACK : DOWN_BACK + 128, 128:256]),
        ],
        sems,
    )
    for d in range(2):
        start = POOL_Z + (d * 9 + SLOTS) * C
        store[start : start + C, :] = jnp.zeros((C, 512), BF)

    def put(d, lane, value):
        rows = slice(POOL + d // 2 * 512, POOL + d // 2 * 512 + 512)
        store[rows, d % 2 * 256 + lane : d % 2 * 256 + lane + 128] = value

    def put_z(d, lane, value):
        start = POOL_Z + d * 9 * C
        store[start : start + 512, lane : lane + 128] = value

    roll_blocks(xm, put, put_z)
    copies[0].wait()
    down = store[DOWN : DOWN + 128, :]
    table = regroup()
    store[DOWN : DOWN + 128, :] = dot(down, table, NT).astype(BF)
    store[DOWN_BACK : DOWN_BACK + 512, 0:128] = dot(table, down, NT).astype(BF)
    copies[1].wait()
    store[CONV : CONV + C, 0:448] = conv[...]
    copies[2].wait()


YA, OCT, XA, XB, YB, SEND = 0, 256, 768, 1024, 1280, 1536


def main_kernel(
    nb, cmap, lat_hbm,
    xm, got_xa, got_xb, got_ya, got_yb, got_xy, store,
    hg_ref, mine_ref, other_ref, send,
    sums_ref, lat_ref, lat_sem, reach, taps, slope, act2, routed, far, maps_v, maps_s, sem,
):
    px, py = parities()
    for j, got in enumerate((got_xa, got_ya)):
        maps_v[j] = got[768:784, :].astype(F32).astype(jnp.int32)
    maps_v[2] = got_xy[512:528, :].astype(F32).astype(jnp.int32)
    copy = pltpu.make_async_copy(maps_v, maps_s, sem)
    copy.start()
    lat_copy = pltpu.make_async_copy(lat_hbm, lat_ref, lat_sem)
    lat_copy.start()
    head = store[DOWN_BACK : DOWN_BACK + 128, 128:256]

    spreads = [spread(axis) for axis in range(2)]
    for got, axis, direction in (
        (got_xa, 0, 1 - px), (got_xb, 0, px), (got_ya, 1, 3 - py), (got_yb, 1, 2 + py),
    ):
        wide = dot(got[0:256, :], spreads[axis]).astype(BF).reshape(4, C, 512)
        reach[direction, 8:12] = wide[:, :, 0:256]
        reach[direction, 12:16] = wide[:, :, 256:512]
    for d in range(4):
        for b in range(SLOTS):
            reach[d, b] = pool_at(store, d, b)
        reach[d, 16] = jnp.zeros((C, 256), BF)

    masks, masks_z = rim_masks()
    low = lane_of((C, 128)) < 64
    conv = store[CONV : CONV + C, 0:448]
    for pair in range(SLOTS // 2):
        acts = []
        for b in (2 * pair, 2 * pair + 1):
            block = xm[b * C : (b + 1) * C, :]
            taps[b, 0:C, :] = block
            for d in range(4):
                moved = jnp.where(masks[d], reach[d, nb[b, d]], reach[d, b])
                for k, piece in enumerate(weave(d, moved, block)):
                    taps[b, (d + 1) * C : (d + 2) * C, k * 128 : (k + 1) * 128] = piece
            for d in range(2):
                near = jnp.minimum(nb[b, d + 4], SLOTS)
                taps[b, (d + 5) * C : (d + 6) * C, :] = jnp.where(
                    masks_z[d], pool_z_at(store, d, near), pool_z_at(store, d, b)
                )
            hidden = dot(conv, taps[b])
            gate = 0.5 * jnp.tanh(0.5 * hidden) + 0.5
            slope[b] = gate * (1.0 + hidden * (1.0 - gate))
            acts.append(hidden * gate)
        lanes = slice(pair * 128, (pair + 1) * 128)
        for k in range(4):
            one, two = (v[:, k * 128 : (k + 1) * 128] for v in acts)
            first = jnp.where(low, one, pltpu.roll(two, 64, 1))
            second = jnp.where(low, pltpu.roll(one, 64, 1), two)
            act2[2 * k * C : (2 * k + 1) * C, lanes] = first.astype(BF)
            act2[(2 * k + 1) * C : (2 * k + 2) * C, lanes] = second.astype(BF)

    octants = dot(store[DOWN : DOWN + 128, :], act2[...]).astype(BF).astype(F32)
    gate = 0.5 * jnp.tanh(0.5 * octants) + 0.5
    oct_act = (octants * gate).astype(BF)
    oct_slope = gate * (1.0 + octants * (1.0 - gate))
    projected = dot(head, oct_act).T.astype(BF)
    send[OCT : OCT + 512, :] = projected

    copy.wait()
    lat_copy.wait()
    for s in range(SLOTS):
        routed[s] = jnp.zeros((C, 128), BF)
    for j, (got, start) in enumerate(((lat_ref, 0), (got_xa, 256), (got_ya, 256), (got_xy, 0))):
        for k in range(8):
            name = cmap[0, k] if j == 0 else maps_s[j - 1, k, 0]
            name = name - j * SLOTS
            name = jnp.where((name >= 0) & (name < SLOTS), name, SLOTS)
            routed[name] = got[start + k * C : start + (k + 1) * C, :]
    grad = routed[0:SLOTS].reshape(SLOTS * C, 128)
    head_back = head.astype(F32).T.astype(BF)
    oct_grad = (dot(head_back, grad, NT) * oct_slope).astype(BF)
    sums_ref[768:896, :] = dot(oct_act, grad).T
    down_sum = dot(oct_grad, act2[...], NT)
    for k in range(4):
        sums_ref[256 + k * 128 : 256 + (k + 1) * 128, :] = down_sum[:, k * 128 : (k + 1) * 128]
    conv_sum = jnp.zeros((C, 448), F32)
    for pair in range(SLOTS // 2):
        patch = dot(store[DOWN_BACK : DOWN_BACK + 512, 0:128], oct_grad[:, pair * 128 : (pair + 1) * 128])
        for side in range(2):
            b = 2 * pair + side
            for k in range(4):
                first = patch[2 * k * C : (2 * k + 1) * C]
                second = patch[(2 * k + 1) * C : (2 * k + 2) * C]
                if side == 0:
                    both = jnp.where(low, first, pltpu.roll(second, 64, 1))
                else:
                    both = jnp.where(low, pltpu.roll(first, 64, 1), second)
                lanes = slice(k * 128, (k + 1) * 128)
                hg_ref[b * C : (b + 1) * C, lanes] = (both * slope[b, :, lanes]).astype(BF)
            conv_sum = conv_sum + dot(hg_ref[b * C : (b + 1) * C, :], taps[b], NT)
    for k in range(3):
        sums_ref[k * C : (k + 1) * C, :] = conv_sum[:, k * 128 : (k + 1) * 128]
    sums_ref[3 * C : 4 * C, 0:C] = conv_sum[:, 384:448]
    sums_ref[3 * C : 4 * C, C:128] = jnp.zeros((C, C), F32)

    first, second = sums_ref[0:448, :].astype(BF), sums_ref[448:896, :].astype(BF)
    mine_ref[...] = jnp.where(py == 0, first, second)
    other_ref[...] = jnp.where(py == 0, second, first)

    for d in range(4):
        for s in range(5):
            far[d, s] = jnp.zeros((C, 128), F32)
    high = lane_of((C, 128)) // 64
    for d in range(4):
        face = dot(parts(hg_ref[...], d ^ 1), pack(d ^ 1))
        for b in range(SLOTS):
            name = nb[b, d] - SLOTS
            away = (name >= 0) & (name < SLOTS)
            row = jnp.where(away, lax.rem(name, 4), 4)
            side = jnp.where(name >= 4, 1, 0)
            far[d, row] += jnp.where(high == side, face[b * C : (b + 1) * C, :], 0.0)
    for at, d in ((XA, 1 - px), (XB, px), (YA, 3 - py), (YB, 2 + py)):
        send[at : at + 256, :] = far[d, 0:4].reshape(256, 128).astype(BF)


def roll_kernel(nb, hg_ref, moved_ref, pool, pool_z, total, total_z):
    def put(d, lane, value):
        pool[d, :, :, lane : lane + 128] = value.reshape(SLOTS, C, 128)

    def put_z(d, lane, value):
        pool_z[d, :, :, lane : lane + 128] = value.reshape(SLOTS, C, 128)

    roll_blocks(hg_ref, put, put_z)
    for s in range(SLOTS):
        for d in range(4):
            total[d, s] = jnp.zeros((C, 256), F32)
        for d in range(2):
            total_z[d, s] = jnp.zeros((C, 512), F32)
    for b in range(SLOTS):
        for d in range(4):
            slot = jnp.minimum(nb[b, d], SLOTS)
            total[d, slot] += pool[d ^ 1, b].astype(F32)
        for d in range(2):
            slot = jnp.minimum(nb[b, d + 4], SLOTS)
            total_z[d, slot] += pool_z[1 - d, b].astype(F32)
    masks, masks_z = rim_masks()
    for b in range(SLOTS):
        for d in range(4):
            rows = slice((d // 2 * SLOTS + b) * C, (d // 2 * SLOTS + b + 1) * C)
            moved_ref[rows, d % 2 * 256 : d % 2 * 256 + 256] = jnp.where(
                masks[d ^ 1], total[d, b].astype(BF), pool[d ^ 1, b]
            )
        for d in range(2):
            rows = slice(((d + 2) * SLOTS + b) * C, ((d + 2) * SLOTS + b + 1) * C)
            moved_ref[rows, :] = jnp.where(
                masks_z[1 - d], total_z[d, b].astype(BF), pool_z[1 - d, b]
            )


def near_kernel(hg_ref, moved_ref, conv_ref, near_ref, fields):
    conv = jnp.concatenate([conv_ref[:, d * C : (d + 1) * C] for d in range(7)], 0)
    for b in range(SLOTS):
        block = hg_ref[b * C : (b + 1) * C, :]
        fields[0:C, :] = block
        for d in range(4):
            rows = slice((d // 2 * SLOTS + b) * C, (d // 2 * SLOTS + b + 1) * C)
            moved = moved_ref[rows, d % 2 * 256 : d % 2 * 256 + 256]
            for k, piece in enumerate(weave(d ^ 1, moved, block)):
                fields[(d + 1) * C : (d + 2) * C, k * 128 : (k + 1) * 128] = piece
        for d in range(2):
            rows = slice(((d + 2) * SLOTS + b) * C, ((d + 2) * SLOTS + b + 1) * C)
            fields[(d + 5) * C : (d + 6) * C, :] = moved_ref[rows, :]
        near_ref[b * C : (b + 1) * C, :] = dot(conv, fields[...], TN)


def far_kernel(counts, near_ref, got_xa, got_xb, got_ya, got_yb, conv_ref, out_ref, rows):
    px, py = parities()
    for got, direction in ((got_xa, px), (got_xb, 1 - px), (got_ya, 2 + py), (got_yb, 3 - py)):
        rows[direction] = got[0:256, :]
    fields = []
    for d in range(4):
        conv = conv_ref[:, (d + 1) * C : (d + 2) * C]
        moved = [dot(conv, rows[d, k * C : (k + 1) * C, :], TN).astype(BF) for k in range(4)]
        table = spread(d // 2, 3 * (1 - d % 2))
        fields.append(dot(jnp.concatenate(moved, 0), table))
    for b in range(SLOTS):
        x_low, x_high, y_low, y_high = (
            fields[d][b % 4 * C : (b % 4 + 1) * C, b // 4 * 256 : b // 4 * 256 + 256]
            for d in (1, 0, 3, 2)
        )
        for k in range(4):
            lanes = slice(k * 128, (k + 1) * 128)
            x, y = (x_low, x_high)[k // 2], (y_low, y_high)[k % 2]
            x, y = (v[:, i * 128 : (i + 1) * 128] for v, i in ((x, k % 2), (y, k // 2)))
            grad = near_ref[b * C : (b + 1) * C, lanes] + (x + y)
            out_ref[b * C : (b + 1) * C, lanes] = jnp.where(b < counts[0], grad, 0.0).astype(BF)


def latent_kernel(cmap, own, got_x, got_ya, got_xy, out_ref, rows):
    rows[0:8] = own[OCT : OCT + 512, :].reshape(8, C, 128)
    rows[8:16] = got_x[...].reshape(8, C, 128)
    rows[16:24] = got_ya[256:768, :].reshape(8, C, 128)
    rows[24:32] = got_xy[...].reshape(8, C, 128)
    rows[32] = jnp.zeros((C, 128), BF)
    for k in range(8):
        out_ref[k * C : (k + 1) * C, :] = rows[cmap[0, k]]


def scale_kernel(scale, conv_in, conv_out, down_out, head_out):
    for k in range(3):
        conv_out[:, k * 128 : (k + 1) * 128] = conv_in[k * C : (k + 1) * C, :].astype(F32) * scale
    conv_out[:, 384:448] = conv_in[3 * C : 4 * C, 0:C].astype(F32) * scale
    down = jnp.concatenate([conv_in[256 + k * 128 : 384 + k * 128, :] for k in range(4)], 1)
    down_out[...] = dot(down, regroup()) * scale
    head_out[...] = conv_in[768:896, :].astype(F32) * scale


def swap(value, axis, bit):
    count = lax.axis_size(axis)
    return lax.ppermute(value, axis, [(i, i ^ bit) for i in range(count)])


def swap_odd(value, axis):
    count = lax.axis_size(axis)
    route = []
    for low in range(1, count - 1, 2):
        route += [(low, low + 1), (low + 1, low)]
    return lax.ppermute(value, axis, route)


def tie(value, *others):
    return lax.optimization_barrier((value, *others))[0]


def core_swap(value, first, second):
    nx, ny = lax.axis_size("gx"), lax.axis_size("gy")
    route = []
    for i in range(nx):
        for j in range(ny):
            axis, bit = (first, second)[j % 2]
            there = (i ^ bit, j) if axis == "gx" else (i, j ^ bit)
            route.append((i * ny + j, there[0] * ny + there[1]))
    return lax.ppermute(value, ("gx", "gy"), route)


def weight_sums(mine, other):
    bit = lax.rem(lax.axis_index("gy"), 2)
    steps = []
    for axis, first in (("gy", 2), ("gx", 1)):
        step = first
        while step < lax.axis_size(axis):
            steps.append((axis, step))
            step *= 2
    steps.append(steps.pop(0))
    turned = []
    for at in range(0, len(steps) - 1, 2):
        turned += [steps[at + 1], steps[at]]
    turned += steps[len(turned) :]
    state = {"sum": mine}

    def step(at, waits):
        sent = tie(state["sum"], *waits) if waits else state["sum"]
        if at > len(steps):
            theirs = swap(sent, "gy", 1)
            return jnp.where(
                bit == 0, jnp.concatenate([sent, theirs]), jnp.concatenate([theirs, sent])
            )
        if at == 0:
            there = swap(other, "gy", 1)
        else:
            there = core_swap(sent, steps[at - 1], turned[at - 1])
        state["sum"] = (sent.astype(F32) + there.astype(F32)).astype(BF)
        return state["sum"]

    return step, len(steps) + 1


def call(kernel, outs, ins, spaces="", scratch=(), last=0, us=1.0):
    kinds = {"s": pltpu.SMEM, "h": pltpu.HBM, "v": pltpu.VMEM}
    spaces = spaces + "v" * (len(ins) - len(spaces))
    ins = [
        pltpu.with_memory_space_constraint(value, pltpu.HBM) if space == "h" else value
        for value, space in zip(ins, spaces)
    ]
    keep = len(outs) - last
    return pl.pallas_call(
        kernel,
        out_shape=[
            pltpu.VMEM(shape, kind) if at < keep else jax.ShapeDtypeStruct(shape, kind)
            for at, (shape, kind) in enumerate(outs)
        ],
        in_specs=[pl.BlockSpec(memory_space=kinds[k]) for k in spaces],
        out_specs=[pl.BlockSpec(memory_space=pltpu.VMEM)] * len(outs),
        scratch_shapes=list(scratch),
        compiler_params=pltpu.CompilerParams(vmem_limit_bytes=32 * 1024 * 1024),
        cost_estimate=pl.CostEstimate(
            flops=int(us * 1e9), bytes_accessed=int(us * 3e6), transcendentals=0
        ),
    )(*ins)


def body(
    features, neighbours, counts, conv_weight, down_weight, head_weight, coarse_map, latent_grad
):
    flat = features.reshape(SLOTS * C, 512)
    lat = latent_grad.reshape(512, 128)
    xm, send_xa, send_xb, send_ya, send_yb = call(
        pack_kernel,
        [
            ((512, 512), BF),
            ((784, 128), BF), ((256, 128), BF), ((784, 128), BF), ((256, 128), BF),
        ],
        (counts, coarse_map, flat, lat),
        "shhh",
        [pltpu.SMEM((1, 8), jnp.int32), pltpu.SemaphoreType.DMA((4,))],
        us=1.5,
    )
    got_xa = swap(send_xa, "gx", 1)
    got_xb = swap_odd(send_xb, "gx")
    got_ya = swap(send_ya, "gy", 1)
    got_yb = swap_odd(send_yb, "gy")
    (store,) = call(
        prep_kernel,
        [((STORE, 512), BF)],
        (xm, conv_weight, down_weight, head_weight),
        "vhhh",
        [pltpu.VMEM((C, 448), BF), pltpu.SemaphoreType.DMA((3,))],
        us=1.5,
    )
    got_xy = swap(tie(got_xa[256:784], got_xb, got_yb, got_ya), "gy", 1)
    hg, mine, other, send = call(
        main_kernel,
        [((512, 512), BF), ((448, 128), BF), ((448, 128), BF), ((SEND, 128), BF)],
        (neighbours, coarse_map, lat, xm, got_xa, got_xb, got_ya, got_yb, got_xy, store),
        "ssh",
        [
            pltpu.VMEM((896, 128), F32),
            pltpu.VMEM((512, 128), BF),
            pltpu.SemaphoreType.DMA,
            pltpu.VMEM((4, 17, C, 256), BF),
            pltpu.VMEM((SLOTS, 448, 512), BF),
            pltpu.VMEM((SLOTS, C, 512), F32),
            pltpu.VMEM((512, 512), BF),
            pltpu.VMEM((SLOTS + 1, C, 128), BF),
            pltpu.VMEM((4, 5, C, 128), F32),
            pltpu.VMEM((3, 16, 128), jnp.int32),
            pltpu.SMEM((3, 16, 128), jnp.int32),
            pltpu.SemaphoreType.DMA,
        ],
        us=6.0,
    )

    sum_step, steps = weight_sums(mine, other)
    mine = sum_step(0, ())
    got_xa = swap(tie(send[XA : XA + 256], mine), "gx", 1)
    got_xb = swap_odd(tie(send[XB : XB + 256], mine), "gx")
    got_yb = swap_odd(tie(send[YB : YB + 256], mine), "gy")
    (moved,) = call(
        roll_kernel,
        [((2048, 512), BF)],
        (neighbours, tie(hg, mine, got_yb)),
        "s",
        [
            pltpu.VMEM((4, 8, C, 256), BF),
            pltpu.VMEM((2, 8, C, 512), BF),
            pltpu.VMEM((4, 9, C, 256), F32),
            pltpu.VMEM((2, 9, C, 512), F32),
        ],
        us=2.5,
    )
    mine = sum_step(1, ())
    got_ya = swap(tie(send[YA : OCT + 512], mine), "gy", 1)
    (near,) = call(
        near_kernel,
        [((512, 512), F32)],
        (hg, tie(moved, mine), conv_weight),
        "",
        [pltpu.VMEM((448, 512), BF)],
        us=1.0,
    )
    mine = sum_step(2, (got_xa, got_xb, got_yb, moved))
    (grad,) = call(
        far_kernel,
        [((512, 512), BF)],
        (counts, tie(near, mine), got_xa, got_xb, got_ya, got_yb, conv_weight),
        "s",
        [pltpu.VMEM((4, 256, 128), BF)],
        1,
        us=1.8,
    )
    got_x = swap(tie(send[OCT : OCT + 512], grad), "gx", 1)
    mine = sum_step(3, (near, got_ya))
    got_xy = swap(tie(got_x, mine), "gy", 1)
    (latent,) = call(
        latent_kernel,
        [((512, 128), BF)],
        (coarse_map, send, got_x, got_ya, got_xy),
        "s",
        [pltpu.VMEM((33, C, 128), BF)],
        1,
        us=1.2,
    )
    mine = sum_step(4, (grad,))
    for at in range(5, steps):
        mine = sum_step(at, ())
    summed = sum_step(steps, (got_xy,))
    scale = float(SLOTS * lax.axis_size("gx") * lax.axis_size("gy")) ** (-0.5)
    conv_grad, down_grad, head_grad = call(
        lambda *refs: scale_kernel(scale, *refs),
        [((C, 448), F32), ((128, 512), F32), ((128, 128), F32)],
        (summed,),
        last=3,
    )
    return (
        latent.reshape(1, 512, 128), grad.reshape(SLOTS, C, 512), conv_grad, down_grad, head_grad,
    )


def solution(mesh):
    both = ("gx", "gy")
    placed = (
        P(both, None, None), P(both, None), P(both), P(), P(), P(), P(both, None),
        P(both, None, None),
    )
    return jax.shard_map(
        body,
        mesh=mesh,
        in_specs=placed,
        out_specs=(P(both, None, None), P(both, None, None), P(), P(), P()),
        check_vma=False,
    )
```

time: 74.2 us -> 56.6 us (0.76)
  the two profiles are of different devices: /device:TPU:9 before, /device:TPU:7 now
where the time goes in v2:
time: 56.6 us; the launch traced here: 56.3 us
  starting transfers between devices  28.1 us (50%)
  Pallas kernels  17 us (30%)
  waiting for transfers between devices  9.37 us (17%)
  between operations  1.53 us (3%)
    ppermute x9, starting transfers between devices, swap(): return lax.ppermute(value, axis, [(i, i ^ bit) for i in range(count)])  19 us
    pallas_call x8, Pallas kernels, call(): pl.pallas_call(kernel, out_shape=[pltpu.VMEM(shape, kind) if at < keep el...  17 us
    ppermute x4, starting transfers between devices, swap_odd(): return lax.ppermute(value, axis, route)  7.38 us
    ppermute x9, waiting for transfers between devices, swap(): return lax.ppermute(value, axis, [(i, i ^ bit) for i in range(count)])  4.34 us
    ppermute x4, waiting for transfers between devices, swap_odd(): return lax.ppermute(value, axis, route)  3.12 us
    ppermute x4, waiting for transfers between devices, core_swap(): return lax.ppermute(value, ('gx', 'gy'), route)  1.91 us
    ppermute x4, starting transfers between devices, core_swap(): return lax.ppermute(value, ('gx', 'gy'), route)  1.75 us
  transfers between devices with their start and end apart: 17, of which 7 were waited for; matrix products, arithmetic and copies ran while one was open for 0% of the time, Pallas kernels for 14%

profile of v2, /device:TPU:7, one launch (start us, length us, event | category | flops | bytes accessed | tf_op | source)
XLA Modules:
  0.0 56.3 jit_solution(4012073206205958578)
XLA Ops:
  1.3 1.6 %shard_map.119 = (bf16[512,512]{1,0:T(8,128)(2,1)S(1)}, bf16[784,128]{1,0:T(8,128)(2,1)S(1)}, bf16[256,128]{1,0:T(8,128)(2,1)S(1)}, bf16[784,128]{1,0:T(8,128)(2,1)S(1)}, bf16[256,128]{1,0:T(8,128)(2,1)S(1)}) custom-call(s32[1]{0:T(128)S(6)} %copy.13.counts, s32[1,8]{1,0:T(1,128)} %cmap.3, bf16[512,512]{1,0:T(8,128)(2,1)} %bitcast.4, bf16[512,128]{1,0:T(8,128)(2,1)} %bitcast.5), custom_call_target="tpu_custom_call" | custom-call | flops 1500000000 | bytes 4500000 | tf_op jit(solution)/shard_map/pallas_call | solution.py:499
  2.9 0.3 collective-permute-start
  3.2 1.0 %collective-permute-start.2 = (bf16[784,128]{1,0:T(8,128)(2,1)S(1)}, bf16[784,128]{1,0:T(8,128)(2,1)S(1)}, u32[]{:S(2)}, u32[]{:S(2)}) collective-permute-start(bf16[784,128]{1,0:T(8,128)(2,1)S(1)} %get-tuple-element.34), channel_id=1, source_target_pairs={{0,1},{1,0},{2,3},{3,2},{4,5},{5,4},{6,7},{7,6},{8,9},{9,8},{10,11... | collective-permute-start | bytes 602120 | tf_op jit(solution)/shard_map/ppermute | solution.py:433
  4.1 4.1 %collective-permute-start.1 = (bf16[256,128]{1,0:T(8,128)(2,1)S(1)}, bf16[256,128]{1,0:T(8,128)(2,1)S(1)}, u32[]{:S(2)}, u32[]{:S(2)}) collective-permute-start(bf16[256,128]{1,0:T(8,128)(2,1)S(1)} %get-tuple-element.33), channel_id=1, source_target_pairs={{4,8},{8,4},{12,16},{16,12},{20,24},{24,20},{5,9},{9,5},{13,17},{1... | collective-permute-start | bytes 196616 | tf_op jit(solution)/shard_map/ppermute | solution.py:441
  8.3 0.7 %collective-permute-start.3 = (bf16[256,128]{1,0:T(8,128)(2,1)S(1)}, bf16[256,128]{1,0:T(8,128)(2,1)S(1)}, u32[]{:S(2)}, u32[]{:S(2)}) collective-permute-start(bf16[256,128]{1,0:T(8,128)(2,1)S(1)} %get-tuple-element.35), channel_id=1, source_target_pairs={{1,2},{2,1},{5,6},{6,5},{9,10},{10,9},{13,14},{14,13},{17,18},{18,... | collective-permute-start | bytes 196616 | tf_op jit(solution)/shard_map/ppermute | solution.py:441
  9.0 1.7 %collective-permute-done.1.got_xb = bf16[256,128]{1,0:T(8,128)(2,1)S(1)} collective-permute-done((bf16[256,128]{1,0:T(8,128)(2,1)S(1)}, bf16[256,128]{1,0:T(8,128)(2,1)S(1)}, u32[]{:S(2)}, u32[]{:S(2)}) %collective-permute-start.1) | collective-permute-done | bytes 65568 | tf_op jit(solution)/shard_map/ppermute | solution.py:441
  10.7 3.5 %collective-permute-start.4 = (bf16[528,128]{1,0:T(8,128)(2,1)S(1)}, bf16[528,128]{1,0:T(8,128)(2,1)S(1)}, u32[]{:S(2)}, u32[]{:S(2)}) collective-permute-start(bf16[528,128]{1,0:T(8,128)(2,1)S(1)} %slice.24), channel_id=1, source_target_pairs={{0,1},{1,0},{2,3},{3,2},{4,5},{5,4},{6,7},{7,6},{8,9},{9,8},{10,11... | collective-permute-start | bytes 405512 | tf_op jit(solution)/shard_map/ppermute | solution.py:433
  14.1 1.5 %shard_map.120.store = bf16[2880,512]{1,0:T(8,128)(2,1)S(1)} custom-call(bf16[512,512]{1,0:T(8,128)(2,1)S(1)} %get-tuple-element.31.xm, bf16[64,448]{1,0:T(8,128)(2,1)} %conv_ref.3, bf16[128,512]{1,0:T(8,128)(2,1)} %down_hbm.1, bf16[128,128]{1,0:T(8,128)(2,1)} %head_hbm.1), custom_call_target="tpu_custom_call" | custom-call | flops 1500000000 | bytes 4500000 | tf_op jit(solution)/shard_map/pallas_call | solution.py:499
  15.7 6.3 %shard_map.121 = (bf16[512,512]{1,0:T(8,128)(2,1)S(1)}, bf16[448,128]{1,0:T(8,128)(2,1)S(1)}, bf16[448,128]{1,0:T(8,128)(2,1)S(1)}, bf16[1536,128]{1,0:T(8,128)(2,1)S(1)}) custom-call(s32[8,6]{1,0:T(8,128)S(1)} %copy-done.1, s32[1,8]{1,0:T(1,128)S(1)} %copy-done.2, bf16[512,128]{1,0:T(8,128)(2,1)} %bitcast.6, bf16[512,512]{1,0:T(8,128)(2,1)S(1)} %get-tuple-element.31.xm, ...), custom_call_target="tpu_custom_call" | custom-call | flops 6000000000 | bytes 18000000 | tf_op jit(solution)/shard_map/pallas_call | solution.py:499
  22.0 0.1 collective-permute-start.5
  22.1 1.3 %collective-permute-done.5 = bf16[448,128]{1,0:T(8,128)(2,1)S(1)} collective-permute-done((bf16[448,128]{1,0:T(8,128)(2,1)S(1)}, bf16[448,128]{1,0:T(8,128)(2,1)S(1)}, u32[]{:S(2)}, u32[]{:S(2)}) %collective-permute-start.5) | collective-permute-done | bytes 114720 | tf_op jit(solution)/shard_map/ppermute | solution.py:433
  23.5 0.7 %collective-permute-start.6 = (bf16[256,128]{1,0:T(8,128)(2,1)S(1)}, bf16[256,128]{1,0:T(8,128)(2,1)S(1)}, u32[]{:S(2)}, u32[]{:S(2)}) collective-permute-start(bf16[256,128]{1,0:T(8,128)(2,1)S(1)} %get-tuple-element.41), channel_id=1, source_target_pairs={{1,2},{2,1},{5,6},{6,5},{9,10},{10,9},{13,14},{14,13},{17,18},{18,... | collective-permute-start | bytes 196616 | tf_op jit(solution)/shard_map/ppermute | solution.py:441
  24.1 1.4 %collective-permute-start.7 = (bf16[448,128]{1,0:T(8,128)(2,1)S(1)}, bf16[448,128]{1,0:T(8,128)(2,1)S(1)}, u32[]{:S(2)}, u32[]{:S(2)}) collective-permute-start(bf16[448,128]{1,0:T(8,128)(2,1)S(1)} %add_convert_fusion.4), channel_id=1, source_target_pairs={{0,4},{1,9},{2,6},{3,11},{4,0},{5,13},{6,2},{7,15},{8,12},{9,1},{1... | collective-permute-start | bytes 344072 | tf_op jit(solution)/shard_map/ppermute | solution.py:456
  25.5 1.9 %collective-permute-start.9 = (bf16[256,128]{1,0:T(8,128)(2,1)S(1)}, bf16[256,128]{1,0:T(8,128)(2,1)S(1)}, u32[]{:S(2)}, u32[]{:S(2)}) collective-permute-start(bf16[256,128]{1,0:T(8,128)(2,1)S(1)} %get-tuple-element.45), channel_id=1, source_target_pairs={{4,8},{8,4},{12,16},{16,12},{20,24},{24,20},{5,9},{9,5},{13,17},{1... | collective-permute-start | bytes 196616 | tf_op jit(solution)/shard_map/ppermute | solution.py:441
  27.4 0.1 collective-permute-start.8
  27.5 2.5 %shard_map.122.moved_ref = bf16[2048,512]{1,0:T(8,128)(2,1)S(1)} custom-call(s32[8,6]{1,0:T(8,128)S(1)} %copy-done.1, bf16[512,512]{1,0:T(8,128)(2,1)S(1)} %get-tuple-element.42.hg_ref), custom_call_target="tpu_custom_call" | custom-call | flops 2500000000 | bytes 7500000 | tf_op jit(solution)/shard_map/pallas_call | solution.py:499
  30.1 1.4 %collective-permute-done.9.got_xb = bf16[256,128]{1,0:T(8,128)(2,1)S(1)} collective-permute-done((bf16[256,128]{1,0:T(8,128)(2,1)S(1)}, bf16[256,128]{1,0:T(8,128)(2,1)S(1)}, u32[]{:S(2)}, u32[]{:S(2)}) %collective-permute-start.9) | collective-permute-done | bytes 65568 | tf_op jit(solution)/shard_map/ppermute | solution.py:441
  31.5 0.1 collective-permute-start.10
  31.6 6.0 %collective-permute-start.11 = (bf16[768,128]{1,0:T(8,128)(2,1)S(1)}, bf16[768,128]{1,0:T(8,128)(2,1)S(1)}, u32[]{:S(2)}, u32[]{:S(2)}) collective-permute-start(bf16[768,128]{1,0:T(8,128)(2,1)S(1)} %slice.23), channel_id=1, source_target_pairs={{0,1},{1,0},{2,3},{3,2},{4,5},{5,4},{6,7},{7,6},{8,9},{9,8},{10,11... | collective-permute-start | bytes 589832 | tf_op jit(solution)/shard_map/ppermute | solution.py:433
  37.6 1.1 %shard_map.123.near_ref = f32[512,512]{1,0:T(8,128)S(1)} custom-call(bf16[512,512]{1,0:T(8,128)(2,1)S(1)} %get-tuple-element.42.hg_ref, bf16[2048,512]{1,0:T(8,128)(2,1)S(1)} %shard_map.122.moved_ref, bf16[64,448]{1,0:T(8,128)(2,1)S(1)} %copy-done), custom_call_target="tpu_custom_call" | custom-call | flops 1000000000 | bytes 3000000 | tf_op jit(solution)/shard_map/pallas_call | solution.py:499
  38.8 0.2 collective-permute-start.13
  39.0 1.8 %shard_map.124 = bf16[512,512]{1,0:T(8,128)(2,1)} custom-call(s32[1]{0:T(128)S(6)} %copy.13.counts, f32[512,512]{1,0:T(8,128)S(1)} %shard_map.123.near_ref, bf16[256,128]{1,0:T(8,128)(2,1)S(1)} %collective-permute-done.8.got_xa, bf16[256,128]{1,0:T(8,128)(2,1)S(1)} %collective-permute-done.9.got_xb, bf16[768,128]{1,0:T(8,128)(2,1)S(1)} %collective-permute-done.11.got_ya, ...), custom_call_target="tpu_custom_call" | custom-call | flops 1800000000 | bytes 5400000 | tf_op jit(solution)/shard_map/pallas_call | solution.py:499
  40.8 1.6 %collective-permute-done.13 = bf16[448,128]{1,0:T(8,128)(2,1)S(1)} collective-permute-done((bf16[448,128]{1,0:T(8,128)(2,1)S(1)}, bf16[448,128]{1,0:T(8,128)(2,1)S(1)}, u32[]{:S(2)}, u32[]{:S(2)}) %collective-permute-start.13) | collective-permute-done | bytes 114720 | tf_op jit(solution)/shard_map/ppermute | solution.py:456
  42.5 0.1 collective-permute-start.15
  42.6 2.4 %collective-permute-done.12.got_x = bf16[512,128]{1,0:T(8,128)(2,1)S(1)} collective-permute-done((bf16[512,128]{1,0:T(8,128)(2,1)S(1)}, bf16[512,128]{1,0:T(8,128)(2,1)S(1)}, u32[]{:S(2)}, u32[]{:S(2)}) %collective-permute-start.12) | collective-permute-done | bytes 131104 | tf_op jit(solution)/shard_map/ppermute | solution.py:433
  44.9 4.3 %collective-permute-start.14 = (bf16[512,128]{1,0:T(8,128)(2,1)S(1)}, bf16[512,128]{1,0:T(8,128)(2,1)S(1)}, u32[]{:S(2)}, u32[]{:S(2)}) collective-permute-start(bf16[512,128]{1,0:T(8,128)(2,1)S(1)} %collective-permute-done.12.got_x), channel_id=1, source_target_pairs={{0,1},{1,0},{2,3},{3,2},{4,5},{5,4},{6,7},{7,6},{8,9},{9,8},{10,11... | collective-permute-start | bytes 393224 | tf_op jit(solution)/shard_map/ppermute | solution.py:433
  49.2 0.3 collective-permute-done.15
  49.5 0.7 %collective-permute-done.14.got_xy = bf16[512,128]{1,0:T(8,128)(2,1)S(1)} collective-permute-done((bf16[512,128]{1,0:T(8,128)(2,1)S(1)}, bf16[512,128]{1,0:T(8,128)(2,1)S(1)}, u32[]{:S(2)}, u32[]{:S(2)}) %collective-permute-start.14) | collective-permute-done | bytes 131104 | tf_op jit(solution)/shard_map/ppermute | solution.py:433
  50.2 3.8 %collective-permute-start.16 = (bf16[448,128]{1,0:T(8,128)(2,1)S(1)}, bf16[448,128]{1,0:T(8,128)(2,1)S(1)}, u32[]{:S(2)}, u32[]{:S(2)}) collective-permute-start(bf16[448,128]{1,0:T(8,128)(2,1)S(1)} %add_convert_fusion), channel_id=1, source_target_pairs={{0,1},{1,0},{2,3},{3,2},{4,5},{5,4},{6,7},{7,6},{8,9},{9,8},{10,11... | collective-permute-start | bytes 344072 | tf_op jit(solution)/shard_map/ppermute | solution.py:433
  54.1 1.2 %shard_map.125 = bf16[512,128]{1,0:T(8,128)(2,1)} custom-call(s32[1,8]{1,0:T(1,128)S(1)} %copy-done.2, bf16[1536,128]{1,0:T(8,128)(2,1)S(1)} %get-tuple-element.37.own, bf16[512,128]{1,0:T(8,128)(2,1)S(1)} %collective-permute-done.12.got_x, bf16[768,128]{1,0:T(8,128)(2,1)S(1)} %collective-permute-done.11.got_ya, ...), custom_call_target="tpu_custom_call" | custom-call | flops 1200000000 | bytes 3600000 | tf_op jit(solution)/shard_map/pallas_call | solution.py:499
  55.3 0.1 maximum_select_fusion.refs_0_
  55.4 1.0 %shard_map.126 = (f32[64,448]{1,0:T(8,128)}, f32[128,512]{1,0:T(8,128)}, f32[128,128]{1,0:T(8,128)}) custom-call(bf16[896,128]{1,0:T(8,128)(2,1)S(1)} %maximum_select_fusion.refs_0_), custom_call_target="tpu_custom_call" | custom-call | flops 1000000000 | bytes 3000000 | tf_op jit(solution)/shard_map/pallas_call | solution.py:499
  (26 shorter events, 0.3 us)
Async XLA Ops:
  2.9 12.8 %copy-start.1 = (s32[8,6]{1,0:T(8,128)S(1)}, s32[8,6]{1,0:T(8,128)}, u32[]{:S(2)}) copy-start(s32[8,6]{1,0:T(8,128)} %nb.3) | copy-start | bytes 580
  2.9 12.8 %copy-start.2 = (s32[1,8]{1,0:T(1,128)S(1)}, s32[1,8]{1,0:T(1,128)}, u32[]{:S(2)}) copy-start(s32[1,8]{1,0:T(1,128)} %cmap.3) | copy-start | bytes 100
  2.9 6.1 %collective-permute-start = (bf16[784,128]{1,0:T(8,128)(2,1)S(1)}, bf16[784,128]{1,0:T(8,128)(2,1)S(1)}, u32[]{:S(2)}, u32[]{:S(2)}) collective-permute-start(bf16[784,128]{1,0:T(8,128)(2,1)S(1)} %get-tuple-element.32), channel_id=1, source_target_pairs={{0,4},{4,0},{8,12},{12,8},{16,20},{20,16},{24,28},{28,24},{1,5},{5... | collective-permute-start | bytes 602120 | tf_op jit(solution)/shard_map/ppermute | solution.py:433
  3.2 7.5 %collective-permute-start.2 = (bf16[784,128]{1,0:T(8,128)(2,1)S(1)}, bf16[784,128]{1,0:T(8,128)(2,1)S(1)}, u32[]{:S(2)}, u32[]{:S(2)}) collective-permute-start(bf16[784,128]{1,0:T(8,128)(2,1)S(1)} %get-tuple-element.34), channel_id=1, source_target_pairs={{0,1},{1,0},{2,3},{3,2},{4,5},{5,4},{6,7},{7,6},{8,9},{9,8},{10,11... | collective-permute-start | bytes 602120 | tf_op jit(solution)/shard_map/ppermute | solution.py:433
  4.1 6.5 %collective-permute-start.1 = (bf16[256,128]{1,0:T(8,128)(2,1)S(1)}, bf16[256,128]{1,0:T(8,128)(2,1)S(1)}, u32[]{:S(2)}, u32[]{:S(2)}) collective-permute-start(bf16[256,128]{1,0:T(8,128)(2,1)S(1)} %get-tuple-element.33), channel_id=1, source_target_pairs={{4,8},{8,4},{12,16},{16,12},{20,24},{24,20},{5,9},{9,5},{13,17},{1... | collective-permute-start | bytes 196616 | tf_op jit(solution)/shard_map/ppermute | solution.py:441
  8.3 2.4 %collective-permute-start.3 = (bf16[256,128]{1,0:T(8,128)(2,1)S(1)}, bf16[256,128]{1,0:T(8,128)(2,1)S(1)}, u32[]{:S(2)}, u32[]{:S(2)}) collective-permute-start(bf16[256,128]{1,0:T(8,128)(2,1)S(1)} %get-tuple-element.35), channel_id=1, source_target_pairs={{1,2},{2,1},{5,6},{6,5},{9,10},{10,9},{13,14},{14,13},{17,18},{18,... | collective-permute-start | bytes 196616 | tf_op jit(solution)/shard_map/ppermute | solution.py:441
  10.7 5.0 %collective-permute-start.4 = (bf16[528,128]{1,0:T(8,128)(2,1)S(1)}, bf16[528,128]{1,0:T(8,128)(2,1)S(1)}, u32[]{:S(2)}, u32[]{:S(2)}) collective-permute-start(bf16[528,128]{1,0:T(8,128)(2,1)S(1)} %slice.24), channel_id=1, source_target_pairs={{0,1},{1,0},{2,3},{3,2},{4,5},{5,4},{6,7},{7,6},{8,9},{9,8},{10,11... | collective-permute-start | bytes 405512 | tf_op jit(solution)/shard_map/ppermute | solution.py:433
  22.0 1.4 %collective-permute-start.5 = (bf16[448,128]{1,0:T(8,128)(2,1)S(1)}, bf16[448,128]{1,0:T(8,128)(2,1)S(1)}, u32[]{:S(2)}, u32[]{:S(2)}) collective-permute-start(bf16[448,128]{1,0:T(8,128)(2,1)S(1)} %get-tuple-element.40), channel_id=1, source_target_pairs={{0,1},{1,0},{2,3},{3,2},{4,5},{5,4},{6,7},{7,6},{8,9},{9,8},{10,11... | collective-permute-start | bytes 344072 | tf_op jit(solution)/shard_map/ppermute | solution.py:433
  23.5 4.0 %collective-permute-start.6 = (bf16[256,128]{1,0:T(8,128)(2,1)S(1)}, bf16[256,128]{1,0:T(8,128)(2,1)S(1)}, u32[]{:S(2)}, u32[]{:S(2)}) collective-permute-start(bf16[256,128]{1,0:T(8,128)(2,1)S(1)} %get-tuple-element.41), channel_id=1, source_target_pairs={{1,2},{2,1},{5,6},{6,5},{9,10},{10,9},{13,14},{14,13},{17,18},{18,... | collective-permute-start | bytes 196616 | tf_op jit(solution)/shard_map/ppermute | solution.py:441
  24.1 5.9 %collective-permute-start.7 = (bf16[448,128]{1,0:T(8,128)(2,1)S(1)}, bf16[448,128]{1,0:T(8,128)(2,1)S(1)}, u32[]{:S(2)}, u32[]{:S(2)}) collective-permute-start(bf16[448,128]{1,0:T(8,128)(2,1)S(1)} %add_convert_fusion.4), channel_id=1, source_target_pairs={{0,4},{1,9},{2,6},{3,11},{4,0},{5,13},{6,2},{7,15},{8,12},{9,1},{1... | collective-permute-start | bytes 344072 | tf_op jit(solution)/shard_map/ppermute | solution.py:456
  25.5 6.0 %collective-permute-start.9 = (bf16[256,128]{1,0:T(8,128)(2,1)S(1)}, bf16[256,128]{1,0:T(8,128)(2,1)S(1)}, u32[]{:S(2)}, u32[]{:S(2)}) collective-permute-start(bf16[256,128]{1,0:T(8,128)(2,1)S(1)} %get-tuple-element.45), channel_id=1, source_target_pairs={{4,8},{8,4},{12,16},{16,12},{20,24},{24,20},{5,9},{9,5},{13,17},{1... | collective-permute-start | bytes 196616 | tf_op jit(solution)/shard_map/ppermute | solution.py:441
  27.4 4.1 %collective-permute-start.8 = (bf16[256,128]{1,0:T(8,128)(2,1)S(1)}, bf16[256,128]{1,0:T(8,128)(2,1)S(1)}, u32[]{:S(2)}, u32[]{:S(2)}) collective-permute-start(bf16[256,128]{1,0:T(8,128)(2,1)S(1)} %get-tuple-element.44), channel_id=1, source_target_pairs={{0,4},{4,0},{8,12},{12,8},{16,20},{20,16},{24,28},{28,24},{1,5},{5... | collective-permute-start | bytes 196616 | tf_op jit(solution)/shard_map/ppermute | solution.py:433
  27.5 10.1 %copy-start = (bf16[64,448]{1,0:T(8,128)(2,1)S(1)}, bf16[64,448]{1,0:T(8,128)(2,1)}, u32[]{:S(2)}) copy-start(bf16[64,448]{1,0:T(8,128)(2,1)} %conv_ref.3) | copy-start | bytes 172036
  31.5 7.2 %collective-permute-start.10 = (bf16[448,128]{1,0:T(8,128)(2,1)S(1)}, bf16[448,128]{1,0:T(8,128)(2,1)S(1)}, u32[]{:S(2)}, u32[]{:S(2)}) collective-permute-start(bf16[448,128]{1,0:T(8,128)(2,1)S(1)} %add_convert_fusion.3), channel_id=1, source_target_pairs={{0,8},{1,5},{2,10},{3,7},{4,12},{5,1},{6,14},{7,3},{8,0},{9,13},{1... | collective-permute-start | bytes 344072 | tf_op jit(solution)/shard_map/ppermute | solution.py:456
  31.6 7.1 %collective-permute-start.11 = (bf16[768,128]{1,0:T(8,128)(2,1)S(1)}, bf16[768,128]{1,0:T(8,128)(2,1)S(1)}, u32[]{:S(2)}, u32[]{:S(2)}) collective-permute-start(bf16[768,128]{1,0:T(8,128)(2,1)S(1)} %slice.23), channel_id=1, source_target_pairs={{0,1},{1,0},{2,3},{3,2},{4,5},{5,4},{6,7},{7,6},{8,9},{9,8},{10,11... | collective-permute-start | bytes 589832 | tf_op jit(solution)/shard_map/ppermute | solution.py:433
  38.8 3.7 %collective-permute-start.13 = (bf16[448,128]{1,0:T(8,128)(2,1)S(1)}, bf16[448,128]{1,0:T(8,128)(2,1)S(1)}, u32[]{:S(2)}, u32[]{:S(2)}) collective-permute-start(bf16[448,128]{1,0:T(8,128)(2,1)S(1)} %add_convert_fusion.2), channel_id=1, source_target_pairs={{0,16},{1,3},{2,18},{3,1},{4,20},{5,7},{6,22},{7,5},{8,24},{9,11},... | collective-permute-start | bytes 344072 | tf_op jit(solution)/shard_map/ppermute | solution.py:456
  40.8 4.1 %collective-permute-start.12 = (bf16[512,128]{1,0:T(8,128)(2,1)S(1)}, bf16[512,128]{1,0:T(8,128)(2,1)S(1)}, u32[]{:S(2)}, u32[]{:S(2)}) collective-permute-start(bf16[512,128]{1,0:T(8,128)(2,1)S(1)} %slice.19), channel_id=1, source_target_pairs={{0,4},{4,0},{8,12},{12,8},{16,20},{20,16},{24,28},{28,24},{1,5},{5... | collective-permute-start | bytes 393224 | tf_op jit(solution)/shard_map/ppermute | solution.py:433
  42.5 7.0 %collective-permute-start.15 = (bf16[448,128]{1,0:T(8,128)(2,1)S(1)}, bf16[448,128]{1,0:T(8,128)(2,1)S(1)}, u32[]{:S(2)}, u32[]{:S(2)}) collective-permute-start(bf16[448,128]{1,0:T(8,128)(2,1)S(1)} %add_convert_fusion.1), channel_id=1, source_target_pairs={{0,2},{1,17},{2,0},{3,19},{4,6},{5,21},{6,4},{7,23},{8,10},{9,25},... | collective-permute-start | bytes 344072 | tf_op jit(solution)/shard_map/ppermute | solution.py:456
  44.9 5.3 %collective-permute-start.14 = (bf16[512,128]{1,0:T(8,128)(2,1)S(1)}, bf16[512,128]{1,0:T(8,128)(2,1)S(1)}, u32[]{:S(2)}, u32[]{:S(2)}) collective-permute-start(bf16[512,128]{1,0:T(8,128)(2,1)S(1)} %collective-permute-done.12.got_x), channel_id=1, source_target_pairs={{0,1},{1,0},{2,3},{3,2},{4,5},{5,4},{6,7},{7,6},{8,9},{9,8},{10,11... | collective-permute-start | bytes 393224 | tf_op jit(solution)/shard_map/ppermute | solution.py:433
  50.2 5.1 %collective-permute-start.16 = (bf16[448,128]{1,0:T(8,128)(2,1)S(1)}, bf16[448,128]{1,0:T(8,128)(2,1)S(1)}, u32[]{:S(2)}, u32[]{:S(2)}) collective-permute-start(bf16[448,128]{1,0:T(8,128)(2,1)S(1)} %add_convert_fusion), channel_id=1, source_target_pairs={{0,1},{1,0},{2,3},{3,2},{4,5},{5,4},{6,7},{7,6},{8,9},{9,8},{10,11... | collective-permute-start | bytes 344072 | tf_op jit(solution)/shard_map/ppermute | solution.py:433

commit v3 on v2

--- a/solution.py
+++ b/solution.py
@@ -222,9 +222,8 @@
     sums_ref, lat_ref, lat_sem, reach, taps, slope, act2, routed, far, maps_v, maps_s, sem,
 ):
     px, py = parities()
-    for j, got in enumerate((got_xa, got_ya)):
+    for j, got in enumerate((got_xa, got_ya, got_xy)):
         maps_v[j] = got[768:784, :].astype(F32).astype(jnp.int32)
-    maps_v[2] = got_xy[512:528, :].astype(F32).astype(jnp.int32)
     copy = pltpu.make_async_copy(maps_v, maps_s, sem)
     copy.start()
     lat_copy = pltpu.make_async_copy(lat_hbm, lat_ref, lat_sem)
@@ -235,7 +234,10 @@
     for got, axis, direction in (
         (got_xa, 0, 1 - px), (got_xb, 0, px), (got_ya, 1, 3 - py), (got_yb, 1, 2 + py),
     ):
-        wide = dot(got[0:256, :], spreads[axis]).astype(BF).reshape(4, C, 512)
+        wide = dot(got[0:256, :], spreads[axis]).astype(BF)
+        if got is got_xb or got is got_yb:
+            wide = jnp.where(inner(("gx", "gy")[axis]), wide, jnp.zeros_like(wide))
+        wide = wide.reshape(4, C, 512)
         reach[direction, 8:12] = wide[:, :, 0:256]
         reach[direction, 12:16] = wide[:, :, 256:512]
     for d in range(4):
@@ -283,7 +285,7 @@
     lat_copy.wait()
     for s in range(SLOTS):
         routed[s] = jnp.zeros((C, 128), BF)
-    for j, (got, start) in enumerate(((lat_ref, 0), (got_xa, 256), (got_ya, 256), (got_xy, 0))):
+    for j, (got, start) in enumerate(((lat_ref, 0), (got_xa, 256), (got_ya, 256), (got_xy, 256))):
         for k in range(8):
             name = cmap[0, k] if j == 0 else maps_s[j - 1, k, 0]
             name = name - j * SLOTS
@@ -317,8 +319,9 @@
     sums_ref[3 * C : 4 * C, C:128] = jnp.zeros((C, C), F32)
 
     first, second = sums_ref[0:448, :].astype(BF), sums_ref[448:896, :].astype(BF)
-    mine_ref[...] = jnp.where(py == 0, first, second)
-    other_ref[...] = jnp.where(py == 0, second, first)
+    even = parity() == 0
+    mine_ref[...] = jnp.where(even, first, second)
+    other_ref[...] = jnp.where(even, second, first)
 
     for d in range(4):
         for s in range(5):
@@ -389,7 +392,10 @@
 def far_kernel(counts, near_ref, got_xa, got_xb, got_ya, got_yb, conv_ref, out_ref, rows):
     px, py = parities()
     for got, direction in ((got_xa, px), (got_xb, 1 - px), (got_ya, 2 + py), (got_yb, 3 - py)):
-        rows[direction] = got[0:256, :]
+        value = got[0:256, :]
+        if got is got_xb or got is got_yb:
+            value = jnp.where(inner("gx" if got is got_xb else "gy"), value, jnp.zeros_like(value))
+        rows[direction] = value
     fields = []
     for d in range(4):
         conv = conv_ref[:, (d + 1) * C : (d + 2) * C]
@@ -419,7 +425,15 @@
         out_ref[k * C : (k + 1) * C, :] = rows[cmap[0, k]]
 
 
-def scale_kernel(scale, conv_in, conv_out, down_out, head_out):
+def scale_kernel(scale, mine, theirs, conv_out, down_out, head_out):
+    even = parity() == 0
+    conv_in = jnp.concatenate(
+        [
+            jnp.where(even, mine[...], theirs[...]),
+            jnp.where(even, theirs[...], mine[...]),
+        ],
+        0,
+    )
     for k in range(3):
         conv_out[:, k * 128 : (k + 1) * 128] = conv_in[k * C : (k + 1) * C, :].astype(F32) * scale
     conv_out[:, 384:448] = conv_in[3 * C : 4 * C, 0:C].astype(F32) * scale
@@ -428,64 +442,92 @@
     head_out[...] = conv_in[768:896, :].astype(F32) * scale
 
 
-def swap(value, axis, bit):
-    count = lax.axis_size(axis)
-    return lax.ppermute(value, axis, [(i, i ^ bit) for i in range(count)])
-
-
-def swap_odd(value, axis):
-    count = lax.axis_size(axis)
-    route = []
-    for low in range(1, count - 1, 2):
-        route += [(low, low + 1), (low + 1, low)]
-    return lax.ppermute(value, axis, route)
+def route(there):
+    nx, ny = lax.axis_size("gx"), lax.axis_size("gy")
+    pairs = []
+    for i in range(nx):
+        for j in range(ny):
+            x, y = there(i, j)
+            pairs.append((i * ny + j, x * ny + y))
+    return pairs
+
+
+def send_to(value, there):
+    return lax.ppermute(value, ("gx", "gy"), route(there))
+
+
+def beside_x(value):
+    return send_to(value, lambda i, j: (i ^ 1, j))
+
+
+def beside_core(value):
+    return send_to(value, lambda i, j: (i, j ^ 1))
+
+
+def beside_both(value):
+    return send_to(value, lambda i, j: (i ^ 1, j ^ 1))
+
+
+def odd_partner(i, count):
+    return min(max(i + 2 * (i % 2) - 1, -1), count)
+
+
+def odd_x(value):
+    nx = lax.axis_size("gx")
+    return send_to(value, lambda i, j: (odd_partner(i, nx), j) if 0 < i < nx - 1 else (i, j ^ 1))
+
+
+def odd_y(value):
+    ny = lax.axis_size("gy")
+    return send_to(value, lambda i, j: (i, odd_partner(j, ny) if 0 < j < ny - 1 else ny - 1 - j))
+
+
+def inner(axis):
+    at = lax.axis_index(axis)
+    return (at > 0) & (at < lax.axis_size(axis) - 1)
+
+
+def parity():
+    bits = lax.axis_index("gx") * lax.axis_size("gy") + lax.axis_index("gy")
+    count = 0
+    for k in range((lax.axis_size("gx") * lax.axis_size("gy") - 1).bit_length()):
+        count = count + lax.rem(lax.div(bits, 1 << k), 2)
+    return lax.rem(count, 2)
 
 
 def tie(value, *others):
     return lax.optimization_barrier((value, *others))[0]
 
 
-def core_swap(value, first, second):
-    nx, ny = lax.axis_size("gx"), lax.axis_size("gy")
-    route = []
-    for i in range(nx):
-        for j in range(ny):
-            axis, bit = (first, second)[j % 2]
-            there = (i ^ bit, j) if axis == "gx" else (i, j ^ bit)
-            route.append((i * ny + j, there[0] * ny + there[1]))
-    return lax.ppermute(value, ("gx", "gy"), route)
-
-
 def weight_sums(mine, other):
-    bit = lax.rem(lax.axis_index("gy"), 2)
-    steps = []
+    bits = []
     for axis, first in (("gy", 2), ("gx", 1)):
-        step = first
-        while step < lax.axis_size(axis):
-            steps.append((axis, step))
-            step *= 2
-    steps.append(steps.pop(0))
+        bit = first
+        while bit < lax.axis_size(axis):
+            bits.append((axis, bit))
+            bit *= 2
     turned = []
-    for at in range(0, len(steps) - 1, 2):
-        turned += [steps[at + 1], steps[at]]
-    turned += steps[len(turned) :]
+    for at in range(0, len(bits) - 1, 2):
+        turned += [bits[at + 1], bits[at]]
+    turned += bits[len(turned) :]
     state = {"sum": mine}
+
+    def there(at, i, j):
+        axis, bit = (bits, turned)[(i.bit_count() + j.bit_count()) % 2][at]
+        return (i ^ bit, j ^ 1) if axis == "gx" else (i, j ^ bit ^ 1)
 
     def step(at, waits):
         sent = tie(state["sum"], *waits) if waits else state["sum"]
-        if at > len(steps):
-            theirs = swap(sent, "gy", 1)
-            return jnp.where(
-                bit == 0, jnp.concatenate([sent, theirs]), jnp.concatenate([theirs, sent])
-            )
+        if at > len(bits):
+            return sent, beside_core(sent)
         if at == 0:
-            there = swap(other, "gy", 1)
+            got = beside_core(other)
         else:
-            there = core_swap(sent, steps[at - 1], turned[at - 1])
-        state["sum"] = (sent.astype(F32) + there.astype(F32)).astype(BF)
+            got = send_to(sent, lambda i, j: there(at - 1, i, j))
+        state["sum"] = (sent.astype(F32) + got.astype(F32)).astype(BF)
         return state["sum"]
 
-    return step, len(steps) + 1
+    return step, len(bits) + 1
 
 
 def call(kernel, outs, ins, spaces="", scratch=(), last=0, us=1.0):
@@ -528,10 +570,10 @@
         [pltpu.SMEM((1, 8), jnp.int32), pltpu.SemaphoreType.DMA((4,))],
         us=1.5,
     )
-    got_xa = swap(send_xa, "gx", 1)
-    got_xb = swap_odd(send_xb, "gx")
-    got_ya = swap(send_ya, "gy", 1)
-    got_yb = swap_odd(send_yb, "gy")
+    got_xy = beside_both(send_xa)
+    got_xb = odd_x(send_xb)
+    got_ya = beside_core(send_ya)
+    got_yb = odd_y(send_yb)
     (store,) = call(
         prep_kernel,
         [((STORE, 512), BF)],
@@ -540,7 +582,7 @@
         [pltpu.VMEM((C, 448), BF), pltpu.SemaphoreType.DMA((3,))],
         us=1.5,
     )
-    got_xy = swap(tie(got_xa[256:784], got_xb, got_yb, got_ya), "gy", 1)
+    got_xa = beside_core(tie(got_xy, got_xb, got_yb, got_ya))
     hg, mine, other, send = call(
         main_kernel,
         [((512, 512), BF), ((448, 128), BF), ((448, 128), BF), ((SEND, 128), BF)],
@@ -565,9 +607,9 @@
 
     sum_step, steps = weight_sums(mine, other)
     mine = sum_step(0, ())
-    got_xa = swap(tie(send[XA : XA + 256], mine), "gx", 1)
-    got_xb = swap_odd(tie(send[XB : XB + 256], mine), "gx")
-    got_yb = swap_odd(tie(send[YB : YB + 256], mine), "gy")
+    got_xa = beside_x(tie(send[XA : XA + 256], mine))
+    got_xb = odd_x(tie(send[XB : XB + 256], mine))
+    got_yb = odd_y(tie(send[YB : YB + 256], mine))
     (moved,) = call(
         roll_kernel,
         [((2048, 512), BF)],
@@ -582,7 +624,7 @@
         us=2.5,
     )
     mine = sum_step(1, ())
-    got_ya = swap(tie(send[YA : OCT + 512], mine), "gy", 1)
+    got_ya = beside_core(tie(send[YA : OCT + 512], mine))
     (near,) = call(
         near_kernel,
         [((512, 512), F32)],
@@ -601,9 +643,9 @@
         1,
         us=1.8,
     )
-    got_x = swap(tie(send[OCT : OCT + 512], grad), "gx", 1)
+    got_xy = beside_both(tie(send[OCT : OCT + 512], grad))
     mine = sum_step(3, (near, got_ya))
-    got_xy = swap(tie(got_x, mine), "gy", 1)
+    got_x = beside_core(tie(got_xy, mine))
     (latent,) = call(
         latent_kernel,
         [((512, 128), BF)],
@@ -616,12 +658,12 @@
     mine = sum_step(4, (grad,))
     for at in range(5, steps):
         mine = sum_step(at, ())
-    summed = sum_step(steps, (got_xy,))
+    mine, theirs = sum_step(steps, (got_x,))
     scale = float(SLOTS * lax.axis_size("gx") * lax.axis_size("gy")) ** (-0.5)
     conv_grad, down_grad, head_grad = call(
         lambda *refs: scale_kernel(scale, *refs),
         [((C, 448), F32), ((128, 512), F32), ((128, 128), F32)],
-        (summed,),
+        (mine, theirs),
         last=3,
     )
     return (

time: 56.6 us -> 49.1 us (0.87)
  the two profiles are of different devices: /device:TPU:7 before, /device:TPU:0 now
where the time goes in v3:
time: 49.1 us; the launch traced here: 49 us
  starting transfers between devices  20.7 us (42%)
  Pallas kernels  17 us (35%)
  waiting for transfers between devices  9.57 us (19%)
  between operations  1.45 us (3%)
    ppermute x17, starting transfers between devices, send_to(): return lax.ppermute(value, ('gx', 'gy'), route(there))  20.7 us
    pallas_call x8, Pallas kernels, call(): pl.pallas_call(kernel, out_shape=[pltpu.VMEM(shape, kind) if at < keep el...  17 us
    ppermute x17, waiting for transfers between devices, send_to(): return lax.ppermute(value, ('gx', 'gy'), route(there))  9.57 us
  transfers between devices with their start and end apart: 17, of which 7 were waited for; matrix products, arithmetic and copies ran while one was open for 0% of the time, Pallas kernels for 17%

profile of v3, /device:TPU:0, one launch (start us, length us, event | category | flops | bytes accessed | tf_op | source)
XLA Modules:
  0.0 49.0 jit_solution(89099624681826666)
XLA Ops:
  1.3 1.5 %shard_map.119 = (bf16[512,512]{1,0:T(8,128)(2,1)S(1)}, bf16[784,128]{1,0:T(8,128)(2,1)S(1)}, bf16[256,128]{1,0:T(8,128)(2,1)S(1)}, bf16[784,128]{1,0:T(8,128)(2,1)S(1)}, bf16[256,128]{1,0:T(8,128)(2,1)S(1)}) custom-call(s32[1]{0:T(128)S(6)} %copy.13.counts, s32[1,8]{1,0:T(1,128)} %cmap.3, bf16[512,512]{1,0:T(8,128)(2,1)} %bitcast.4, bf16[512,128]{1,0:T(8,128)(2,1)} %bitcast.5), custom_call_target="tpu_custom_call" | custom-call | flops 1500000000 | bytes 4500000 | tf_op jit(solution)/shard_map/pallas_call | solution.py:541
  2.8 0.0 copy-start.1
  2.9 2.5 %collective-permute-start = (bf16[784,128]{1,0:T(8,128)(2,1)S(1)}, bf16[784,128]{1,0:T(8,128)(2,1)S(1)}, u32[]{:S(2)}, u32[]{:S(2)}) collective-permute-start(bf16[784,128]{1,0:T(8,128)(2,1)S(1)} %get-tuple-element.32), channel_id=1, source_target_pairs={{0,5},{1,4},{2,7},{3,6},{4,1},{5,0},{6,3},{7,2},{8,13},{9,12},{10,... | collective-permute-start | bytes 602120 | tf_op jit(solution)/shard_map/ppermute | solution.py:456
  5.4 0.7 %collective-permute-start.3 = (bf16[784,128]{1,0:T(8,128)(2,1)S(1)}, bf16[784,128]{1,0:T(8,128)(2,1)S(1)}, u32[]{:S(2)}, u32[]{:S(2)}) collective-permute-start(bf16[784,128]{1,0:T(8,128)(2,1)S(1)} %get-tuple-element.35), channel_id=1, source_target_pairs={{0,1},{1,0},{2,3},{3,2},{4,5},{5,4},{6,7},{7,6},{8,9},{9,8},{10,11... | collective-permute-start | bytes 602120 | tf_op jit(solution)/shard_map/ppermute | solution.py:456
  6.0 1.6 %collective-permute-start.2 = (bf16[256,128]{1,0:T(8,128)(2,1)S(1)}, bf16[256,128]{1,0:T(8,128)(2,1)S(1)}, u32[]{:S(2)}, u32[]{:S(2)}) collective-permute-start(bf16[256,128]{1,0:T(8,128)(2,1)S(1)} %get-tuple-element.34), channel_id=1, source_target_pairs={{0,3},{1,2},{2,1},{3,0},{4,7},{5,6},{6,5},{7,4},{8,11},{9,10},{10,... | collective-permute-start | bytes 196616 | tf_op jit(solution)/shard_map/ppermute | solution.py:456
  7.6 2.2 %collective-permute-done.2.got_yb = bf16[256,128]{1,0:T(8,128)(2,1)S(1)} collective-permute-done((bf16[256,128]{1,0:T(8,128)(2,1)S(1)}, bf16[256,128]{1,0:T(8,128)(2,1)S(1)}, u32[]{:S(2)}, u32[]{:S(2)}) %collective-permute-start.2) | collective-permute-done | bytes 65568 | tf_op jit(solution)/shard_map/ppermute | solution.py:456
  9.8 2.4 %collective-permute-done.got_xy = bf16[784,128]{1,0:T(8,128)(2,1)S(1)} collective-permute-done((bf16[784,128]{1,0:T(8,128)(2,1)S(1)}, bf16[784,128]{1,0:T(8,128)(2,1)S(1)}, u32[]{:S(2)}, u32[]{:S(2)}) %collective-permute-start) | collective-permute-done | bytes 200736 | tf_op jit(solution)/shard_map/ppermute | solution.py:456
  12.1 0.1 collective-permute-start.4
  12.2 1.5 %shard_map.120.store = bf16[2880,512]{1,0:T(8,128)(2,1)S(1)} custom-call(bf16[512,512]{1,0:T(8,128)(2,1)S(1)} %get-tuple-element.31.xm, bf16[64,448]{1,0:T(8,128)(2,1)} %conv_ref.3, bf16[128,512]{1,0:T(8,128)(2,1)} %down_hbm.1, bf16[128,128]{1,0:T(8,128)(2,1)} %head_hbm.1), custom_call_target="tpu_custom_call" | custom-call | flops 1500000000 | bytes 4500000 | tf_op jit(solution)/shard_map/pallas_call | solution.py:541
  13.8 6.3 %shard_map.121 = (bf16[512,512]{1,0:T(8,128)(2,1)S(1)}, bf16[448,128]{1,0:T(8,128)(2,1)S(1)}, bf16[448,128]{1,0:T(8,128)(2,1)S(1)}, bf16[1536,128]{1,0:T(8,128)(2,1)S(1)}) custom-call(s32[8,6]{1,0:T(8,128)S(1)} %copy-done.1, s32[1,8]{1,0:T(1,128)S(1)} %copy-done.2, bf16[512,128]{1,0:T(8,128)(2,1)} %bitcast.6, bf16[512,512]{1,0:T(8,128)(2,1)S(1)} %get-tuple-element.31.xm, ...), custom_call_target="tpu_custom_call" | custom-call | flops 6000000000 | bytes 18000000 | tf_op jit(solution)/shard_map/pallas_call | solution.py:541
  20.1 0.5 %collective-permute-start.5 = (bf16[448,128]{1,0:T(8,128)(2,1)S(1)}, bf16[448,128]{1,0:T(8,128)(2,1)S(1)}, u32[]{:S(2)}, u32[]{:S(2)}) collective-permute-start(bf16[448,128]{1,0:T(8,128)(2,1)S(1)} %get-tuple-element.40), channel_id=1, source_target_pairs={{0,1},{1,0},{2,3},{3,2},{4,5},{5,4},{6,7},{7,6},{8,9},{9,8},{10,11... | collective-permute-start | bytes 344072 | tf_op jit(solution)/shard_map/ppermute | solution.py:456
  20.6 0.9 %collective-permute-done.5 = bf16[448,128]{1,0:T(8,128)(2,1)S(1)} collective-permute-done((bf16[448,128]{1,0:T(8,128)(2,1)S(1)}, bf16[448,128]{1,0:T(8,128)(2,1)S(1)}, u32[]{:S(2)}, u32[]{:S(2)}) %collective-permute-start.5) | collective-permute-done | bytes 114720 | tf_op jit(solution)/shard_map/ppermute | solution.py:456
  21.6 1.5 %collective-permute-start.6 = (bf16[256,128]{1,0:T(8,128)(2,1)S(1)}, bf16[256,128]{1,0:T(8,128)(2,1)S(1)}, u32[]{:S(2)}, u32[]{:S(2)}) collective-permute-start(bf16[256,128]{1,0:T(8,128)(2,1)S(1)} %get-tuple-element.41), channel_id=1, source_target_pairs={{0,3},{1,2},{2,1},{3,0},{4,7},{5,6},{6,5},{7,4},{8,11},{9,10},{10,... | collective-permute-start | bytes 196616 | tf_op jit(solution)/shard_map/ppermute | solution.py:456
  23.1 0.3 collective-permute-start.7
  23.4 2.2 %collective-permute-start.8 = (bf16[256,128]{1,0:T(8,128)(2,1)S(1)}, bf16[256,128]{1,0:T(8,128)(2,1)S(1)}, u32[]{:S(2)}, u32[]{:S(2)}) collective-permute-start(bf16[256,128]{1,0:T(8,128)(2,1)S(1)} %get-tuple-element.44), channel_id=1, source_target_pairs={{0,4},{1,5},{2,6},{3,7},{4,0},{5,1},{6,2},{7,3},{8,12},{9,13},{10,... | collective-permute-start | bytes 196616 | tf_op jit(solution)/shard_map/ppermute | solution.py:456
  25.6 0.4 collective-permute-start.9
  26.0 2.5 %shard_map.122.moved_ref = bf16[2048,512]{1,0:T(8,128)(2,1)S(1)} custom-call(s32[8,6]{1,0:T(8,128)S(1)} %copy-done.1, bf16[512,512]{1,0:T(8,128)(2,1)S(1)} %get-tuple-element.42.hg_ref), custom_call_target="tpu_custom_call" | custom-call | flops 2500000000 | bytes 7500000 | tf_op jit(solution)/shard_map/pallas_call | solution.py:541
  28.5 1.2 %collective-permute-done.8.got_xa = bf16[256,128]{1,0:T(8,128)(2,1)S(1)} collective-permute-done((bf16[256,128]{1,0:T(8,128)(2,1)S(1)}, bf16[256,128]{1,0:T(8,128)(2,1)S(1)}, u32[]{:S(2)}, u32[]{:S(2)}) %collective-permute-start.8) | collective-permute-done | bytes 65568 | tf_op jit(solution)/shard_map/ppermute | solution.py:456
  29.7 2.3 %collective-permute-start.10 = (bf16[448,128]{1,0:T(8,128)(2,1)S(1)}, bf16[448,128]{1,0:T(8,128)(2,1)S(1)}, u32[]{:S(2)}, u32[]{:S(2)}) collective-permute-start(bf16[448,128]{1,0:T(8,128)(2,1)S(1)} %add_convert_fusion.3), channel_id=1, source_target_pairs={{0,5},{1,2},{2,1},{3,6},{4,7},{5,0},{6,3},{7,4},{8,11},{9,12},{10,... | collective-permute-start | bytes 344072 | tf_op jit(solution)/shard_map/ppermute | solution.py:456
  32.1 0.1 collective-permute-start.11
  32.1 1.1 %shard_map.123.near_ref = f32[512,512]{1,0:T(8,128)S(1)} custom-call(bf16[512,512]{1,0:T(8,128)(2,1)S(1)} %get-tuple-element.42.hg_ref, bf16[2048,512]{1,0:T(8,128)(2,1)S(1)} %shard_map.122.moved_ref, bf16[64,448]{1,0:T(8,128)(2,1)S(1)} %copy-done), custom_call_target="tpu_custom_call" | custom-call | flops 1000000000 | bytes 3000000 | tf_op jit(solution)/shard_map/pallas_call | solution.py:541
  33.2 1.3 %collective-permute-done.10 = bf16[448,128]{1,0:T(8,128)(2,1)S(1)} collective-permute-done((bf16[448,128]{1,0:T(8,128)(2,1)S(1)}, bf16[448,128]{1,0:T(8,128)(2,1)S(1)}, u32[]{:S(2)}, u32[]{:S(2)}) %collective-permute-start.10) | collective-permute-done | bytes 114720 | tf_op jit(solution)/shard_map/ppermute | solution.py:456
  34.5 2.1 %collective-permute-start.13 = (bf16[448,128]{1,0:T(8,128)(2,1)S(1)}, bf16[448,128]{1,0:T(8,128)(2,1)S(1)}, u32[]{:S(2)}, u32[]{:S(2)}) collective-permute-start(bf16[448,128]{1,0:T(8,128)(2,1)S(1)} %add_convert_fusion.2), channel_id=1, source_target_pairs={{0,9},{1,16},{2,19},{3,10},{4,21},{5,12},{6,15},{7,22},{8,25},{9,0... | collective-permute-start | bytes 344072 | tf_op jit(solution)/shard_map/ppermute | solution.py:456
  36.6 1.9 %shard_map.124 = bf16[512,512]{1,0:T(8,128)(2,1)} custom-call(s32[1]{0:T(128)S(6)} %copy.13.counts, f32[512,512]{1,0:T(8,128)S(1)} %shard_map.123.near_ref, bf16[256,128]{1,0:T(8,128)(2,1)S(1)} %collective-permute-done.8.got_xa, bf16[256,128]{1,0:T(8,128)(2,1)S(1)} %collective-permute-done.9.got_xb, bf16[768,128]{1,0:T(8,128)(2,1)S(1)} %collective-permute-done.11.got_ya, ...), custom_call_target="tpu_custom_call" | custom-call | flops 1800000000 | bytes 5400000 | tf_op jit(solution)/shard_map/pallas_call | solution.py:541
  38.5 1.7 %collective-permute-start.12 = (bf16[512,128]{1,0:T(8,128)(2,1)S(1)}, bf16[512,128]{1,0:T(8,128)(2,1)S(1)}, u32[]{:S(2)}, u32[]{:S(2)}) collective-permute-start(bf16[512,128]{1,0:T(8,128)(2,1)S(1)} %slice.15), channel_id=1, source_target_pairs={{0,5},{1,4},{2,7},{3,6},{4,1},{5,0},{6,3},{7,2},{8,13},{9,12},{10,... | collective-permute-start | bytes 393224 | tf_op jit(solution)/shard_map/ppermute | solution.py:456
  40.2 2.8 %collective-permute-start.15 = (bf16[448,128]{1,0:T(8,128)(2,1)S(1)}, bf16[448,128]{1,0:T(8,128)(2,1)S(1)}, u32[]{:S(2)}, u32[]{:S(2)}) collective-permute-start(bf16[448,128]{1,0:T(8,128)(2,1)S(1)} %add_convert_fusion.1), channel_id=1, source_target_pairs={{0,17},{1,8},{2,11},{3,18},{4,13},{5,20},{6,23},{7,14},{8,1},{9,24... | collective-permute-start | bytes 344072 | tf_op jit(solution)/shard_map/ppermute | solution.py:456
  43.1 0.3 collective-permute-done.12.got_xy
  43.4 1.3 %collective-permute-start.14 = (bf16[512,128]{1,0:T(8,128)(2,1)S(1)}, bf16[512,128]{1,0:T(8,128)(2,1)S(1)}, u32[]{:S(2)}, u32[]{:S(2)}) collective-permute-start(bf16[512,128]{1,0:T(8,128)(2,1)S(1)} %collective-permute-done.12.got_xy), channel_id=1, source_target_pairs={{0,1},{1,0},{2,3},{3,2},{4,5},{5,4},{6,7},{7,6},{8,9},{9,8},{10,11... | collective-permute-start | bytes 393224 | tf_op jit(solution)/shard_map/ppermute | solution.py:456
  44.6 1.3 %collective-permute-done.15 = bf16[448,128]{1,0:T(8,128)(2,1)S(1)} collective-permute-done((bf16[448,128]{1,0:T(8,128)(2,1)S(1)}, bf16[448,128]{1,0:T(8,128)(2,1)S(1)}, u32[]{:S(2)}, u32[]{:S(2)}) %collective-permute-start.15) | collective-permute-done | bytes 114720 | tf_op jit(solution)/shard_map/ppermute | solution.py:456
  46.0 0.7 %collective-permute-start.16 = (bf16[448,128]{1,0:T(8,128)(2,1)S(1)}, bf16[448,128]{1,0:T(8,128)(2,1)S(1)}, u32[]{:S(2)}, u32[]{:S(2)}) collective-permute-start(bf16[448,128]{1,0:T(8,128)(2,1)S(1)} %add_convert_fusion.refs_0_), channel_id=1, source_target_pairs={{0,1},{1,0},{2,3},{3,2},{4,5},{5,4},{6,7},{7,6},{8,9},{9,8},{10,11... | collective-permute-start | bytes 344072 | tf_op jit(solution)/shard_map/ppermute | solution.py:456
  46.7 1.2 %shard_map.125 = bf16[512,128]{1,0:T(8,128)(2,1)} custom-call(s32[1,8]{1,0:T(1,128)S(1)} %copy-done.2, bf16[1536,128]{1,0:T(8,128)(2,1)S(1)} %get-tuple-element.37.own, bf16[512,128]{1,0:T(8,128)(2,1)S(1)} %collective-permute-done.14.got_x, bf16[768,128]{1,0:T(8,128)(2,1)S(1)} %collective-permute-done.11.got_ya, ...), custom_call_target="tpu_custom_call" | custom-call | flops 1200000000 | bytes 3600000 | tf_op jit(solution)/shard_map/pallas_call | solution.py:541
  48.0 1.0 %shard_map.126 = (f32[64,448]{1,0:T(8,128)}, f32[128,512]{1,0:T(8,128)}, f32[128,128]{1,0:T(8,128)}) custom-call(bf16[448,128]{1,0:T(8,128)(2,1)S(1)} %add_convert_fusion.refs_0_, bf16[448,128]{1,0:T(8,128)(2,1)S(1)} %collective-permute-done.16.refs_1_), custom_call_target="tpu_custom_call" | custom-call | flops 1000000000 | bytes 3000000 | tf_op jit(solution)/shard_map/pallas_call | solution.py:541
  (24 shorter events, 0.2 us)
Async XLA Ops:
  2.8 10.9 %copy-start.1 = (s32[8,6]{1,0:T(8,128)S(1)}, s32[8,6]{1,0:T(8,128)}, u32[]{:S(2)}) copy-start(s32[8,6]{1,0:T(8,128)} %nb.3) | copy-start | bytes 580
  2.8 10.9 %copy-start.2 = (s32[1,8]{1,0:T(1,128)S(1)}, s32[1,8]{1,0:T(1,128)}, u32[]{:S(2)}) copy-start(s32[1,8]{1,0:T(1,128)} %cmap.3) | copy-start | bytes 100
  2.9 9.3 %collective-permute-start = (bf16[784,128]{1,0:T(8,128)(2,1)S(1)}, bf16[784,128]{1,0:T(8,128)(2,1)S(1)}, u32[]{:S(2)}, u32[]{:S(2)}) collective-permute-start(bf16[784,128]{1,0:T(8,128)(2,1)S(1)} %get-tuple-element.32), channel_id=1, source_target_pairs={{0,5},{1,4},{2,7},{3,6},{4,1},{5,0},{6,3},{7,2},{8,13},{9,12},{10,... | collective-permute-start | bytes 602120 | tf_op jit(solution)/shard_map/ppermute | solution.py:456
  5.4 6.8 %collective-permute-start.3 = (bf16[784,128]{1,0:T(8,128)(2,1)S(1)}, bf16[784,128]{1,0:T(8,128)(2,1)S(1)}, u32[]{:S(2)}, u32[]{:S(2)}) collective-permute-start(bf16[784,128]{1,0:T(8,128)(2,1)S(1)} %get-tuple-element.35), channel_id=1, source_target_pairs={{0,1},{1,0},{2,3},{3,2},{4,5},{5,4},{6,7},{7,6},{8,9},{9,8},{10,11... | collective-permute-start | bytes 602120 | tf_op jit(solution)/shard_map/ppermute | solution.py:456
  6.0 1.6 %collective-permute-start.1 = (bf16[256,128]{1,0:T(8,128)(2,1)S(1)}, bf16[256,128]{1,0:T(8,128)(2,1)S(1)}, u32[]{:S(2)}, u32[]{:S(2)}) collective-permute-start(bf16[256,128]{1,0:T(8,128)(2,1)S(1)} %get-tuple-element.33), channel_id=1, source_target_pairs={{0,1},{1,0},{2,3},{3,2},{4,8},{5,9},{6,10},{7,11},{8,4},{9,5},{10,... | collective-permute-start | bytes 196616 | tf_op jit(solution)/shard_map/ppermute | solution.py:456
  6.0 3.7 %collective-permute-start.2 = (bf16[256,128]{1,0:T(8,128)(2,1)S(1)}, bf16[256,128]{1,0:T(8,128)(2,1)S(1)}, u32[]{:S(2)}, u32[]{:S(2)}) collective-permute-start(bf16[256,128]{1,0:T(8,128)(2,1)S(1)} %get-tuple-element.34), channel_id=1, source_target_pairs={{0,3},{1,2},{2,1},{3,0},{4,7},{5,6},{6,5},{7,4},{8,11},{9,10},{10,... | collective-permute-start | bytes 196616 | tf_op jit(solution)/shard_map/ppermute | solution.py:456
  12.1 1.6 %collective-permute-start.4 = (bf16[784,128]{1,0:T(8,128)(2,1)S(1)}, bf16[784,128]{1,0:T(8,128)(2,1)S(1)}, u32[]{:S(2)}, u32[]{:S(2)}) collective-permute-start(bf16[784,128]{1,0:T(8,128)(2,1)S(1)} %collective-permute-done.got_xy), channel_id=1, source_target_pairs={{0,1},{1,0},{2,3},{3,2},{4,5},{5,4},{6,7},{7,6},{8,9},{9,8},{10,11... | collective-permute-start | bytes 602120 | tf_op jit(solution)/shard_map/ppermute | solution.py:456
  20.1 1.5 %collective-permute-start.5 = (bf16[448,128]{1,0:T(8,128)(2,1)S(1)}, bf16[448,128]{1,0:T(8,128)(2,1)S(1)}, u32[]{:S(2)}, u32[]{:S(2)}) collective-permute-start(bf16[448,128]{1,0:T(8,128)(2,1)S(1)} %get-tuple-element.40), channel_id=1, source_target_pairs={{0,1},{1,0},{2,3},{3,2},{4,5},{5,4},{6,7},{7,6},{8,9},{9,8},{10,11... | collective-permute-start | bytes 344072 | tf_op jit(solution)/shard_map/ppermute | solution.py:456
  21.6 4.4 %collective-permute-start.6 = (bf16[256,128]{1,0:T(8,128)(2,1)S(1)}, bf16[256,128]{1,0:T(8,128)(2,1)S(1)}, u32[]{:S(2)}, u32[]{:S(2)}) collective-permute-start(bf16[256,128]{1,0:T(8,128)(2,1)S(1)} %get-tuple-element.41), channel_id=1, source_target_pairs={{0,3},{1,2},{2,1},{3,0},{4,7},{5,6},{6,5},{7,4},{8,11},{9,10},{10,... | collective-permute-start | bytes 196616 | tf_op jit(solution)/shard_map/ppermute | solution.py:456
  23.1 5.4 %collective-permute-start.7 = (bf16[448,128]{1,0:T(8,128)(2,1)S(1)}, bf16[448,128]{1,0:T(8,128)(2,1)S(1)}, u32[]{:S(2)}, u32[]{:S(2)}) collective-permute-start(bf16[448,128]{1,0:T(8,128)(2,1)S(1)} %add_convert_fusion.4), channel_id=1, source_target_pairs={{0,3},{1,4},{2,7},{3,0},{4,1},{5,6},{6,5},{7,2},{8,13},{9,10},{10,... | collective-permute-start | bytes 344072 | tf_op jit(solution)/shard_map/ppermute | solution.py:456
  23.4 6.3 %collective-permute-start.8 = (bf16[256,128]{1,0:T(8,128)(2,1)S(1)}, bf16[256,128]{1,0:T(8,128)(2,1)S(1)}, u32[]{:S(2)}, u32[]{:S(2)}) collective-permute-start(bf16[256,128]{1,0:T(8,128)(2,1)S(1)} %get-tuple-element.44), channel_id=1, source_target_pairs={{0,4},{1,5},{2,6},{3,7},{4,0},{5,1},{6,2},{7,3},{8,12},{9,13},{10,... | collective-permute-start | bytes 196616 | tf_op jit(solution)/shard_map/ppermute | solution.py:456
  25.6 4.1 %collective-permute-start.9 = (bf16[256,128]{1,0:T(8,128)(2,1)S(1)}, bf16[256,128]{1,0:T(8,128)(2,1)S(1)}, u32[]{:S(2)}, u32[]{:S(2)}) collective-permute-start(bf16[256,128]{1,0:T(8,128)(2,1)S(1)} %get-tuple-element.45), channel_id=1, source_target_pairs={{0,1},{1,0},{2,3},{3,2},{4,8},{5,9},{6,10},{7,11},{8,4},{9,5},{10,... | collective-permute-start | bytes 196616 | tf_op jit(solution)/shard_map/ppermute | solution.py:456
  26.0 6.2 %copy-start = (bf16[64,448]{1,0:T(8,128)(2,1)S(1)}, bf16[64,448]{1,0:T(8,128)(2,1)}, u32[]{:S(2)}) copy-start(bf16[64,448]{1,0:T(8,128)(2,1)} %conv_ref.3) | copy-start | bytes 172036
  29.7 4.8 %collective-permute-start.10 = (bf16[448,128]{1,0:T(8,128)(2,1)S(1)}, bf16[448,128]{1,0:T(8,128)(2,1)S(1)}, u32[]{:S(2)}, u32[]{:S(2)}) collective-permute-start(bf16[448,128]{1,0:T(8,128)(2,1)S(1)} %add_convert_fusion.3), channel_id=1, source_target_pairs={{0,5},{1,2},{2,1},{3,6},{4,7},{5,0},{6,3},{7,4},{8,11},{9,12},{10,... | collective-permute-start | bytes 344072 | tf_op jit(solution)/shard_map/ppermute | solution.py:456
  32.1 2.5 %collective-permute-start.11 = (bf16[768,128]{1,0:T(8,128)(2,1)S(1)}, bf16[768,128]{1,0:T(8,128)(2,1)S(1)}, u32[]{:S(2)}, u32[]{:S(2)}) collective-permute-start(bf16[768,128]{1,0:T(8,128)(2,1)S(1)} %slice.19), channel_id=1, source_target_pairs={{0,1},{1,0},{2,3},{3,2},{4,5},{5,4},{6,7},{7,6},{8,9},{9,8},{10,11... | collective-permute-start | bytes 589832 | tf_op jit(solution)/shard_map/ppermute | solution.py:456
  34.5 5.7 %collective-permute-start.13 = (bf16[448,128]{1,0:T(8,128)(2,1)S(1)}, bf16[448,128]{1,0:T(8,128)(2,1)S(1)}, u32[]{:S(2)}, u32[]{:S(2)}) collective-permute-start(bf16[448,128]{1,0:T(8,128)(2,1)S(1)} %add_convert_fusion.2), channel_id=1, source_target_pairs={{0,9},{1,16},{2,19},{3,10},{4,21},{5,12},{6,15},{7,22},{8,25},{9,0... | collective-permute-start | bytes 344072 | tf_op jit(solution)/shard_map/ppermute | solution.py:456
  38.5 4.9 %collective-permute-start.12 = (bf16[512,128]{1,0:T(8,128)(2,1)S(1)}, bf16[512,128]{1,0:T(8,128)(2,1)S(1)}, u32[]{:S(2)}, u32[]{:S(2)}) collective-permute-start(bf16[512,128]{1,0:T(8,128)(2,1)S(1)} %slice.15), channel_id=1, source_target_pairs={{0,5},{1,4},{2,7},{3,6},{4,1},{5,0},{6,3},{7,2},{8,13},{9,12},{10,... | collective-permute-start | bytes 393224 | tf_op jit(solution)/shard_map/ppermute | solution.py:456
  40.2 5.7 %collective-permute-start.15 = (bf16[448,128]{1,0:T(8,128)(2,1)S(1)}, bf16[448,128]{1,0:T(8,128)(2,1)S(1)}, u32[]{:S(2)}, u32[]{:S(2)}) collective-permute-start(bf16[448,128]{1,0:T(8,128)(2,1)S(1)} %add_convert_fusion.1), channel_id=1, source_target_pairs={{0,17},{1,8},{2,11},{3,18},{4,13},{5,20},{6,23},{7,14},{8,1},{9,24... | collective-permute-start | bytes 344072 | tf_op jit(solution)/shard_map/ppermute | solution.py:456
  43.4 2.6 %collective-permute-start.14 = (bf16[512,128]{1,0:T(8,128)(2,1)S(1)}, bf16[512,128]{1,0:T(8,128)(2,1)S(1)}, u32[]{:S(2)}, u32[]{:S(2)}) collective-permute-start(bf16[512,128]{1,0:T(8,128)(2,1)S(1)} %collective-permute-done.12.got_xy), channel_id=1, source_target_pairs={{0,1},{1,0},{2,3},{3,2},{4,5},{5,4},{6,7},{7,6},{8,9},{9,8},{10,11... | collective-permute-start | bytes 393224 | tf_op jit(solution)/shard_map/ppermute | solution.py:456
  46.0 2.0 %collective-permute-start.16 = (bf16[448,128]{1,0:T(8,128)(2,1)S(1)}, bf16[448,128]{1,0:T(8,128)(2,1)S(1)}, u32[]{:S(2)}, u32[]{:S(2)}) collective-permute-start(bf16[448,128]{1,0:T(8,128)(2,1)S(1)} %add_convert_fusion.refs_0_), channel_id=1, source_target_pairs={{0,1},{1,0},{2,3},{3,2},{4,5},{5,4},{6,7},{7,6},{8,9},{9,8},{10,11... | collective-permute-start | bytes 344072 | tf_op jit(solution)/shard_map/ppermute | solution.py:456

commit v4 on v3

--- a/solution.py
+++ b/solution.py
@@ -216,18 +216,17 @@
 
 
 def main_kernel(
-    nb, cmap, lat_hbm,
+    nb_hbm, cmap_hbm, lat_hbm,
     xm, got_xa, got_xb, got_ya, got_yb, got_xy, store,
     hg_ref, mine_ref, other_ref, send,
-    sums_ref, lat_ref, lat_sem, reach, taps, slope, act2, routed, far, maps_v, maps_s, sem,
+    nb, cmap, sems, sums_ref, lat_ref, reach, taps, hg_row, slope, act2, routed, far, maps_v, maps_s, sem,
 ):
     px, py = parities()
     for j, got in enumerate((got_xa, got_ya, got_xy)):
         maps_v[j] = got[768:784, :].astype(F32).astype(jnp.int32)
     copy = pltpu.make_async_copy(maps_v, maps_s, sem)
     copy.start()
-    lat_copy = pltpu.make_async_copy(lat_hbm, lat_ref, lat_sem)
-    lat_copy.start()
+    copies = load([(nb_hbm, nb), (cmap_hbm, cmap), (lat_hbm, lat_ref)], sems)
     head = store[DOWN_BACK : DOWN_BACK + 128, 128:256]
 
     spreads = [spread(axis) for axis in range(2)]
@@ -247,22 +246,25 @@
 
     masks, masks_z = rim_masks()
     low = lane_of((C, 128)) < 64
+    copies[0].wait()
     conv = store[CONV : CONV + C, 0:448]
     for pair in range(SLOTS // 2):
         acts = []
         for b in (2 * pair, 2 * pair + 1):
             block = xm[b * C : (b + 1) * C, :]
-            taps[b, 0:C, :] = block
+            at = b * 512
+            taps[0:C, at : at + 512] = block
             for d in range(4):
                 moved = jnp.where(masks[d], reach[d, nb[b, d]], reach[d, b])
                 for k, piece in enumerate(weave(d, moved, block)):
-                    taps[b, (d + 1) * C : (d + 2) * C, k * 128 : (k + 1) * 128] = piece
+                    lanes = slice(at + k * 128, at + (k + 1) * 128)
+                    taps[(d + 1) * C : (d + 2) * C, lanes] = piece
             for d in range(2):
                 near = jnp.minimum(nb[b, d + 4], SLOTS)
-                taps[b, (d + 5) * C : (d + 6) * C, :] = jnp.where(
+                taps[(d + 5) * C : (d + 6) * C, at : at + 512] = jnp.where(
                     masks_z[d], pool_z_at(store, d, near), pool_z_at(store, d, b)
                 )
-            hidden = dot(conv, taps[b])
+            hidden = dot(conv, taps[:, at : at + 512])
             gate = 0.5 * jnp.tanh(0.5 * hidden) + 0.5
             slope[b] = gate * (1.0 + hidden * (1.0 - gate))
             acts.append(hidden * gate)
@@ -282,7 +284,8 @@
     send[OCT : OCT + 512, :] = projected
 
     copy.wait()
-    lat_copy.wait()
+    copies[1].wait()
+    copies[2].wait()
     for s in range(SLOTS):
         routed[s] = jnp.zeros((C, 128), BF)
     for j, (got, start) in enumerate(((lat_ref, 0), (got_xa, 256), (got_ya, 256), (got_xy, 256))):
@@ -298,7 +301,6 @@
     down_sum = dot(oct_grad, act2[...], NT)
     for k in range(4):
         sums_ref[256 + k * 128 : 256 + (k + 1) * 128, :] = down_sum[:, k * 128 : (k + 1) * 128]
-    conv_sum = jnp.zeros((C, 448), F32)
     for pair in range(SLOTS // 2):
         patch = dot(store[DOWN_BACK : DOWN_BACK + 512, 0:128], oct_grad[:, pair * 128 : (pair + 1) * 128])
         for side in range(2):
@@ -311,8 +313,10 @@
                 else:
                     both = jnp.where(low, pltpu.roll(first, 64, 1), second)
                 lanes = slice(k * 128, (k + 1) * 128)
-                hg_ref[b * C : (b + 1) * C, lanes] = (both * slope[b, :, lanes]).astype(BF)
-            conv_sum = conv_sum + dot(hg_ref[b * C : (b + 1) * C, :], taps[b], NT)
+                both = (both * slope[b, :, lanes]).astype(BF)
+                hg_ref[b * C : (b + 1) * C, lanes] = both
+                hg_row[:, b * 512 + k * 128 : b * 512 + (k + 1) * 128] = both
+    conv_sum = dot(hg_row[...], taps[...], NT)
     for k in range(3):
         sums_ref[k * C : (k + 1) * C, :] = conv_sum[:, k * 128 : (k + 1) * 128]
     sums_ref[3 * C : 4 * C, 0:C] = conv_sum[:, 384:448]
@@ -339,7 +343,10 @@
         send[at : at + 256, :] = far[d, 0:4].reshape(256, 128).astype(BF)
 
 
-def roll_kernel(nb, hg_ref, moved_ref, pool, pool_z, total, total_z):
+def roll_kernel(nb_hbm, hg_ref, moved_ref, pool, pool_z, total, total_z, nb, sem):
+    copy = pltpu.make_async_copy(nb_hbm, nb, sem)
+    copy.start()
+
     def put(d, lane, value):
         pool[d, :, :, lane : lane + 128] = value.reshape(SLOTS, C, 128)
 
@@ -352,6 +359,7 @@
             total[d, s] = jnp.zeros((C, 256), F32)
         for d in range(2):
             total_z[d, s] = jnp.zeros((C, 512), F32)
+    copy.wait()
     for b in range(SLOTS):
         for d in range(4):
             slot = jnp.minimum(nb[b, d], SLOTS)
@@ -582,18 +590,21 @@
         [pltpu.VMEM((C, 448), BF), pltpu.SemaphoreType.DMA((3,))],
         us=1.5,
     )
-    got_xa = beside_core(tie(got_xy, got_xb, got_yb, got_ya))
+    got_xa = beside_core(tie(got_xy, got_xb, got_yb, got_ya, store))
     hg, mine, other, send = call(
         main_kernel,
         [((512, 512), BF), ((448, 128), BF), ((448, 128), BF), ((SEND, 128), BF)],
         (neighbours, coarse_map, lat, xm, got_xa, got_xb, got_ya, got_yb, got_xy, store),
-        "ssh",
+        "hhh",
         [
+            pltpu.SMEM((SLOTS, 6), jnp.int32),
+            pltpu.SMEM((1, 8), jnp.int32),
+            pltpu.SemaphoreType.DMA((3,)),
             pltpu.VMEM((896, 128), F32),
             pltpu.VMEM((512, 128), BF),
-            pltpu.SemaphoreType.DMA,
             pltpu.VMEM((4, 17, C, 256), BF),
-            pltpu.VMEM((SLOTS, 448, 512), BF),
+            pltpu.VMEM((448, SLOTS * 512), BF),
+            pltpu.VMEM((C, SLOTS * 512), BF),
             pltpu.VMEM((SLOTS, C, 512), F32),
             pltpu.VMEM((512, 512), BF),
             pltpu.VMEM((SLOTS + 1, C, 128), BF),
@@ -608,23 +619,26 @@
     sum_step, steps = weight_sums(mine, other)
     mine = sum_step(0, ())
     got_xa = beside_x(tie(send[XA : XA + 256], mine))
-    got_xb = odd_x(tie(send[XB : XB + 256], mine))
+    got_xb = odd_x(send[XB : XB + 256])
     got_yb = odd_y(tie(send[YB : YB + 256], mine))
+    mine = sum_step(1, ())
+    got_ya = beside_core(tie(send[YA : OCT + 512], mine))
     (moved,) = call(
         roll_kernel,
         [((2048, 512), BF)],
-        (neighbours, tie(hg, mine, got_yb)),
-        "s",
+        (neighbours, tie(hg, mine, got_xb)),
+        "h",
         [
             pltpu.VMEM((4, 8, C, 256), BF),
             pltpu.VMEM((2, 8, C, 512), BF),
             pltpu.VMEM((4, 9, C, 256), F32),
             pltpu.VMEM((2, 9, C, 512), F32),
+            pltpu.SMEM((SLOTS, 6), jnp.int32),
+            pltpu.SemaphoreType.DMA,
         ],
         us=2.5,
     )
-    mine = sum_step(1, ())
-    got_ya = beside_core(tie(send[YA : OCT + 512], mine))
+    mine = sum_step(2, ())
     (near,) = call(
         near_kernel,
         [((512, 512), F32)],
@@ -633,7 +647,8 @@
         [pltpu.VMEM((448, 512), BF)],
         us=1.0,
     )
-    mine = sum_step(2, (got_xa, got_xb, got_yb, moved))
+    got_xy = beside_both(tie(send[OCT : OCT + 512], near))
+    mine = sum_step(3, (moved, got_ya, got_xa, got_yb, got_xb,))
     (grad,) = call(
         far_kernel,
         [((512, 512), BF)],
@@ -643,8 +658,6 @@
         1,
         us=1.8,
     )
-    got_xy = beside_both(tie(send[OCT : OCT + 512], grad))
-    mine = sum_step(3, (near, got_ya))
     got_x = beside_core(tie(got_xy, mine))
     (latent,) = call(
         latent_kernel,
@@ -655,10 +668,10 @@
         1,
         us=1.2,
     )
-    mine = sum_step(4, (grad,))
+    mine = sum_step(4, (near,))
     for at in range(5, steps):
         mine = sum_step(at, ())
-    mine, theirs = sum_step(steps, (got_x,))
+    mine, theirs = sum_step(steps, (grad, got_x,))
     scale = float(SLOTS * lax.axis_size("gx") * lax.axis_size("gy")) ** (-0.5)
     conv_grad, down_grad, head_grad = call(
         lambda *refs: scale_kernel(scale, *refs),

time: 49.1 us -> 44.4 us (0.904)
  starting transfers between devices: 20.7 us -> 18.8 us
  Pallas kernels: 17 us -> 15.2 us
  waiting for transfers between devices: 9.57 us -> 8.47 us
    ppermute x17, starting transfers between devices: 20.7 us -> 18.8 us  [send_to(): return lax.ppermute(value, ('gx', 'gy'), route(there))]
    pallas_call x8, Pallas kernels: 17 us -> 15.2 us  [call(): pl.pallas_call(kernel, out_shape=[pltpu.VMEM(shape, kind) if at < keep el...]
    ppermute x17, waiting for transfers between devices: 9.57 us -> 8.47 us  [send_to(): return lax.ppermute(value, ('gx', 'gy'), route(there))]
where the time goes in v4:
time: 44.4 us; the launch traced here: 44.2 us
  starting transfers between devices  18.8 us (42%)
  Pallas kernels  15.2 us (34%)
  waiting for transfers between devices  8.47 us (19%)
  between operations  1.42 us (3%)
    ppermute x17, starting transfers between devices, send_to(): return lax.ppermute(value, ('gx', 'gy'), route(there))  18.8 us
    pallas_call x8, Pallas kernels, call(): pl.pallas_call(kernel, out_shape=[pltpu.VMEM(shape, kind) if at < keep el...  15.2 us
    ppermute x17, waiting for transfers between devices, send_to(): return lax.ppermute(value, ('gx', 'gy'), route(there))  8.47 us
  transfers between devices with their start and end apart: 17, of which 7 were waited for; matrix products, arithmetic and copies ran while one was open for 0% of the time, Pallas kernels for 17%

profile of v4, /device:TPU:0, one launch (start us, length us, event | category | flops | bytes accessed | tf_op | source)
XLA Modules:
  0.0 44.2 jit_solution(3017848802394020748)
XLA Ops:
  1.3 1.6 %shard_map.119 = (bf16[512,512]{1,0:T(8,128)(2,1)S(1)}, bf16[784,128]{1,0:T(8,128)(2,1)S(1)}, bf16[256,128]{1,0:T(8,128)(2,1)S(1)}, bf16[784,128]{1,0:T(8,128)(2,1)S(1)}, bf16[256,128]{1,0:T(8,128)(2,1)S(1)}) custom-call(s32[1]{0:T(128)S(6)} %copy.13.counts, s32[1,8]{1,0:T(1,128)} %cmap.1, bf16[512,512]{1,0:T(8,128)(2,1)} %bitcast.4, bf16[512,128]{1,0:T(8,128)(2,1)} %bitcast.5), custom_call_target="tpu_custom_call" | custom-call | flops 1500000000 | bytes 4500000 | tf_op jit(solution)/shard_map/pallas_call | solution.py:549
  2.8 2.5 %collective-permute-start = (bf16[784,128]{1,0:T(8,128)(2,1)S(1)}, bf16[784,128]{1,0:T(8,128)(2,1)S(1)}, u32[]{:S(2)}, u32[]{:S(2)}) collective-permute-start(bf16[784,128]{1,0:T(8,128)(2,1)S(1)} %get-tuple-element.30), channel_id=1, source_target_pairs={{0,5},{1,4},{2,7},{3,6},{4,1},{5,0},{6,3},{7,2},{8,13},{9,12},{10,... | collective-permute-start | bytes 602120 | tf_op jit(solution)/shard_map/ppermute | solution.py:464
  5.3 0.7 %collective-permute-start.3 = (bf16[784,128]{1,0:T(8,128)(2,1)S(1)}, bf16[784,128]{1,0:T(8,128)(2,1)S(1)}, u32[]{:S(2)}, u32[]{:S(2)}) collective-permute-start(bf16[784,128]{1,0:T(8,128)(2,1)S(1)} %get-tuple-element.33), channel_id=1, source_target_pairs={{0,1},{1,0},{2,3},{3,2},{4,5},{5,4},{6,7},{7,6},{8,9},{9,8},{10,11... | collective-permute-start | bytes 602120 | tf_op jit(solution)/shard_map/ppermute | solution.py:464
  6.0 1.6 %collective-permute-start.2 = (bf16[256,128]{1,0:T(8,128)(2,1)S(1)}, bf16[256,128]{1,0:T(8,128)(2,1)S(1)}, u32[]{:S(2)}, u32[]{:S(2)}) collective-permute-start(bf16[256,128]{1,0:T(8,128)(2,1)S(1)} %get-tuple-element.32), channel_id=1, source_target_pairs={{0,3},{1,2},{2,1},{3,0},{4,7},{5,6},{6,5},{7,4},{8,11},{9,10},{10,... | collective-permute-start | bytes 196616 | tf_op jit(solution)/shard_map/ppermute | solution.py:464
  7.6 1.5 %shard_map.120.store = bf16[2880,512]{1,0:T(8,128)(2,1)S(1)} custom-call(bf16[512,512]{1,0:T(8,128)(2,1)S(1)} %get-tuple-element.29.xm, bf16[64,448]{1,0:T(8,128)(2,1)} %conv_ref.3, bf16[128,512]{1,0:T(8,128)(2,1)} %down_hbm.1, bf16[128,128]{1,0:T(8,128)(2,1)} %head_hbm.1), custom_call_target="tpu_custom_call" | custom-call | flops 1500000000 | bytes 4500000 | tf_op jit(solution)/shard_map/pallas_call | solution.py:549
  9.1 0.6 %collective-permute-done.2.got_yb = bf16[256,128]{1,0:T(8,128)(2,1)S(1)} collective-permute-done((bf16[256,128]{1,0:T(8,128)(2,1)S(1)}, bf16[256,128]{1,0:T(8,128)(2,1)S(1)}, u32[]{:S(2)}, u32[]{:S(2)}) %collective-permute-start.2) | collective-permute-done | bytes 65568 | tf_op jit(solution)/shard_map/ppermute | solution.py:464
  9.7 2.4 %collective-permute-done.got_xy = bf16[784,128]{1,0:T(8,128)(2,1)S(1)} collective-permute-done((bf16[784,128]{1,0:T(8,128)(2,1)S(1)}, bf16[784,128]{1,0:T(8,128)(2,1)S(1)}, u32[]{:S(2)}, u32[]{:S(2)}) %collective-permute-start) | collective-permute-done | bytes 200736 | tf_op jit(solution)/shard_map/ppermute | solution.py:464
  12.1 0.1 collective-permute-start.4
  12.2 1.4 %collective-permute-done.4.got_xa = bf16[784,128]{1,0:T(8,128)(2,1)S(1)} collective-permute-done((bf16[784,128]{1,0:T(8,128)(2,1)S(1)}, bf16[784,128]{1,0:T(8,128)(2,1)S(1)}, u32[]{:S(2)}, u32[]{:S(2)}) %collective-permute-start.4) | collective-permute-done | bytes 200736 | tf_op jit(solution)/shard_map/ppermute | solution.py:464
  13.6 4.9 %shard_map.121 = (bf16[512,512]{1,0:T(8,128)(2,1)S(1)}, bf16[448,128]{1,0:T(8,128)(2,1)S(1)}, bf16[448,128]{1,0:T(8,128)(2,1)S(1)}, bf16[1536,128]{1,0:T(8,128)(2,1)S(1)}) custom-call(s32[8,6]{1,0:T(8,128)} %nb_hbm.3, s32[1,8]{1,0:T(1,128)} %cmap.1, bf16[512,128]{1,0:T(8,128)(2,1)} %bitcast.6, bf16[512,512]{1,0:T(8,128)(2,1)S(1)} %get-tuple-element.29.xm, ...), custom_call_target="tpu_custom_call" | custom-call | flops 6000000000 | bytes 18000000 | tf_op jit(solution)/shard_map/pallas_call | solution.py:549
  18.5 0.2 collective-permute-start.5
  18.7 1.2 %collective-permute-done.5 = bf16[448,128]{1,0:T(8,128)(2,1)S(1)} collective-permute-done((bf16[448,128]{1,0:T(8,128)(2,1)S(1)}, bf16[448,128]{1,0:T(8,128)(2,1)S(1)}, u32[]{:S(2)}, u32[]{:S(2)}) %collective-permute-start.5) | collective-permute-done | bytes 114720 | tf_op jit(solution)/shard_map/ppermute | solution.py:464
  19.9 1.3 %collective-permute-start.6 = (bf16[448,128]{1,0:T(8,128)(2,1)S(1)}, bf16[448,128]{1,0:T(8,128)(2,1)S(1)}, u32[]{:S(2)}, u32[]{:S(2)}) collective-permute-start(bf16[448,128]{1,0:T(8,128)(2,1)S(1)} %add_convert_fusion.4), channel_id=1, source_target_pairs={{0,3},{1,4},{2,7},{3,0},{4,1},{5,6},{6,5},{7,2},{8,13},{9,10},{10,... | collective-permute-start | bytes 344072 | tf_op jit(solution)/shard_map/ppermute | solution.py:464
  21.2 1.4 %collective-permute-start.7 = (bf16[256,128]{1,0:T(8,128)(2,1)S(1)}, bf16[256,128]{1,0:T(8,128)(2,1)S(1)}, u32[]{:S(2)}, u32[]{:S(2)}) collective-permute-start(bf16[256,128]{1,0:T(8,128)(2,1)S(1)} %get-tuple-element.55), channel_id=1, source_target_pairs={{0,1},{1,0},{2,3},{3,2},{4,8},{5,9},{6,10},{7,11},{8,4},{9,5},{10,... | collective-permute-start | bytes 196616 | tf_op jit(solution)/shard_map/ppermute | solution.py:464
  22.6 2.7 %collective-permute-start.11 = (bf16[256,128]{1,0:T(8,128)(2,1)S(1)}, bf16[256,128]{1,0:T(8,128)(2,1)S(1)}, u32[]{:S(2)}, u32[]{:S(2)}) collective-permute-start(bf16[256,128]{1,0:T(8,128)(2,1)S(1)} %get-tuple-element.43), channel_id=1, source_target_pairs={{0,4},{1,5},{2,6},{3,7},{4,0},{5,1},{6,2},{7,3},{8,12},{9,13},{10,... | collective-permute-start | bytes 196616 | tf_op jit(solution)/shard_map/ppermute | solution.py:464
  25.3 0.9 %collective-permute-start.12 = (bf16[256,128]{1,0:T(8,128)(2,1)S(1)}, bf16[256,128]{1,0:T(8,128)(2,1)S(1)}, u32[]{:S(2)}, u32[]{:S(2)}) collective-permute-start(bf16[256,128]{1,0:T(8,128)(2,1)S(1)} %get-tuple-element.44), channel_id=1, source_target_pairs={{0,3},{1,2},{2,1},{3,0},{4,7},{5,6},{6,5},{7,4},{8,11},{9,10},{10,... | collective-permute-start | bytes 196616 | tf_op jit(solution)/shard_map/ppermute | solution.py:464
  26.3 0.2 collective-permute-start.8
  26.5 1.1 %collective-permute-start.10 = (bf16[768,128]{1,0:T(8,128)(2,1)S(1)}, bf16[768,128]{1,0:T(8,128)(2,1)S(1)}, u32[]{:S(2)}, u32[]{:S(2)}) collective-permute-start(bf16[768,128]{1,0:T(8,128)(2,1)S(1)} %slice.17), channel_id=1, source_target_pairs={{0,1},{1,0},{2,3},{3,2},{4,5},{5,4},{6,7},{7,6},{8,9},{9,8},{10,11... | collective-permute-start | bytes 589832 | tf_op jit(solution)/shard_map/ppermute | solution.py:464
  27.6 2.0 %shard_map.122.moved_ref = bf16[2048,512]{1,0:T(8,128)(2,1)S(1)} custom-call(s32[8,6]{1,0:T(8,128)} %nb_hbm.3, bf16[512,512]{1,0:T(8,128)(2,1)S(1)} %get-tuple-element.39.hg_ref), custom_call_target="tpu_custom_call" | custom-call | flops 2500000000 | bytes 7500000 | tf_op jit(solution)/shard_map/pallas_call | solution.py:549
  29.6 0.9 %collective-permute-done.8 = bf16[448,128]{1,0:T(8,128)(2,1)S(1)} collective-permute-done((bf16[448,128]{1,0:T(8,128)(2,1)S(1)}, bf16[448,128]{1,0:T(8,128)(2,1)S(1)}, u32[]{:S(2)}, u32[]{:S(2)}) %collective-permute-start.8) | collective-permute-done | bytes 114720 | tf_op jit(solution)/shard_map/ppermute | solution.py:464
  30.6 1.2 %collective-permute-start.13 = (bf16[448,128]{1,0:T(8,128)(2,1)S(1)}, bf16[448,128]{1,0:T(8,128)(2,1)S(1)}, u32[]{:S(2)}, u32[]{:S(2)}) collective-permute-start(bf16[448,128]{1,0:T(8,128)(2,1)S(1)} %add_convert_fusion.2), channel_id=1, source_target_pairs={{0,9},{1,16},{2,19},{3,10},{4,21},{5,12},{6,15},{7,22},{8,25},{9,0... | collective-permute-start | bytes 344072 | tf_op jit(solution)/shard_map/ppermute | solution.py:464
  31.8 1.1 %shard_map.123.near_ref = f32[512,512]{1,0:T(8,128)S(1)} custom-call(bf16[512,512]{1,0:T(8,128)(2,1)S(1)} %get-tuple-element.39.hg_ref, bf16[2048,512]{1,0:T(8,128)(2,1)S(1)} %shard_map.122.moved_ref, bf16[64,448]{1,0:T(8,128)(2,1)S(1)} %copy-done), custom_call_target="tpu_custom_call" | custom-call | flops 1000000000 | bytes 3000000 | tf_op jit(solution)/shard_map/pallas_call | solution.py:549
  32.9 1.0 %collective-permute-start.9 = (bf16[512,128]{1,0:T(8,128)(2,1)S(1)}, bf16[512,128]{1,0:T(8,128)(2,1)S(1)}, u32[]{:S(2)}, u32[]{:S(2)}) collective-permute-start(bf16[512,128]{1,0:T(8,128)(2,1)S(1)} %slice.15), channel_id=1, source_target_pairs={{0,5},{1,4},{2,7},{3,6},{4,1},{5,0},{6,3},{7,2},{8,13},{9,12},{10,... | collective-permute-start | bytes 393224 | tf_op jit(solution)/shard_map/ppermute | solution.py:464
  33.9 1.0 %collective-permute-done.13 = bf16[448,128]{1,0:T(8,128)(2,1)S(1)} collective-permute-done((bf16[448,128]{1,0:T(8,128)(2,1)S(1)}, bf16[448,128]{1,0:T(8,128)(2,1)S(1)}, u32[]{:S(2)}, u32[]{:S(2)}) %collective-permute-start.13) | collective-permute-done | bytes 114720 | tf_op jit(solution)/shard_map/ppermute | solution.py:464
  35.0 0.0 copy-start.1
  35.0 3.1 %collective-permute-start.15 = (bf16[448,128]{1,0:T(8,128)(2,1)S(1)}, bf16[448,128]{1,0:T(8,128)(2,1)S(1)}, u32[]{:S(2)}, u32[]{:S(2)}) collective-permute-start(bf16[448,128]{1,0:T(8,128)(2,1)S(1)} %add_convert_fusion.1), channel_id=1, source_target_pairs={{0,17},{1,8},{2,11},{3,18},{4,13},{5,20},{6,23},{7,14},{8,1},{9,24... | collective-permute-start | bytes 344072 | tf_op jit(solution)/shard_map/ppermute | solution.py:464
  38.1 0.7 %collective-permute-start.14 = (bf16[512,128]{1,0:T(8,128)(2,1)S(1)}, bf16[512,128]{1,0:T(8,128)(2,1)S(1)}, u32[]{:S(2)}, u32[]{:S(2)}) collective-permute-start(bf16[512,128]{1,0:T(8,128)(2,1)S(1)} %collective-permute-done.9.got_xy), channel_id=1, source_target_pairs={{0,1},{1,0},{2,3},{3,2},{4,5},{5,4},{6,7},{7,6},{8,9},{9,8},{10,11... | collective-permute-start | bytes 393224 | tf_op jit(solution)/shard_map/ppermute | solution.py:464
  38.8 1.8 %shard_map.125 = bf16[512,512]{1,0:T(8,128)(2,1)} custom-call(s32[1]{0:T(128)S(6)} %copy.13.counts, f32[512,512]{1,0:T(8,128)S(1)} %shard_map.123.near_ref, bf16[256,128]{1,0:T(8,128)(2,1)S(1)} %collective-permute-done.11.got_xa, bf16[256,128]{1,0:T(8,128)(2,1)S(1)} %collective-permute-done.7.got_xb, bf16[768,128]{1,0:T(8,128)(2,1)S(1)} %collective-permute-done.10.got_ya, ...), custom_call_target="tpu_custom_call" | custom-call | flops 1800000000 | bytes 5400000 | tf_op jit(solution)/shard_map/pallas_call | solution.py:549
  40.7 0.9 %collective-permute-done.15 = bf16[448,128]{1,0:T(8,128)(2,1)S(1)} collective-permute-done((bf16[448,128]{1,0:T(8,128)(2,1)S(1)}, bf16[448,128]{1,0:T(8,128)(2,1)S(1)}, u32[]{:S(2)}, u32[]{:S(2)}) %collective-permute-start.15) | collective-permute-done | bytes 114720 | tf_op jit(solution)/shard_map/ppermute | solution.py:464
  41.6 0.3 collective-permute-start.16
  41.9 1.2 %shard_map.124 = bf16[512,128]{1,0:T(8,128)(2,1)} custom-call(s32[1,8]{1,0:T(1,128)S(1)} %copy-done.1, bf16[1536,128]{1,0:T(8,128)(2,1)S(1)} %get-tuple-element.35.own, bf16[512,128]{1,0:T(8,128)(2,1)S(1)} %collective-permute-done.14.got_x, bf16[768,128]{1,0:T(8,128)(2,1)S(1)} %collective-permute-done.10.got_ya, ...), custom_call_target="tpu_custom_call" | custom-call | flops 1200000000 | bytes 3600000 | tf_op jit(solution)/shard_map/pallas_call | solution.py:549
  43.2 1.0 %shard_map.126 = (f32[64,448]{1,0:T(8,128)}, f32[128,512]{1,0:T(8,128)}, f32[128,128]{1,0:T(8,128)}) custom-call(bf16[448,128]{1,0:T(8,128)(2,1)S(1)} %add_convert_fusion.refs_0_, bf16[448,128]{1,0:T(8,128)(2,1)S(1)} %collective-permute-done.16.refs_1_), custom_call_target="tpu_custom_call" | custom-call | flops 1000000000 | bytes 3000000 | tf_op jit(solution)/shard_map/pallas_call | solution.py:549
  (22 shorter events, 0.2 us)
Async XLA Ops:
  2.8 9.3 %collective-permute-start = (bf16[784,128]{1,0:T(8,128)(2,1)S(1)}, bf16[784,128]{1,0:T(8,128)(2,1)S(1)}, u32[]{:S(2)}, u32[]{:S(2)}) collective-permute-start(bf16[784,128]{1,0:T(8,128)(2,1)S(1)} %get-tuple-element.30), channel_id=1, source_target_pairs={{0,5},{1,4},{2,7},{3,6},{4,1},{5,0},{6,3},{7,2},{8,13},{9,12},{10,... | collective-permute-start | bytes 602120 | tf_op jit(solution)/shard_map/ppermute | solution.py:464
  5.3 6.8 %collective-permute-start.3 = (bf16[784,128]{1,0:T(8,128)(2,1)S(1)}, bf16[784,128]{1,0:T(8,128)(2,1)S(1)}, u32[]{:S(2)}, u32[]{:S(2)}) collective-permute-start(bf16[784,128]{1,0:T(8,128)(2,1)S(1)} %get-tuple-element.33), channel_id=1, source_target_pairs={{0,1},{1,0},{2,3},{3,2},{4,5},{5,4},{6,7},{7,6},{8,9},{9,8},{10,11... | collective-permute-start | bytes 602120 | tf_op jit(solution)/shard_map/ppermute | solution.py:464
  6.0 3.1 %collective-permute-start.1 = (bf16[256,128]{1,0:T(8,128)(2,1)S(1)}, bf16[256,128]{1,0:T(8,128)(2,1)S(1)}, u32[]{:S(2)}, u32[]{:S(2)}) collective-permute-start(bf16[256,128]{1,0:T(8,128)(2,1)S(1)} %get-tuple-element.31), channel_id=1, source_target_pairs={{0,1},{1,0},{2,3},{3,2},{4,8},{5,9},{6,10},{7,11},{8,4},{9,5},{10,... | collective-permute-start | bytes 196616 | tf_op jit(solution)/shard_map/ppermute | solution.py:464
  6.0 3.7 %collective-permute-start.2 = (bf16[256,128]{1,0:T(8,128)(2,1)S(1)}, bf16[256,128]{1,0:T(8,128)(2,1)S(1)}, u32[]{:S(2)}, u32[]{:S(2)}) collective-permute-start(bf16[256,128]{1,0:T(8,128)(2,1)S(1)} %get-tuple-element.32), channel_id=1, source_target_pairs={{0,3},{1,2},{2,1},{3,0},{4,7},{5,6},{6,5},{7,4},{8,11},{9,10},{10,... | collective-permute-start | bytes 196616 | tf_op jit(solution)/shard_map/ppermute | solution.py:464
  12.1 1.4 %collective-permute-start.4 = (bf16[784,128]{1,0:T(8,128)(2,1)S(1)}, bf16[784,128]{1,0:T(8,128)(2,1)S(1)}, u32[]{:S(2)}, u32[]{:S(2)}) collective-permute-start(bf16[784,128]{1,0:T(8,128)(2,1)S(1)} %collective-permute-done.got_xy), channel_id=1, source_target_pairs={{0,1},{1,0},{2,3},{3,2},{4,5},{5,4},{6,7},{7,6},{8,9},{9,8},{10,11... | collective-permute-start | bytes 602120 | tf_op jit(solution)/shard_map/ppermute | solution.py:464
  18.5 1.4 %collective-permute-start.5 = (bf16[448,128]{1,0:T(8,128)(2,1)S(1)}, bf16[448,128]{1,0:T(8,128)(2,1)S(1)}, u32[]{:S(2)}, u32[]{:S(2)}) collective-permute-start(bf16[448,128]{1,0:T(8,128)(2,1)S(1)} %get-tuple-element.38), channel_id=1, source_target_pairs={{0,1},{1,0},{2,3},{3,2},{4,5},{5,4},{6,7},{7,6},{8,9},{9,8},{10,11... | collective-permute-start | bytes 344072 | tf_op jit(solution)/shard_map/ppermute | solution.py:464
  19.9 6.3 %collective-permute-start.6 = (bf16[448,128]{1,0:T(8,128)(2,1)S(1)}, bf16[448,128]{1,0:T(8,128)(2,1)S(1)}, u32[]{:S(2)}, u32[]{:S(2)}) collective-permute-start(bf16[448,128]{1,0:T(8,128)(2,1)S(1)} %add_convert_fusion.4), channel_id=1, source_target_pairs={{0,3},{1,4},{2,7},{3,0},{4,1},{5,6},{6,5},{7,2},{8,13},{9,10},{10,... | collective-permute-start | bytes 344072 | tf_op jit(solution)/shard_map/ppermute | solution.py:464
  21.2 5.3 %collective-permute-start.7 = (bf16[256,128]{1,0:T(8,128)(2,1)S(1)}, bf16[256,128]{1,0:T(8,128)(2,1)S(1)}, u32[]{:S(2)}, u32[]{:S(2)}) collective-permute-start(bf16[256,128]{1,0:T(8,128)(2,1)S(1)} %get-tuple-element.55), channel_id=1, source_target_pairs={{0,1},{1,0},{2,3},{3,2},{4,8},{5,9},{6,10},{7,11},{8,4},{9,5},{10,... | collective-permute-start | bytes 196616 | tf_op jit(solution)/shard_map/ppermute | solution.py:464
  22.6 8.0 %collective-permute-start.11 = (bf16[256,128]{1,0:T(8,128)(2,1)S(1)}, bf16[256,128]{1,0:T(8,128)(2,1)S(1)}, u32[]{:S(2)}, u32[]{:S(2)}) collective-permute-start(bf16[256,128]{1,0:T(8,128)(2,1)S(1)} %get-tuple-element.43), channel_id=1, source_target_pairs={{0,4},{1,5},{2,6},{3,7},{4,0},{5,1},{6,2},{7,3},{8,12},{9,13},{10,... | collective-permute-start | bytes 196616 | tf_op jit(solution)/shard_map/ppermute | solution.py:464
  25.3 5.3 %collective-permute-start.12 = (bf16[256,128]{1,0:T(8,128)(2,1)S(1)}, bf16[256,128]{1,0:T(8,128)(2,1)S(1)}, u32[]{:S(2)}, u32[]{:S(2)}) collective-permute-start(bf16[256,128]{1,0:T(8,128)(2,1)S(1)} %get-tuple-element.44), channel_id=1, source_target_pairs={{0,3},{1,2},{2,1},{3,0},{4,7},{5,6},{6,5},{7,4},{8,11},{9,10},{10,... | collective-permute-start | bytes 196616 | tf_op jit(solution)/shard_map/ppermute | solution.py:464
  26.3 4.3 %collective-permute-start.8 = (bf16[448,128]{1,0:T(8,128)(2,1)S(1)}, bf16[448,128]{1,0:T(8,128)(2,1)S(1)}, u32[]{:S(2)}, u32[]{:S(2)}) collective-permute-start(bf16[448,128]{1,0:T(8,128)(2,1)S(1)} %add_convert_fusion.3), channel_id=1, source_target_pairs={{0,5},{1,2},{2,1},{3,6},{4,7},{5,0},{6,3},{7,4},{8,11},{9,12},{10,... | collective-permute-start | bytes 344072 | tf_op jit(solution)/shard_map/ppermute | solution.py:464
  26.5 5.3 %copy-start = (bf16[64,448]{1,0:T(8,128)(2,1)S(1)}, bf16[64,448]{1,0:T(8,128)(2,1)}, u32[]{:S(2)}) copy-start(bf16[64,448]{1,0:T(8,128)(2,1)} %conv_ref.3) | copy-start | bytes 172036
  26.5 4.1 %collective-permute-start.10 = (bf16[768,128]{1,0:T(8,128)(2,1)S(1)}, bf16[768,128]{1,0:T(8,128)(2,1)S(1)}, u32[]{:S(2)}, u32[]{:S(2)}) collective-permute-start(bf16[768,128]{1,0:T(8,128)(2,1)S(1)} %slice.17), channel_id=1, source_target_pairs={{0,1},{1,0},{2,3},{3,2},{4,5},{5,4},{6,7},{7,6},{8,9},{9,8},{10,11... | collective-permute-start | bytes 589832 | tf_op jit(solution)/shard_map/ppermute | solution.py:464
  30.6 4.3 %collective-permute-start.13 = (bf16[448,128]{1,0:T(8,128)(2,1)S(1)}, bf16[448,128]{1,0:T(8,128)(2,1)S(1)}, u32[]{:S(2)}, u32[]{:S(2)}) collective-permute-start(bf16[448,128]{1,0:T(8,128)(2,1)S(1)} %add_convert_fusion.2), channel_id=1, source_target_pairs={{0,9},{1,16},{2,19},{3,10},{4,21},{5,12},{6,15},{7,22},{8,25},{9,0... | collective-permute-start | bytes 344072 | tf_op jit(solution)/shard_map/ppermute | solution.py:464
  32.9 5.2 %collective-permute-start.9 = (bf16[512,128]{1,0:T(8,128)(2,1)S(1)}, bf16[512,128]{1,0:T(8,128)(2,1)S(1)}, u32[]{:S(2)}, u32[]{:S(2)}) collective-permute-start(bf16[512,128]{1,0:T(8,128)(2,1)S(1)} %slice.15), channel_id=1, source_target_pairs={{0,5},{1,4},{2,7},{3,6},{4,1},{5,0},{6,3},{7,2},{8,13},{9,12},{10,... | collective-permute-start | bytes 393224 | tf_op jit(solution)/shard_map/ppermute | solution.py:464
  35.0 6.9 %copy-start.1 = (s32[1,8]{1,0:T(1,128)S(1)}, s32[1,8]{1,0:T(1,128)}, u32[]{:S(2)}) copy-start(s32[1,8]{1,0:T(1,128)} %cmap.1) | copy-start | bytes 100
  35.0 6.6 %collective-permute-start.15 = (bf16[448,128]{1,0:T(8,128)(2,1)S(1)}, bf16[448,128]{1,0:T(8,128)(2,1)S(1)}, u32[]{:S(2)}, u32[]{:S(2)}) collective-permute-start(bf16[448,128]{1,0:T(8,128)(2,1)S(1)} %add_convert_fusion.1), channel_id=1, source_target_pairs={{0,17},{1,8},{2,11},{3,18},{4,13},{5,20},{6,23},{7,14},{8,1},{9,24... | collective-permute-start | bytes 344072 | tf_op jit(solution)/shard_map/ppermute | solution.py:464
  38.1 3.5 %collective-permute-start.14 = (bf16[512,128]{1,0:T(8,128)(2,1)S(1)}, bf16[512,128]{1,0:T(8,128)(2,1)S(1)}, u32[]{:S(2)}, u32[]{:S(2)}) collective-permute-start(bf16[512,128]{1,0:T(8,128)(2,1)S(1)} %collective-permute-done.9.got_xy), channel_id=1, source_target_pairs={{0,1},{1,0},{2,3},{3,2},{4,5},{5,4},{6,7},{7,6},{8,9},{9,8},{10,11... | collective-permute-start | bytes 393224 | tf_op jit(solution)/shard_map/ppermute | solution.py:464
  41.6 1.5 %collective-permute-start.16 = (bf16[448,128]{1,0:T(8,128)(2,1)S(1)}, bf16[448,128]{1,0:T(8,128)(2,1)S(1)}, u32[]{:S(2)}, u32[]{:S(2)}) collective-permute-start(bf16[448,128]{1,0:T(8,128)(2,1)S(1)} %add_convert_fusion.refs_0_), channel_id=1, source_target_pairs={{0,1},{1,0},{2,3},{3,2},{4,5},{5,4},{6,7},{7,6},{8,9},{9,8},{10,11... | collective-permute-start | bytes 344072 | tf_op jit(solution)/shard_map/ppermute | solution.py:464

commit v5 on v4

--- a/solution.py
+++ b/solution.py
@@ -63,7 +63,7 @@
     return one_hot(lane % 8 * 64 + lane // 8, 512)
 
 
-CONV, DOWN, DOWN_BACK, POOL, POOL_Z, STORE = 0, 64, 192, 704, 1728, 2880
+CONV, DOWN, DOWN_BACK, POOL, POOL_Z, XM, STORE = 0, 64, 192, 704, 1728, 2880, 3392
 
 
 def pool_at(store, d, slot):
@@ -138,13 +138,13 @@
 
 
 def pack_kernel(
-    counts, cmap_hbm, x_hbm, lat_hbm,
-    xm, send_xa, send_xb, send_ya, send_yb,
-    cmap, sems,
+    cmap_hbm, x_hbm, lat_hbm,
+    send_xa, send_xb, send_ya, send_yb,
+    x_ref, cmap, sems,
 ):
     copies = load(
         [
-            (cmap_hbm, cmap), (x_hbm, xm),
+            (cmap_hbm, cmap), (x_hbm, x_ref),
             (lat_hbm, send_xa.at[256:768]), (lat_hbm, send_ya.at[256:768]),
         ],
         sems,
@@ -153,15 +153,11 @@
     packs = [pack(d) for d in range(4)]
     for copy in copies[:2]:
         copy.wait()
-    for b in range(1, SLOTS):
-        @pl.when(b >= counts[0])
-        def _():
-            xm[b * C : (b + 1) * C, :] = jnp.zeros((C, 512), BF)
-    masked = xm[...]
+    cube = x_ref[...]
     low = lane_of((256, 128)) < 64
     faces = []
     for d in range(4):
-        packed = dot(parts(masked, d), packs[d])
+        packed = dot(parts(cube, d), packs[d])
         faces.append(jnp.where(low, packed[0:256], packed[256:512]))
     even = px == 0
     send_xa[0:256, :] = jnp.where(even, faces[0], faces[1]).astype(BF)
@@ -180,9 +176,10 @@
         copy.wait()
 
 
-def prep_kernel(xm, conv_hbm, down_hbm, head_hbm, store, conv, sems):
+def prep_kernel(counts, x_hbm, conv_hbm, down_hbm, head_hbm, store, conv, sems):
     copies = load(
         [
+            (x_hbm, store.at[XM : XM + 512]),
             (down_hbm, store.at[DOWN : DOWN + 128]),
             (conv_hbm, conv),
             (head_hbm, store.at[DOWN_BACK : DOWN_BACK + 128, 128:256]),
@@ -201,15 +198,20 @@
         start = POOL_Z + d * 9 * C
         store[start : start + 512, lane : lane + 128] = value
 
-    roll_blocks(xm, put, put_z)
     copies[0].wait()
+    for b in range(1, SLOTS):
+        @pl.when(b >= counts[0])
+        def _():
+            store[XM + b * C : XM + (b + 1) * C, :] = jnp.zeros((C, 512), BF)
+    roll_blocks(store.at[XM : XM + 512], put, put_z)
+    copies[1].wait()
     down = store[DOWN : DOWN + 128, :]
     table = regroup()
     store[DOWN : DOWN + 128, :] = dot(down, table, NT).astype(BF)
     store[DOWN_BACK : DOWN_BACK + 512, 0:128] = dot(table, down, NT).astype(BF)
-    copies[1].wait()
+    copies[2].wait()
     store[CONV : CONV + C, 0:448] = conv[...]
-    copies[2].wait()
+    copies[3].wait()
 
 
 YA, OCT, XA, XB, YB, SEND = 0, 256, 768, 1024, 1280, 1536
@@ -217,7 +219,7 @@
 
 def main_kernel(
     nb_hbm, cmap_hbm, lat_hbm,
-    xm, got_xa, got_xb, got_ya, got_yb, got_xy, store,
+    got_xa, got_xb, got_ya, got_yb, got_xy, store,
     hg_ref, mine_ref, other_ref, send,
     nb, cmap, sems, sums_ref, lat_ref, reach, taps, hg_row, slope, act2, routed, far, maps_v, maps_s, sem,
 ):
@@ -251,7 +253,7 @@
     for pair in range(SLOTS // 2):
         acts = []
         for b in (2 * pair, 2 * pair + 1):
-            block = xm[b * C : (b + 1) * C, :]
+            block = store[XM + b * C : XM + (b + 1) * C, :]
             at = b * 512
             taps[0:C, at : at + 512] = block
             for d in range(4):
@@ -514,6 +516,8 @@
         while bit < lax.axis_size(axis):
             bits.append((axis, bit))
             bit *= 2
+    if len(bits) > 2:
+        bits.insert(1, bits.pop(2))
     turned = []
     for at in range(0, len(bits) - 1, 2):
         turned += [bits[at + 1], bits[at]]
@@ -567,15 +571,14 @@
 ):
     flat = features.reshape(SLOTS * C, 512)
     lat = latent_grad.reshape(512, 128)
-    xm, send_xa, send_xb, send_ya, send_yb = call(
+    send_xa, send_xb, send_ya, send_yb = call(
         pack_kernel,
         [
-            ((512, 512), BF),
             ((784, 128), BF), ((256, 128), BF), ((784, 128), BF), ((256, 128), BF),
         ],
-        (counts, coarse_map, flat, lat),
-        "shhh",
-        [pltpu.SMEM((1, 8), jnp.int32), pltpu.SemaphoreType.DMA((4,))],
+        (coarse_map, flat, lat),
+        "hhh",
+        [pltpu.VMEM((512, 512), BF), pltpu.SMEM((1, 8), jnp.int32), pltpu.SemaphoreType.DMA((4,))],
         us=1.5,
     )
     got_xy = beside_both(send_xa)
@@ -585,16 +588,16 @@
     (store,) = call(
         prep_kernel,
         [((STORE, 512), BF)],
-        (xm, conv_weight, down_weight, head_weight),
-        "vhhh",
-        [pltpu.VMEM((C, 448), BF), pltpu.SemaphoreType.DMA((3,))],
+        (counts, flat, conv_weight, down_weight, head_weight),
+        "shhhh",
+        [pltpu.VMEM((C, 448), BF), pltpu.SemaphoreType.DMA((4,))],
         us=1.5,
     )
     got_xa = beside_core(tie(got_xy, got_xb, got_yb, got_ya, store))
     hg, mine, other, send = call(
         main_kernel,
         [((512, 512), BF), ((448, 128), BF), ((448, 128), BF), ((SEND, 128), BF)],
-        (neighbours, coarse_map, lat, xm, got_xa, got_xb, got_ya, got_yb, got_xy, store),
+        (neighbours, coarse_map, lat, got_xa, got_xb, got_ya, got_yb, got_xy, store),
         "hhh",
         [
             pltpu.SMEM((SLOTS, 6), jnp.int32),

time: 44.4 us -> 42.2 us (0.950)
  waiting for transfers between devices: 8.47 us -> 5.61 us
  Pallas kernels: 15.2 us -> 16 us
    ppermute x17, waiting for transfers between devices: 8.47 us -> 5.61 us  [send_to(): return lax.ppermute(value, ('gx', 'gy'), route(there))]
    pallas_call x8, Pallas kernels: 15.2 us -> 16 us  [call(): pl.pallas_call(kernel, out_shape=[pltpu.VMEM(shape, kind) if at < keep el...]
  transfers between devices with their start and end apart: 17 -> 17, of which waited for: 7 -> 6; matrix products, arithmetic and copies ran while one was open for 0% -> 0% of each run, Pallas kernels for 17% -> 21%
where the time goes in v5:
time: 42.2 us; the launch traced here: 42 us
  starting transfers between devices  18.7 us (44%)
  Pallas kernels  16 us (38%)
  waiting for transfers between devices  5.61 us (13%)
  between operations  1.45 us (3%)
    ppermute x17, starting transfers between devices, send_to(): return lax.ppermute(value, ('gx', 'gy'), route(there))  18.7 us
    pallas_call x8, Pallas kernels, call(): pl.pallas_call(kernel, out_shape=[pltpu.VMEM(shape, kind) if at < keep el...  16 us
    ppermute x17, waiting for transfers between devices, send_to(): return lax.ppermute(value, ('gx', 'gy'), route(there))  5.61 us
  transfers between devices with their start and end apart: 17, of which 6 were waited for; matrix products, arithmetic and copies ran while one was open for 0% of the time, Pallas kernels for 21%

profile of v5, /device:TPU:0, one launch (start us, length us, event | category | flops | bytes accessed | tf_op | source)
XLA Modules:
  0.0 42.0 jit_solution(5301206012125583720)
XLA Ops:
  0.6 1.5 %shard_map.119 = (bf16[784,128]{1,0:T(8,128)(2,1)S(1)}, bf16[256,128]{1,0:T(8,128)(2,1)S(1)}, bf16[784,128]{1,0:T(8,128)(2,1)S(1)}, bf16[256,128]{1,0:T(8,128)(2,1)S(1)}) custom-call(s32[1,8]{1,0:T(1,128)} %cmap.1, bf16[512,512]{1,0:T(8,128)(2,1)} %bitcast.4, bf16[512,128]{1,0:T(8,128)(2,1)} %bitcast.6), custom_call_target="tpu_custom_call" | custom-call | flops 1500000000 | bytes 4500000 | tf_op jit(solution)/shard_map/pallas_call | solution.py:553
  2.1 2.5 %collective-permute-start = (bf16[784,128]{1,0:T(8,128)(2,1)S(1)}, bf16[784,128]{1,0:T(8,128)(2,1)S(1)}, u32[]{:S(2)}, u32[]{:S(2)}) collective-permute-start(bf16[784,128]{1,0:T(8,128)(2,1)S(1)} %get-tuple-element.28), channel_id=1, source_target_pairs={{0,5},{1,4},{2,7},{3,6},{4,1},{5,0},{6,3},{7,2},{8,13},{9,12},{10,... | collective-permute-start | bytes 602120 | tf_op jit(solution)/shard_map/ppermute | solution.py:466
  4.6 0.7 %collective-permute-start.3 = (bf16[784,128]{1,0:T(8,128)(2,1)S(1)}, bf16[784,128]{1,0:T(8,128)(2,1)S(1)}, u32[]{:S(2)}, u32[]{:S(2)}) collective-permute-start(bf16[784,128]{1,0:T(8,128)(2,1)S(1)} %get-tuple-element.31), channel_id=1, source_target_pairs={{0,1},{1,0},{2,3},{3,2},{4,5},{5,4},{6,7},{7,6},{8,9},{9,8},{10,11... | collective-permute-start | bytes 602120 | tf_op jit(solution)/shard_map/ppermute | solution.py:466
  5.3 0.0 collective-permute-start.1
  5.3 1.6 %collective-permute-start.2 = (bf16[256,128]{1,0:T(8,128)(2,1)S(1)}, bf16[256,128]{1,0:T(8,128)(2,1)S(1)}, u32[]{:S(2)}, u32[]{:S(2)}) collective-permute-start(bf16[256,128]{1,0:T(8,128)(2,1)S(1)} %get-tuple-element.30), channel_id=1, source_target_pairs={{0,3},{1,2},{2,1},{3,0},{4,7},{5,6},{6,5},{7,4},{8,11},{9,10},{10,... | collective-permute-start | bytes 196616 | tf_op jit(solution)/shard_map/ppermute | solution.py:466
  7.6 2.5 %shard_map.120.store = bf16[3392,512]{1,0:T(8,128)(2,1)S(1)} custom-call(s32[1]{0:T(128)S(6)} %copy.13.counts, bf16[512,512]{1,0:T(8,128)(2,1)} %bitcast.5, bf16[64,448]{1,0:T(8,128)(2,1)} %conv_ref.3, bf16[128,512]{1,0:T(8,128)(2,1)} %down_hbm.1, bf16[128,128]{1,0:T(8,128)(2,1)} %head_hbm.1), custom_call_target="tpu_custom_call" | custom-call | flops 1500000000 | bytes 4500000 | tf_op jit(solution)/shard_map/pallas_call | solution.py:553
  10.1 0.0 collective-permute-done.2.got_yb
  10.1 1.3 %collective-permute-done.got_xy = bf16[784,128]{1,0:T(8,128)(2,1)S(1)} collective-permute-done((bf16[784,128]{1,0:T(8,128)(2,1)S(1)}, bf16[784,128]{1,0:T(8,128)(2,1)S(1)}, u32[]{:S(2)}, u32[]{:S(2)}) %collective-permute-start) | collective-permute-done | bytes 200736 | tf_op jit(solution)/shard_map/ppermute | solution.py:466
  11.4 0.1 collective-permute-start.4
  11.5 1.4 %collective-permute-done.4.got_xa = bf16[784,128]{1,0:T(8,128)(2,1)S(1)} collective-permute-done((bf16[784,128]{1,0:T(8,128)(2,1)S(1)}, bf16[784,128]{1,0:T(8,128)(2,1)S(1)}, u32[]{:S(2)}, u32[]{:S(2)}) %collective-permute-start.4) | collective-permute-done | bytes 200736 | tf_op jit(solution)/shard_map/ppermute | solution.py:466
  12.9 4.7 %shard_map.121 = (bf16[512,512]{1,0:T(8,128)(2,1)S(1)}, bf16[448,128]{1,0:T(8,128)(2,1)S(1)}, bf16[448,128]{1,0:T(8,128)(2,1)S(1)}, bf16[1536,128]{1,0:T(8,128)(2,1)S(1)}) custom-call(s32[8,6]{1,0:T(8,128)} %nb_hbm.3, s32[1,8]{1,0:T(1,128)} %cmap.1, bf16[512,128]{1,0:T(8,128)(2,1)} %bitcast.7, bf16[784,128]{1,0:T(8,128)(2,1)S(1)} %collective-permute-done.4.got_xa, ...), custom_call_target="tpu_custom_call" | custom-call | flops 6000000000 | bytes 18000000 | tf_op jit(solution)/shard_map/pallas_call | solution.py:553
  17.6 0.2 collective-permute-start.5
  17.8 1.2 %collective-permute-done.5 = bf16[448,128]{1,0:T(8,128)(2,1)S(1)} collective-permute-done((bf16[448,128]{1,0:T(8,128)(2,1)S(1)}, bf16[448,128]{1,0:T(8,128)(2,1)S(1)}, u32[]{:S(2)}, u32[]{:S(2)}) %collective-permute-start.5) | collective-permute-done | bytes 114720 | tf_op jit(solution)/shard_map/ppermute | solution.py:466
  19.0 1.3 %collective-permute-start.6 = (bf16[448,128]{1,0:T(8,128)(2,1)S(1)}, bf16[448,128]{1,0:T(8,128)(2,1)S(1)}, u32[]{:S(2)}, u32[]{:S(2)}) collective-permute-start(bf16[448,128]{1,0:T(8,128)(2,1)S(1)} %add_convert_fusion.4), channel_id=1, source_target_pairs={{0,3},{1,8},{2,11},{3,0},{4,13},{5,6},{6,5},{7,14},{8,1},{9,10},{1... | collective-permute-start | bytes 344072 | tf_op jit(solution)/shard_map/ppermute | solution.py:466
  20.4 1.4 %collective-permute-start.7 = (bf16[256,128]{1,0:T(8,128)(2,1)S(1)}, bf16[256,128]{1,0:T(8,128)(2,1)S(1)}, u32[]{:S(2)}, u32[]{:S(2)}) collective-permute-start(bf16[256,128]{1,0:T(8,128)(2,1)S(1)} %get-tuple-element.53), channel_id=1, source_target_pairs={{0,1},{1,0},{2,3},{3,2},{4,8},{5,9},{6,10},{7,11},{8,4},{9,5},{10,... | collective-permute-start | bytes 196616 | tf_op jit(solution)/shard_map/ppermute | solution.py:466
  21.7 1.4 %collective-permute-start.11 = (bf16[256,128]{1,0:T(8,128)(2,1)S(1)}, bf16[256,128]{1,0:T(8,128)(2,1)S(1)}, u32[]{:S(2)}, u32[]{:S(2)}) collective-permute-start(bf16[256,128]{1,0:T(8,128)(2,1)S(1)} %get-tuple-element.41), channel_id=1, source_target_pairs={{0,4},{1,5},{2,6},{3,7},{4,0},{5,1},{6,2},{7,3},{8,12},{9,13},{10,... | collective-permute-start | bytes 196616 | tf_op jit(solution)/shard_map/ppermute | solution.py:466
  23.1 1.1 %collective-permute-start.12 = (bf16[256,128]{1,0:T(8,128)(2,1)S(1)}, bf16[256,128]{1,0:T(8,128)(2,1)S(1)}, u32[]{:S(2)}, u32[]{:S(2)}) collective-permute-start(bf16[256,128]{1,0:T(8,128)(2,1)S(1)} %get-tuple-element.42), channel_id=1, source_target_pairs={{0,3},{1,2},{2,1},{3,0},{4,7},{5,6},{6,5},{7,4},{8,11},{9,10},{10,... | collective-permute-start | bytes 196616 | tf_op jit(solution)/shard_map/ppermute | solution.py:466
  24.3 2.0 %collective-permute-start.8 = (bf16[448,128]{1,0:T(8,128)(2,1)S(1)}, bf16[448,128]{1,0:T(8,128)(2,1)S(1)}, u32[]{:S(2)}, u32[]{:S(2)}) collective-permute-start(bf16[448,128]{1,0:T(8,128)(2,1)S(1)} %add_convert_fusion.3), channel_id=1, source_target_pairs={{0,9},{1,2},{2,1},{3,10},{4,7},{5,12},{6,15},{7,4},{8,11},{9,0},{1... | collective-permute-start | bytes 344072 | tf_op jit(solution)/shard_map/ppermute | solution.py:466
  26.3 2.1 %shard_map.122.moved_ref = bf16[2048,512]{1,0:T(8,128)(2,1)S(1)} custom-call(s32[8,6]{1,0:T(8,128)} %nb_hbm.3, bf16[512,512]{1,0:T(8,128)(2,1)S(1)} %get-tuple-element.37.hg_ref), custom_call_target="tpu_custom_call" | custom-call | flops 2500000000 | bytes 7500000 | tf_op jit(solution)/shard_map/pallas_call | solution.py:553
  28.3 0.4 collective-permute-done.8
  28.8 1.7 %collective-permute-start.13 = (bf16[448,128]{1,0:T(8,128)(2,1)S(1)}, bf16[448,128]{1,0:T(8,128)(2,1)S(1)}, u32[]{:S(2)}, u32[]{:S(2)}) collective-permute-start(bf16[448,128]{1,0:T(8,128)(2,1)S(1)} %add_convert_fusion.2), channel_id=1, source_target_pairs={{0,5},{1,16},{2,19},{3,6},{4,21},{5,0},{6,3},{7,22},{8,25},{9,12},... | collective-permute-start | bytes 344072 | tf_op jit(solution)/shard_map/ppermute | solution.py:466
  30.6 1.1 %shard_map.123.near_ref = f32[512,512]{1,0:T(8,128)S(1)} custom-call(bf16[512,512]{1,0:T(8,128)(2,1)S(1)} %get-tuple-element.37.hg_ref, bf16[2048,512]{1,0:T(8,128)(2,1)S(1)} %shard_map.122.moved_ref, bf16[64,448]{1,0:T(8,128)(2,1)S(1)} %copy-done), custom_call_target="tpu_custom_call" | custom-call | flops 1000000000 | bytes 3000000 | tf_op jit(solution)/shard_map/pallas_call | solution.py:553
  31.7 0.1 collective-permute-start.9
  31.8 1.3 %collective-permute-done.13 = bf16[448,128]{1,0:T(8,128)(2,1)S(1)} collective-permute-done((bf16[448,128]{1,0:T(8,128)(2,1)S(1)}, bf16[448,128]{1,0:T(8,128)(2,1)S(1)}, u32[]{:S(2)}, u32[]{:S(2)}) %collective-permute-start.13) | collective-permute-done | bytes 114720 | tf_op jit(solution)/shard_map/ppermute | solution.py:466
  33.1 0.0 copy-start.1
  33.2 3.5 %collective-permute-start.15 = (bf16[448,128]{1,0:T(8,128)(2,1)S(1)}, bf16[448,128]{1,0:T(8,128)(2,1)S(1)}, u32[]{:S(2)}, u32[]{:S(2)}) collective-permute-start(bf16[448,128]{1,0:T(8,128)(2,1)S(1)} %add_convert_fusion.1), channel_id=1, source_target_pairs={{0,17},{1,4},{2,7},{3,18},{4,1},{5,20},{6,23},{7,2},{8,13},{9,24},... | collective-permute-start | bytes 344072 | tf_op jit(solution)/shard_map/ppermute | solution.py:466
  36.7 1.0 %collective-permute-start.14 = (bf16[512,128]{1,0:T(8,128)(2,1)S(1)}, bf16[512,128]{1,0:T(8,128)(2,1)S(1)}, u32[]{:S(2)}, u32[]{:S(2)}) collective-permute-start(bf16[512,128]{1,0:T(8,128)(2,1)S(1)} %collective-permute-done.9.got_xy), channel_id=1, source_target_pairs={{0,1},{1,0},{2,3},{3,2},{4,5},{5,4},{6,7},{7,6},{8,9},{9,8},{10,11... | collective-permute-start | bytes 393224 | tf_op jit(solution)/shard_map/ppermute | solution.py:466
  37.7 1.8 %shard_map.125 = bf16[512,512]{1,0:T(8,128)(2,1)} custom-call(s32[1]{0:T(128)S(6)} %copy.13.counts, f32[512,512]{1,0:T(8,128)S(1)} %shard_map.123.near_ref, bf16[256,128]{1,0:T(8,128)(2,1)S(1)} %collective-permute-done.11.got_xa, bf16[256,128]{1,0:T(8,128)(2,1)S(1)} %collective-permute-done.7.got_xb, bf16[768,128]{1,0:T(8,128)(2,1)S(1)} %collective-permute-done.10.got_ya, ...), custom_call_target="tpu_custom_call" | custom-call | flops 1800000000 | bytes 5400000 | tf_op jit(solution)/shard_map/pallas_call | solution.py:553
  39.6 0.1 collective-permute-start.16
  39.7 1.2 %shard_map.124 = bf16[512,128]{1,0:T(8,128)(2,1)} custom-call(s32[1,8]{1,0:T(1,128)S(1)} %copy-done.1, bf16[1536,128]{1,0:T(8,128)(2,1)S(1)} %get-tuple-element.33.own, bf16[512,128]{1,0:T(8,128)(2,1)S(1)} %collective-permute-done.14.got_x, bf16[768,128]{1,0:T(8,128)(2,1)S(1)} %collective-permute-done.10.got_ya, ...), custom_call_target="tpu_custom_call" | custom-call | flops 1200000000 | bytes 3600000 | tf_op jit(solution)/shard_map/pallas_call | solution.py:553
  40.9 0.1 collective-permute-done.16.refs_1_
  41.0 1.0 %shard_map.126 = (f32[64,448]{1,0:T(8,128)}, f32[128,512]{1,0:T(8,128)}, f32[128,128]{1,0:T(8,128)}) custom-call(bf16[448,128]{1,0:T(8,128)(2,1)S(1)} %add_convert_fusion.refs_0_, bf16[448,128]{1,0:T(8,128)(2,1)S(1)} %collective-permute-done.16.refs_1_), custom_call_target="tpu_custom_call" | custom-call | flops 1000000000 | bytes 3000000 | tf_op jit(solution)/shard_map/pallas_call | solution.py:553
  (22 shorter events, 0.2 us)
Async XLA Ops:
  2.1 9.3 %collective-permute-start = (bf16[784,128]{1,0:T(8,128)(2,1)S(1)}, bf16[784,128]{1,0:T(8,128)(2,1)S(1)}, u32[]{:S(2)}, u32[]{:S(2)}) collective-permute-start(bf16[784,128]{1,0:T(8,128)(2,1)S(1)} %get-tuple-element.28), channel_id=1, source_target_pairs={{0,5},{1,4},{2,7},{3,6},{4,1},{5,0},{6,3},{7,2},{8,13},{9,12},{10,... | collective-permute-start | bytes 602120 | tf_op jit(solution)/shard_map/ppermute | solution.py:466
  4.6 6.8 %collective-permute-start.3 = (bf16[784,128]{1,0:T(8,128)(2,1)S(1)}, bf16[784,128]{1,0:T(8,128)(2,1)S(1)}, u32[]{:S(2)}, u32[]{:S(2)}) collective-permute-start(bf16[784,128]{1,0:T(8,128)(2,1)S(1)} %get-tuple-element.31), channel_id=1, source_target_pairs={{0,1},{1,0},{2,3},{3,2},{4,5},{5,4},{6,7},{7,6},{8,9},{9,8},{10,11... | collective-permute-start | bytes 602120 | tf_op jit(solution)/shard_map/ppermute | solution.py:466
  5.3 4.8 %collective-permute-start.1 = (bf16[256,128]{1,0:T(8,128)(2,1)S(1)}, bf16[256,128]{1,0:T(8,128)(2,1)S(1)}, u32[]{:S(2)}, u32[]{:S(2)}) collective-permute-start(bf16[256,128]{1,0:T(8,128)(2,1)S(1)} %get-tuple-element.29), channel_id=1, source_target_pairs={{0,1},{1,0},{2,3},{3,2},{4,8},{5,9},{6,10},{7,11},{8,4},{9,5},{10,... | collective-permute-start | bytes 196616 | tf_op jit(solution)/shard_map/ppermute | solution.py:466
  5.3 4.8 %collective-permute-start.2 = (bf16[256,128]{1,0:T(8,128)(2,1)S(1)}, bf16[256,128]{1,0:T(8,128)(2,1)S(1)}, u32[]{:S(2)}, u32[]{:S(2)}) collective-permute-start(bf16[256,128]{1,0:T(8,128)(2,1)S(1)} %get-tuple-element.30), channel_id=1, source_target_pairs={{0,3},{1,2},{2,1},{3,0},{4,7},{5,6},{6,5},{7,4},{8,11},{9,10},{10,... | collective-permute-start | bytes 196616 | tf_op jit(solution)/shard_map/ppermute | solution.py:466
  11.4 1.4 %collective-permute-start.4 = (bf16[784,128]{1,0:T(8,128)(2,1)S(1)}, bf16[784,128]{1,0:T(8,128)(2,1)S(1)}, u32[]{:S(2)}, u32[]{:S(2)}) collective-permute-start(bf16[784,128]{1,0:T(8,128)(2,1)S(1)} %collective-permute-done.got_xy), channel_id=1, source_target_pairs={{0,1},{1,0},{2,3},{3,2},{4,5},{5,4},{6,7},{7,6},{8,9},{9,8},{10,11... | collective-permute-start | bytes 602120 | tf_op jit(solution)/shard_map/ppermute | solution.py:466
  17.6 1.4 %collective-permute-start.5 = (bf16[448,128]{1,0:T(8,128)(2,1)S(1)}, bf16[448,128]{1,0:T(8,128)(2,1)S(1)}, u32[]{:S(2)}, u32[]{:S(2)}) collective-permute-start(bf16[448,128]{1,0:T(8,128)(2,1)S(1)} %get-tuple-element.36), channel_id=1, source_target_pairs={{0,1},{1,0},{2,3},{3,2},{4,5},{5,4},{6,7},{7,6},{8,9},{9,8},{10,11... | collective-permute-start | bytes 344072 | tf_op jit(solution)/shard_map/ppermute | solution.py:466
  19.0 5.2 %collective-permute-start.6 = (bf16[448,128]{1,0:T(8,128)(2,1)S(1)}, bf16[448,128]{1,0:T(8,128)(2,1)S(1)}, u32[]{:S(2)}, u32[]{:S(2)}) collective-permute-start(bf16[448,128]{1,0:T(8,128)(2,1)S(1)} %add_convert_fusion.4), channel_id=1, source_target_pairs={{0,3},{1,8},{2,11},{3,0},{4,13},{5,6},{6,5},{7,14},{8,1},{9,10},{1... | collective-permute-start | bytes 344072 | tf_op jit(solution)/shard_map/ppermute | solution.py:466
  20.4 5.9 %collective-permute-start.7 = (bf16[256,128]{1,0:T(8,128)(2,1)S(1)}, bf16[256,128]{1,0:T(8,128)(2,1)S(1)}, u32[]{:S(2)}, u32[]{:S(2)}) collective-permute-start(bf16[256,128]{1,0:T(8,128)(2,1)S(1)} %get-tuple-element.53), channel_id=1, source_target_pairs={{0,1},{1,0},{2,3},{3,2},{4,8},{5,9},{6,10},{7,11},{8,4},{9,5},{10,... | collective-permute-start | bytes 196616 | tf_op jit(solution)/shard_map/ppermute | solution.py:466
  21.7 7.0 %collective-permute-start.11 = (bf16[256,128]{1,0:T(8,128)(2,1)S(1)}, bf16[256,128]{1,0:T(8,128)(2,1)S(1)}, u32[]{:S(2)}, u32[]{:S(2)}) collective-permute-start(bf16[256,128]{1,0:T(8,128)(2,1)S(1)} %get-tuple-element.41), channel_id=1, source_target_pairs={{0,4},{1,5},{2,6},{3,7},{4,0},{5,1},{6,2},{7,3},{8,12},{9,13},{10,... | collective-permute-start | bytes 196616 | tf_op jit(solution)/shard_map/ppermute | solution.py:466
  23.1 5.7 %collective-permute-start.12 = (bf16[256,128]{1,0:T(8,128)(2,1)S(1)}, bf16[256,128]{1,0:T(8,128)(2,1)S(1)}, u32[]{:S(2)}, u32[]{:S(2)}) collective-permute-start(bf16[256,128]{1,0:T(8,128)(2,1)S(1)} %get-tuple-element.42), channel_id=1, source_target_pairs={{0,3},{1,2},{2,1},{3,0},{4,7},{5,6},{6,5},{7,4},{8,11},{9,10},{10,... | collective-permute-start | bytes 196616 | tf_op jit(solution)/shard_map/ppermute | solution.py:466
  24.3 4.5 %collective-permute-start.8 = (bf16[448,128]{1,0:T(8,128)(2,1)S(1)}, bf16[448,128]{1,0:T(8,128)(2,1)S(1)}, u32[]{:S(2)}, u32[]{:S(2)}) collective-permute-start(bf16[448,128]{1,0:T(8,128)(2,1)S(1)} %add_convert_fusion.3), channel_id=1, source_target_pairs={{0,9},{1,2},{2,1},{3,10},{4,7},{5,12},{6,15},{7,4},{8,11},{9,0},{1... | collective-permute-start | bytes 344072 | tf_op jit(solution)/shard_map/ppermute | solution.py:466
  26.3 4.3 %copy-start = (bf16[64,448]{1,0:T(8,128)(2,1)S(1)}, bf16[64,448]{1,0:T(8,128)(2,1)}, u32[]{:S(2)}) copy-start(bf16[64,448]{1,0:T(8,128)(2,1)} %conv_ref.3) | copy-start | bytes 172036
  26.3 2.5 %collective-permute-start.10 = (bf16[768,128]{1,0:T(8,128)(2,1)S(1)}, bf16[768,128]{1,0:T(8,128)(2,1)S(1)}, u32[]{:S(2)}, u32[]{:S(2)}) collective-permute-start(bf16[768,128]{1,0:T(8,128)(2,1)S(1)} %slice.17), channel_id=1, source_target_pairs={{0,1},{1,0},{2,3},{3,2},{4,5},{5,4},{6,7},{7,6},{8,9},{9,8},{10,11... | collective-permute-start | bytes 589832 | tf_op jit(solution)/shard_map/ppermute | solution.py:466
  28.8 4.3 %collective-permute-start.13 = (bf16[448,128]{1,0:T(8,128)(2,1)S(1)}, bf16[448,128]{1,0:T(8,128)(2,1)S(1)}, u32[]{:S(2)}, u32[]{:S(2)}) collective-permute-start(bf16[448,128]{1,0:T(8,128)(2,1)S(1)} %add_convert_fusion.2), channel_id=1, source_target_pairs={{0,5},{1,16},{2,19},{3,6},{4,21},{5,0},{6,3},{7,22},{8,25},{9,12},... | collective-permute-start | bytes 344072 | tf_op jit(solution)/shard_map/ppermute | solution.py:466
  31.7 5.0 %collective-permute-start.9 = (bf16[512,128]{1,0:T(8,128)(2,1)S(1)}, bf16[512,128]{1,0:T(8,128)(2,1)S(1)}, u32[]{:S(2)}, u32[]{:S(2)}) collective-permute-start(bf16[512,128]{1,0:T(8,128)(2,1)S(1)} %slice.15), channel_id=1, source_target_pairs={{0,5},{1,4},{2,7},{3,6},{4,1},{5,0},{6,3},{7,2},{8,13},{9,12},{10,... | collective-permute-start | bytes 393224 | tf_op jit(solution)/shard_map/ppermute | solution.py:466
  33.1 6.5 %copy-start.1 = (s32[1,8]{1,0:T(1,128)S(1)}, s32[1,8]{1,0:T(1,128)}, u32[]{:S(2)}) copy-start(s32[1,8]{1,0:T(1,128)} %cmap.1) | copy-start | bytes 100
  33.2 6.4 %collective-permute-start.15 = (bf16[448,128]{1,0:T(8,128)(2,1)S(1)}, bf16[448,128]{1,0:T(8,128)(2,1)S(1)}, u32[]{:S(2)}, u32[]{:S(2)}) collective-permute-start(bf16[448,128]{1,0:T(8,128)(2,1)S(1)} %add_convert_fusion.1), channel_id=1, source_target_pairs={{0,17},{1,4},{2,7},{3,18},{4,1},{5,20},{6,23},{7,2},{8,13},{9,24},... | collective-permute-start | bytes 344072 | tf_op jit(solution)/shard_map/ppermute | solution.py:466
  36.7 2.9 %collective-permute-start.14 = (bf16[512,128]{1,0:T(8,128)(2,1)S(1)}, bf16[512,128]{1,0:T(8,128)(2,1)S(1)}, u32[]{:S(2)}, u32[]{:S(2)}) collective-permute-start(bf16[512,128]{1,0:T(8,128)(2,1)S(1)} %collective-permute-done.9.got_xy), channel_id=1, source_target_pairs={{0,1},{1,0},{2,3},{3,2},{4,5},{5,4},{6,7},{7,6},{8,9},{9,8},{10,11... | collective-permute-start | bytes 393224 | tf_op jit(solution)/shard_map/ppermute | solution.py:466
  39.6 1.4 %collective-permute-start.16 = (bf16[448,128]{1,0:T(8,128)(2,1)S(1)}, bf16[448,128]{1,0:T(8,128)(2,1)S(1)}, u32[]{:S(2)}, u32[]{:S(2)}) collective-permute-start(bf16[448,128]{1,0:T(8,128)(2,1)S(1)} %add_convert_fusion.refs_0_), channel_id=1, source_target_pairs={{0,1},{1,0},{2,3},{3,2},{4,5},{5,4},{6,7},{7,6},{8,9},{9,8},{10,11... | collective-permute-start | bytes 344072 | tf_op jit(solution)/shard_map/ppermute | solution.py:466

commit v6 on v5

--- a/solution.py
+++ b/solution.py
@@ -299,10 +299,10 @@
     grad = routed[0:SLOTS].reshape(SLOTS * C, 128)
     head_back = head.astype(F32).T.astype(BF)
     oct_grad = (dot(head_back, grad, NT) * oct_slope).astype(BF)
-    sums_ref[768:896, :] = dot(oct_act, grad).T
+    sums_ref[736:864, :] = dot(oct_act, grad).T
     down_sum = dot(oct_grad, act2[...], NT)
     for k in range(4):
-        sums_ref[256 + k * 128 : 256 + (k + 1) * 128, :] = down_sum[:, k * 128 : (k + 1) * 128]
+        sums_ref[224 + k * 128 : 224 + (k + 1) * 128, :] = down_sum[:, k * 128 : (k + 1) * 128]
     for pair in range(SLOTS // 2):
         patch = dot(store[DOWN_BACK : DOWN_BACK + 512, 0:128], oct_grad[:, pair * 128 : (pair + 1) * 128])
         for side in range(2):
@@ -321,10 +321,9 @@
     conv_sum = dot(hg_row[...], taps[...], NT)
     for k in range(3):
         sums_ref[k * C : (k + 1) * C, :] = conv_sum[:, k * 128 : (k + 1) * 128]
-    sums_ref[3 * C : 4 * C, 0:C] = conv_sum[:, 384:448]
-    sums_ref[3 * C : 4 * C, C:128] = jnp.zeros((C, C), F32)
-
-    first, second = sums_ref[0:448, :].astype(BF), sums_ref[448:896, :].astype(BF)
+    sums_ref[192:224, :] = jnp.concatenate([conv_sum[0:32, 384:448], conv_sum[32:64, 384:448]], 1)
+
+    first, second = sums_ref[0:432, :].astype(BF), sums_ref[432:864, :].astype(BF)
     even = parity() == 0
     mine_ref[...] = jnp.where(even, first, second)
     other_ref[...] = jnp.where(even, second, first)
@@ -446,10 +445,12 @@
     )
     for k in range(3):
         conv_out[:, k * 128 : (k + 1) * 128] = conv_in[k * C : (k + 1) * C, :].astype(F32) * scale
-    conv_out[:, 384:448] = conv_in[3 * C : 4 * C, 0:C].astype(F32) * scale
-    down = jnp.concatenate([conv_in[256 + k * 128 : 384 + k * 128, :] for k in range(4)], 1)
+    last = conv_in[192:224, :].astype(F32) * scale
+    conv_out[0:32, 384:448] = last[:, 0:64]
+    conv_out[32:64, 384:448] = last[:, 64:128]
+    down = jnp.concatenate([conv_in[224 + k * 128 : 352 + k * 128, :] for k in range(4)], 1)
     down_out[...] = dot(down, regroup()) * scale
-    head_out[...] = conv_in[768:896, :].astype(F32) * scale
+    head_out[...] = conv_in[736:864, :].astype(F32) * scale
 
 
 def route(there):
@@ -596,14 +597,14 @@
     got_xa = beside_core(tie(got_xy, got_xb, got_yb, got_ya, store))
     hg, mine, other, send = call(
         main_kernel,
-        [((512, 512), BF), ((448, 128), BF), ((448, 128), BF), ((SEND, 128), BF)],
+        [((512, 512), BF), ((432, 128), BF), ((432, 128), BF), ((SEND, 128), BF)],
         (neighbours, coarse_map, lat, got_xa, got_xb, got_ya, got_yb, got_xy, store),
         "hhh",
         [
             pltpu.SMEM((SLOTS, 6), jnp.int32),
             pltpu.SMEM((1, 8), jnp.int32),
             pltpu.SemaphoreType.DMA((3,)),
-            pltpu.VMEM((896, 128), F32),
+            pltpu.VMEM((864, 128), F32),
             pltpu.VMEM((512, 128), BF),
             pltpu.VMEM((4, 17, C, 256), BF),
             pltpu.VMEM((448, SLOTS * 512), BF),

time: 42.2 us -> 42.4 us (level)
  no operation moved by 1% of the time
where the time goes in v6:
time: 42.4 us; the launch traced here: 42.2 us
  starting transfers between devices  19 us (45%)
  Pallas kernels  16 us (38%)
  waiting for transfers between devices  5.52 us (13%)
  between operations  1.45 us (3%)
    ppermute x17, starting transfers between devices, send_to(): return lax.ppermute(value, ('gx', 'gy'), route(there))  19 us
    pallas_call x8, Pallas kernels, call(): pl.pallas_call(kernel, out_shape=[pltpu.VMEM(shape, kind) if at < keep el...  16 us
    ppermute x17, waiting for transfers between devices, send_to(): return lax.ppermute(value, ('gx', 'gy'), route(there))  5.52 us
  transfers between devices with their start and end apart: 17, of which 6 were waited for; matrix products, arithmetic and copies ran while one was open for 0% of the time, Pallas kernels for 21%

profile of v6, /device:TPU:0, one launch (start us, length us, event | category | flops | bytes accessed | tf_op | source)
XLA Modules:
  0.0 42.2 jit_solution(13646624949255101298)
XLA Ops:
  0.6 1.5 %shard_map.119 = (bf16[784,128]{1,0:T(8,128)(2,1)S(1)}, bf16[256,128]{1,0:T(8,128)(2,1)S(1)}, bf16[784,128]{1,0:T(8,128)(2,1)S(1)}, bf16[256,128]{1,0:T(8,128)(2,1)S(1)}) custom-call(s32[1,8]{1,0:T(1,128)} %cmap.1, bf16[512,512]{1,0:T(8,128)(2,1)} %bitcast.4, bf16[512,128]{1,0:T(8,128)(2,1)} %bitcast.6), custom_call_target="tpu_custom_call" | custom-call | flops 1500000000 | bytes 4500000 | tf_op jit(solution)/shard_map/pallas_call | solution.py:554
  2.1 2.5 %collective-permute-start = (bf16[784,128]{1,0:T(8,128)(2,1)S(1)}, bf16[784,128]{1,0:T(8,128)(2,1)S(1)}, u32[]{:S(2)}, u32[]{:S(2)}) collective-permute-start(bf16[784,128]{1,0:T(8,128)(2,1)S(1)} %get-tuple-element.28), channel_id=1, source_target_pairs={{0,5},{1,4},{2,7},{3,6},{4,1},{5,0},{6,3},{7,2},{8,13},{9,12},{10,... | collective-permute-start | bytes 602120 | tf_op jit(solution)/shard_map/ppermute | solution.py:467
  4.6 0.7 %collective-permute-start.3 = (bf16[784,128]{1,0:T(8,128)(2,1)S(1)}, bf16[784,128]{1,0:T(8,128)(2,1)S(1)}, u32[]{:S(2)}, u32[]{:S(2)}) collective-permute-start(bf16[784,128]{1,0:T(8,128)(2,1)S(1)} %get-tuple-element.31), channel_id=1, source_target_pairs={{0,1},{1,0},{2,3},{3,2},{4,5},{5,4},{6,7},{7,6},{8,9},{9,8},{10,11... | collective-permute-start | bytes 602120 | tf_op jit(solution)/shard_map/ppermute | solution.py:467
  5.3 0.0 collective-permute-start.1
  5.3 1.6 %collective-permute-start.2 = (bf16[256,128]{1,0:T(8,128)(2,1)S(1)}, bf16[256,128]{1,0:T(8,128)(2,1)S(1)}, u32[]{:S(2)}, u32[]{:S(2)}) collective-permute-start(bf16[256,128]{1,0:T(8,128)(2,1)S(1)} %get-tuple-element.30), channel_id=1, source_target_pairs={{0,3},{1,2},{2,1},{3,0},{4,7},{5,6},{6,5},{7,4},{8,11},{9,10},{10,... | collective-permute-start | bytes 196616 | tf_op jit(solution)/shard_map/ppermute | solution.py:467
  7.6 2.5 %shard_map.120.store = bf16[3392,512]{1,0:T(8,128)(2,1)S(1)} custom-call(s32[1]{0:T(128)S(6)} %copy.13.counts, bf16[512,512]{1,0:T(8,128)(2,1)} %bitcast.5, bf16[64,448]{1,0:T(8,128)(2,1)} %conv_ref.3, bf16[128,512]{1,0:T(8,128)(2,1)} %down_hbm.1, bf16[128,128]{1,0:T(8,128)(2,1)} %head_hbm.1), custom_call_target="tpu_custom_call" | custom-call | flops 1500000000 | bytes 4500000 | tf_op jit(solution)/shard_map/pallas_call | solution.py:554
  10.1 0.0 collective-permute-done.2.got_yb
  10.1 1.3 %collective-permute-done.got_xy = bf16[784,128]{1,0:T(8,128)(2,1)S(1)} collective-permute-done((bf16[784,128]{1,0:T(8,128)(2,1)S(1)}, bf16[784,128]{1,0:T(8,128)(2,1)S(1)}, u32[]{:S(2)}, u32[]{:S(2)}) %collective-permute-start) | collective-permute-done | bytes 200736 | tf_op jit(solution)/shard_map/ppermute | solution.py:467
  11.4 0.1 collective-permute-start.4
  11.5 1.4 %collective-permute-done.4.got_xa = bf16[784,128]{1,0:T(8,128)(2,1)S(1)} collective-permute-done((bf16[784,128]{1,0:T(8,128)(2,1)S(1)}, bf16[784,128]{1,0:T(8,128)(2,1)S(1)}, u32[]{:S(2)}, u32[]{:S(2)}) %collective-permute-start.4) | collective-permute-done | bytes 200736 | tf_op jit(solution)/shard_map/ppermute | solution.py:467
  12.9 4.7 %shard_map.121 = (bf16[512,512]{1,0:T(8,128)(2,1)S(1)}, bf16[432,128]{1,0:T(8,128)(2,1)S(1)}, bf16[432,128]{1,0:T(8,128)(2,1)S(1)}, bf16[1536,128]{1,0:T(8,128)(2,1)S(1)}) custom-call(s32[8,6]{1,0:T(8,128)} %nb_hbm.3, s32[1,8]{1,0:T(1,128)} %cmap.1, bf16[512,128]{1,0:T(8,128)(2,1)} %bitcast.7, bf16[784,128]{1,0:T(8,128)(2,1)S(1)} %collective-permute-done.4.got_xa, ...), custom_call_target="tpu_custom_call" | custom-call | flops 6000000000 | bytes 18000000 | tf_op jit(solution)/shard_map/pallas_call | solution.py:554
  17.6 0.2 collective-permute-start.5
  17.8 1.2 %collective-permute-done.5 = bf16[432,128]{1,0:T(8,128)(2,1)S(1)} collective-permute-done((bf16[432,128]{1,0:T(8,128)(2,1)S(1)}, bf16[432,128]{1,0:T(8,128)(2,1)S(1)}, u32[]{:S(2)}, u32[]{:S(2)}) %collective-permute-start.5) | collective-permute-done | bytes 110624 | tf_op jit(solution)/shard_map/ppermute | solution.py:467
  19.0 1.3 %collective-permute-start.6 = (bf16[432,128]{1,0:T(8,128)(2,1)S(1)}, bf16[432,128]{1,0:T(8,128)(2,1)S(1)}, u32[]{:S(2)}, u32[]{:S(2)}) collective-permute-start(bf16[432,128]{1,0:T(8,128)(2,1)S(1)} %add_convert_fusion.4), channel_id=1, source_target_pairs={{0,3},{1,8},{2,11},{3,0},{4,13},{5,6},{6,5},{7,14},{8,1},{9,10},{1... | collective-permute-start | bytes 331784 | tf_op jit(solution)/shard_map/ppermute | solution.py:467
  20.4 1.4 %collective-permute-start.7 = (bf16[256,128]{1,0:T(8,128)(2,1)S(1)}, bf16[256,128]{1,0:T(8,128)(2,1)S(1)}, u32[]{:S(2)}, u32[]{:S(2)}) collective-permute-start(bf16[256,128]{1,0:T(8,128)(2,1)S(1)} %get-tuple-element.53), channel_id=1, source_target_pairs={{0,1},{1,0},{2,3},{3,2},{4,8},{5,9},{6,10},{7,11},{8,4},{9,5},{10,... | collective-permute-start | bytes 196616 | tf_op jit(solution)/shard_map/ppermute | solution.py:467
  21.7 1.4 %collective-permute-start.11 = (bf16[256,128]{1,0:T(8,128)(2,1)S(1)}, bf16[256,128]{1,0:T(8,128)(2,1)S(1)}, u32[]{:S(2)}, u32[]{:S(2)}) collective-permute-start(bf16[256,128]{1,0:T(8,128)(2,1)S(1)} %get-tuple-element.41), channel_id=1, source_target_pairs={{0,4},{1,5},{2,6},{3,7},{4,0},{5,1},{6,2},{7,3},{8,12},{9,13},{10,... | collective-permute-start | bytes 196616 | tf_op jit(solution)/shard_map/ppermute | solution.py:467
  23.1 1.1 %collective-permute-start.12 = (bf16[256,128]{1,0:T(8,128)(2,1)S(1)}, bf16[256,128]{1,0:T(8,128)(2,1)S(1)}, u32[]{:S(2)}, u32[]{:S(2)}) collective-permute-start(bf16[256,128]{1,0:T(8,128)(2,1)S(1)} %get-tuple-element.42), channel_id=1, source_target_pairs={{0,3},{1,2},{2,1},{3,0},{4,7},{5,6},{6,5},{7,4},{8,11},{9,10},{10,... | collective-permute-start | bytes 196616 | tf_op jit(solution)/shard_map/ppermute | solution.py:467
  24.3 2.0 %collective-permute-start.8 = (bf16[432,128]{1,0:T(8,128)(2,1)S(1)}, bf16[432,128]{1,0:T(8,128)(2,1)S(1)}, u32[]{:S(2)}, u32[]{:S(2)}) collective-permute-start(bf16[432,128]{1,0:T(8,128)(2,1)S(1)} %add_convert_fusion.3), channel_id=1, source_target_pairs={{0,9},{1,2},{2,1},{3,10},{4,7},{5,12},{6,15},{7,4},{8,11},{9,0},{1... | collective-permute-start | bytes 331784 | tf_op jit(solution)/shard_map/ppermute | solution.py:467
  26.3 2.1 %shard_map.122.moved_ref = bf16[2048,512]{1,0:T(8,128)(2,1)S(1)} custom-call(s32[8,6]{1,0:T(8,128)} %nb_hbm.3, bf16[512,512]{1,0:T(8,128)(2,1)S(1)} %get-tuple-element.37.hg_ref), custom_call_target="tpu_custom_call" | custom-call | flops 2500000000 | bytes 7500000 | tf_op jit(solution)/shard_map/pallas_call | solution.py:554
  28.3 0.4 collective-permute-done.8
  28.8 1.8 %collective-permute-start.13 = (bf16[432,128]{1,0:T(8,128)(2,1)S(1)}, bf16[432,128]{1,0:T(8,128)(2,1)S(1)}, u32[]{:S(2)}, u32[]{:S(2)}) collective-permute-start(bf16[432,128]{1,0:T(8,128)(2,1)S(1)} %add_convert_fusion.2), channel_id=1, source_target_pairs={{0,5},{1,16},{2,19},{3,6},{4,21},{5,0},{6,3},{7,22},{8,25},{9,12},... | collective-permute-start | bytes 331784 | tf_op jit(solution)/shard_map/ppermute | solution.py:467
  30.6 1.1 %shard_map.123.near_ref = f32[512,512]{1,0:T(8,128)S(1)} custom-call(bf16[512,512]{1,0:T(8,128)(2,1)S(1)} %get-tuple-element.37.hg_ref, bf16[2048,512]{1,0:T(8,128)(2,1)S(1)} %shard_map.122.moved_ref, bf16[64,448]{1,0:T(8,128)(2,1)S(1)} %copy-done), custom_call_target="tpu_custom_call" | custom-call | flops 1000000000 | bytes 3000000 | tf_op jit(solution)/shard_map/pallas_call | solution.py:554
  31.7 0.1 collective-permute-start.9
  31.8 1.2 %collective-permute-done.13 = bf16[432,128]{1,0:T(8,128)(2,1)S(1)} collective-permute-done((bf16[432,128]{1,0:T(8,128)(2,1)S(1)}, bf16[432,128]{1,0:T(8,128)(2,1)S(1)}, u32[]{:S(2)}, u32[]{:S(2)}) %collective-permute-start.13) | collective-permute-done | bytes 110624 | tf_op jit(solution)/shard_map/ppermute | solution.py:467
  33.0 0.0 copy-start.1
  33.1 3.5 %collective-permute-start.15 = (bf16[432,128]{1,0:T(8,128)(2,1)S(1)}, bf16[432,128]{1,0:T(8,128)(2,1)S(1)}, u32[]{:S(2)}, u32[]{:S(2)}) collective-permute-start(bf16[432,128]{1,0:T(8,128)(2,1)S(1)} %add_convert_fusion.1), channel_id=1, source_target_pairs={{0,17},{1,4},{2,7},{3,18},{4,1},{5,20},{6,23},{7,2},{8,13},{9,24},... | collective-permute-start | bytes 331784 | tf_op jit(solution)/shard_map/ppermute | solution.py:467
  36.5 1.4 %collective-permute-start.14 = (bf16[512,128]{1,0:T(8,128)(2,1)S(1)}, bf16[512,128]{1,0:T(8,128)(2,1)S(1)}, u32[]{:S(2)}, u32[]{:S(2)}) collective-permute-start(bf16[512,128]{1,0:T(8,128)(2,1)S(1)} %collective-permute-done.9.got_xy), channel_id=1, source_target_pairs={{0,1},{1,0},{2,3},{3,2},{4,5},{5,4},{6,7},{7,6},{8,9},{9,8},{10,11... | collective-permute-start | bytes 393224 | tf_op jit(solution)/shard_map/ppermute | solution.py:467
  37.9 1.9 %shard_map.125 = bf16[512,512]{1,0:T(8,128)(2,1)} custom-call(s32[1]{0:T(128)S(6)} %copy.13.counts, f32[512,512]{1,0:T(8,128)S(1)} %shard_map.123.near_ref, bf16[256,128]{1,0:T(8,128)(2,1)S(1)} %collective-permute-done.11.got_xa, bf16[256,128]{1,0:T(8,128)(2,1)S(1)} %collective-permute-done.7.got_xb, bf16[768,128]{1,0:T(8,128)(2,1)S(1)} %collective-permute-done.10.got_ya, ...), custom_call_target="tpu_custom_call" | custom-call | flops 1800000000 | bytes 5400000 | tf_op jit(solution)/shard_map/pallas_call | solution.py:554
  39.8 0.1 collective-permute-start.16
  39.9 1.2 %shard_map.124 = bf16[512,128]{1,0:T(8,128)(2,1)} custom-call(s32[1,8]{1,0:T(1,128)S(1)} %copy-done.1, bf16[1536,128]{1,0:T(8,128)(2,1)S(1)} %get-tuple-element.33.own, bf16[512,128]{1,0:T(8,128)(2,1)S(1)} %collective-permute-done.14.got_x, bf16[768,128]{1,0:T(8,128)(2,1)S(1)} %collective-permute-done.10.got_ya, ...), custom_call_target="tpu_custom_call" | custom-call | flops 1200000000 | bytes 3600000 | tf_op jit(solution)/shard_map/pallas_call | solution.py:554
  41.2 0.1 collective-permute-done.16.refs_1_
  41.2 1.0 %shard_map.126 = (f32[64,448]{1,0:T(8,128)}, f32[128,512]{1,0:T(8,128)}, f32[128,128]{1,0:T(8,128)}) custom-call(bf16[432,128]{1,0:T(8,128)(2,1)S(1)} %add_convert_fusion.refs_0_, bf16[432,128]{1,0:T(8,128)(2,1)S(1)} %collective-permute-done.16.refs_1_), custom_call_target="tpu_custom_call" | custom-call | flops 1000000000 | bytes 3000000 | tf_op jit(solution)/shard_map/pallas_call | solution.py:554
  (22 shorter events, 0.2 us)
Async XLA Ops:
  2.1 9.3 %collective-permute-start = (bf16[784,128]{1,0:T(8,128)(2,1)S(1)}, bf16[784,128]{1,0:T(8,128)(2,1)S(1)}, u32[]{:S(2)}, u32[]{:S(2)}) collective-permute-start(bf16[784,128]{1,0:T(8,128)(2,1)S(1)} %get-tuple-element.28), channel_id=1, source_target_pairs={{0,5},{1,4},{2,7},{3,6},{4,1},{5,0},{6,3},{7,2},{8,13},{9,12},{10,... | collective-permute-start | bytes 602120 | tf_op jit(solution)/shard_map/ppermute | solution.py:467
  4.6 6.8 %collective-permute-start.3 = (bf16[784,128]{1,0:T(8,128)(2,1)S(1)}, bf16[784,128]{1,0:T(8,128)(2,1)S(1)}, u32[]{:S(2)}, u32[]{:S(2)}) collective-permute-start(bf16[784,128]{1,0:T(8,128)(2,1)S(1)} %get-tuple-element.31), channel_id=1, source_target_pairs={{0,1},{1,0},{2,3},{3,2},{4,5},{5,4},{6,7},{7,6},{8,9},{9,8},{10,11... | collective-permute-start | bytes 602120 | tf_op jit(solution)/shard_map/ppermute | solution.py:467
  5.3 4.8 %collective-permute-start.1 = (bf16[256,128]{1,0:T(8,128)(2,1)S(1)}, bf16[256,128]{1,0:T(8,128)(2,1)S(1)}, u32[]{:S(2)}, u32[]{:S(2)}) collective-permute-start(bf16[256,128]{1,0:T(8,128)(2,1)S(1)} %get-tuple-element.29), channel_id=1, source_target_pairs={{0,1},{1,0},{2,3},{3,2},{4,8},{5,9},{6,10},{7,11},{8,4},{9,5},{10,... | collective-permute-start | bytes 196616 | tf_op jit(solution)/shard_map/ppermute | solution.py:467
  5.3 4.8 %collective-permute-start.2 = (bf16[256,128]{1,0:T(8,128)(2,1)S(1)}, bf16[256,128]{1,0:T(8,128)(2,1)S(1)}, u32[]{:S(2)}, u32[]{:S(2)}) collective-permute-start(bf16[256,128]{1,0:T(8,128)(2,1)S(1)} %get-tuple-element.30), channel_id=1, source_target_pairs={{0,3},{1,2},{2,1},{3,0},{4,7},{5,6},{6,5},{7,4},{8,11},{9,10},{10,... | collective-permute-start | bytes 196616 | tf_op jit(solution)/shard_map/ppermute | solution.py:467
  11.4 1.4 %collective-permute-start.4 = (bf16[784,128]{1,0:T(8,128)(2,1)S(1)}, bf16[784,128]{1,0:T(8,128)(2,1)S(1)}, u32[]{:S(2)}, u32[]{:S(2)}) collective-permute-start(bf16[784,128]{1,0:T(8,128)(2,1)S(1)} %collective-permute-done.got_xy), channel_id=1, source_target_pairs={{0,1},{1,0},{2,3},{3,2},{4,5},{5,4},{6,7},{7,6},{8,9},{9,8},{10,11... | collective-permute-start | bytes 602120 | tf_op jit(solution)/shard_map/ppermute | solution.py:467
  17.6 1.4 %collective-permute-start.5 = (bf16[432,128]{1,0:T(8,128)(2,1)S(1)}, bf16[432,128]{1,0:T(8,128)(2,1)S(1)}, u32[]{:S(2)}, u32[]{:S(2)}) collective-permute-start(bf16[432,128]{1,0:T(8,128)(2,1)S(1)} %get-tuple-element.36), channel_id=1, source_target_pairs={{0,1},{1,0},{2,3},{3,2},{4,5},{5,4},{6,7},{7,6},{8,9},{9,8},{10,11... | collective-permute-start | bytes 331784 | tf_op jit(solution)/shard_map/ppermute | solution.py:467
  19.0 5.2 %collective-permute-start.6 = (bf16[432,128]{1,0:T(8,128)(2,1)S(1)}, bf16[432,128]{1,0:T(8,128)(2,1)S(1)}, u32[]{:S(2)}, u32[]{:S(2)}) collective-permute-start(bf16[432,128]{1,0:T(8,128)(2,1)S(1)} %add_convert_fusion.4), channel_id=1, source_target_pairs={{0,3},{1,8},{2,11},{3,0},{4,13},{5,6},{6,5},{7,14},{8,1},{9,10},{1... | collective-permute-start | bytes 331784 | tf_op jit(solution)/shard_map/ppermute | solution.py:467
  20.4 5.9 %collective-permute-start.7 = (bf16[256,128]{1,0:T(8,128)(2,1)S(1)}, bf16[256,128]{1,0:T(8,128)(2,1)S(1)}, u32[]{:S(2)}, u32[]{:S(2)}) collective-permute-start(bf16[256,128]{1,0:T(8,128)(2,1)S(1)} %get-tuple-element.53), channel_id=1, source_target_pairs={{0,1},{1,0},{2,3},{3,2},{4,8},{5,9},{6,10},{7,11},{8,4},{9,5},{10,... | collective-permute-start | bytes 196616 | tf_op jit(solution)/shard_map/ppermute | solution.py:467
  21.7 7.0 %collective-permute-start.11 = (bf16[256,128]{1,0:T(8,128)(2,1)S(1)}, bf16[256,128]{1,0:T(8,128)(2,1)S(1)}, u32[]{:S(2)}, u32[]{:S(2)}) collective-permute-start(bf16[256,128]{1,0:T(8,128)(2,1)S(1)} %get-tuple-element.41), channel_id=1, source_target_pairs={{0,4},{1,5},{2,6},{3,7},{4,0},{5,1},{6,2},{7,3},{8,12},{9,13},{10,... | collective-permute-start | bytes 196616 | tf_op jit(solution)/shard_map/ppermute | solution.py:467
  23.1 5.6 %collective-permute-start.12 = (bf16[256,128]{1,0:T(8,128)(2,1)S(1)}, bf16[256,128]{1,0:T(8,128)(2,1)S(1)}, u32[]{:S(2)}, u32[]{:S(2)}) collective-permute-start(bf16[256,128]{1,0:T(8,128)(2,1)S(1)} %get-tuple-element.42), channel_id=1, source_target_pairs={{0,3},{1,2},{2,1},{3,0},{4,7},{5,6},{6,5},{7,4},{8,11},{9,10},{10,... | collective-permute-start | bytes 196616 | tf_op jit(solution)/shard_map/ppermute | solution.py:467
  24.3 4.4 %collective-permute-start.8 = (bf16[432,128]{1,0:T(8,128)(2,1)S(1)}, bf16[432,128]{1,0:T(8,128)(2,1)S(1)}, u32[]{:S(2)}, u32[]{:S(2)}) collective-permute-start(bf16[432,128]{1,0:T(8,128)(2,1)S(1)} %add_convert_fusion.3), channel_id=1, source_target_pairs={{0,9},{1,2},{2,1},{3,10},{4,7},{5,12},{6,15},{7,4},{8,11},{9,0},{1... | collective-permute-start | bytes 331784 | tf_op jit(solution)/shard_map/ppermute | solution.py:467
  26.3 4.3 %copy-start = (bf16[64,448]{1,0:T(8,128)(2,1)S(1)}, bf16[64,448]{1,0:T(8,128)(2,1)}, u32[]{:S(2)}) copy-start(bf16[64,448]{1,0:T(8,128)(2,1)} %conv_ref.3) | copy-start | bytes 172036
  26.3 2.5 %collective-permute-start.10 = (bf16[768,128]{1,0:T(8,128)(2,1)S(1)}, bf16[768,128]{1,0:T(8,128)(2,1)S(1)}, u32[]{:S(2)}, u32[]{:S(2)}) collective-permute-start(bf16[768,128]{1,0:T(8,128)(2,1)S(1)} %slice.17), channel_id=1, source_target_pairs={{0,1},{1,0},{2,3},{3,2},{4,5},{5,4},{6,7},{7,6},{8,9},{9,8},{10,11... | collective-permute-start | bytes 589832 | tf_op jit(solution)/shard_map/ppermute | solution.py:467
  28.8 4.2 %collective-permute-start.13 = (bf16[432,128]{1,0:T(8,128)(2,1)S(1)}, bf16[432,128]{1,0:T(8,128)(2,1)S(1)}, u32[]{:S(2)}, u32[]{:S(2)}) collective-permute-start(bf16[432,128]{1,0:T(8,128)(2,1)S(1)} %add_convert_fusion.2), channel_id=1, source_target_pairs={{0,5},{1,16},{2,19},{3,6},{4,21},{5,0},{6,3},{7,22},{8,25},{9,12},... | collective-permute-start | bytes 331784 | tf_op jit(solution)/shard_map/ppermute | solution.py:467
  31.7 4.8 %collective-permute-start.9 = (bf16[512,128]{1,0:T(8,128)(2,1)S(1)}, bf16[512,128]{1,0:T(8,128)(2,1)S(1)}, u32[]{:S(2)}, u32[]{:S(2)}) collective-permute-start(bf16[512,128]{1,0:T(8,128)(2,1)S(1)} %slice.15), channel_id=1, source_target_pairs={{0,5},{1,4},{2,7},{3,6},{4,1},{5,0},{6,3},{7,2},{8,13},{9,12},{10,... | collective-permute-start | bytes 393224 | tf_op jit(solution)/shard_map/ppermute | solution.py:467
  33.0 6.9 %copy-start.1 = (s32[1,8]{1,0:T(1,128)S(1)}, s32[1,8]{1,0:T(1,128)}, u32[]{:S(2)}) copy-start(s32[1,8]{1,0:T(1,128)} %cmap.1) | copy-start | bytes 100
  33.1 6.7 %collective-permute-start.15 = (bf16[432,128]{1,0:T(8,128)(2,1)S(1)}, bf16[432,128]{1,0:T(8,128)(2,1)S(1)}, u32[]{:S(2)}, u32[]{:S(2)}) collective-permute-start(bf16[432,128]{1,0:T(8,128)(2,1)S(1)} %add_convert_fusion.1), channel_id=1, source_target_pairs={{0,17},{1,4},{2,7},{3,18},{4,1},{5,20},{6,23},{7,2},{8,13},{9,24},... | collective-permute-start | bytes 331784 | tf_op jit(solution)/shard_map/ppermute | solution.py:467
  36.5 3.3 %collective-permute-start.14 = (bf16[512,128]{1,0:T(8,128)(2,1)S(1)}, bf16[512,128]{1,0:T(8,128)(2,1)S(1)}, u32[]{:S(2)}, u32[]{:S(2)}) collective-permute-start(bf16[512,128]{1,0:T(8,128)(2,1)S(1)} %collective-permute-done.9.got_xy), channel_id=1, source_target_pairs={{0,1},{1,0},{2,3},{3,2},{4,5},{5,4},{6,7},{7,6},{8,9},{9,8},{10,11... | collective-permute-start | bytes 393224 | tf_op jit(solution)/shard_map/ppermute | solution.py:467
  39.8 1.4 %collective-permute-start.16 = (bf16[432,128]{1,0:T(8,128)(2,1)S(1)}, bf16[432,128]{1,0:T(8,128)(2,1)S(1)}, u32[]{:S(2)}, u32[]{:S(2)}) collective-permute-start(bf16[432,128]{1,0:T(8,128)(2,1)S(1)} %add_convert_fusion.refs_0_), channel_id=1, source_target_pairs={{0,1},{1,0},{2,3},{3,2},{4,5},{5,4},{6,7},{7,6},{8,9},{9,8},{10,11... | collective-permute-start | bytes 331784 | tf_op jit(solution)/shard_map/ppermute | solution.py:467

commit v7 on v5

--- a/solution.py
+++ b/solution.py
@@ -266,7 +266,9 @@
                 taps[(d + 5) * C : (d + 6) * C, at : at + 512] = jnp.where(
                     masks_z[d], pool_z_at(store, d, near), pool_z_at(store, d, b)
                 )
-            hidden = dot(conv, taps[:, at : at + 512])
+        both = dot(conv, taps[:, pair * 1024 : pair * 1024 + 1024])
+        for b in (2 * pair, 2 * pair + 1):
+            hidden = both[:, b % 2 * 512 : b % 2 * 512 + 512]
             gate = 0.5 * jnp.tanh(0.5 * hidden) + 0.5
             slope[b] = gate * (1.0 + hidden * (1.0 - gate))
             acts.append(hidden * gate)

time: 42.2 us -> 42.2 us (level)
  no operation moved by 1% of the time
where the time goes in v7:
time: 42.2 us; the launch traced here: 42 us
  starting transfers between devices  18.7 us (44%)
  Pallas kernels  16 us (38%)
  waiting for transfers between devices  5.61 us (13%)
  between operations  1.45 us (3%)
    ppermute x17, starting transfers between devices, send_to(): return lax.ppermute(value, ('gx', 'gy'), route(there))  18.7 us
    pallas_call x8, Pallas kernels, call(): pl.pallas_call(kernel, out_shape=[pltpu.VMEM(shape, kind) if at < keep el...  16 us
    ppermute x17, waiting for transfers between devices, send_to(): return lax.ppermute(value, ('gx', 'gy'), route(there))  5.61 us
  transfers between devices with their start and end apart: 17, of which 6 were waited for; matrix products, arithmetic and copies ran while one was open for 0% of the time, Pallas kernels for 21%

profile of v7, /device:TPU:0, one launch (start us, length us, event | category | flops | bytes accessed | tf_op | source)
XLA Modules:
  0.0 42.0 jit_solution(8656738789140464253)
XLA Ops:
  0.6 1.5 %shard_map.119 = (bf16[784,128]{1,0:T(8,128)(2,1)S(1)}, bf16[256,128]{1,0:T(8,128)(2,1)S(1)}, bf16[784,128]{1,0:T(8,128)(2,1)S(1)}, bf16[256,128]{1,0:T(8,128)(2,1)S(1)}) custom-call(s32[1,8]{1,0:T(1,128)} %cmap.1, bf16[512,512]{1,0:T(8,128)(2,1)} %bitcast.4, bf16[512,128]{1,0:T(8,128)(2,1)} %bitcast.6), custom_call_target="tpu_custom_call" | custom-call | flops 1500000000 | bytes 4500000 | tf_op jit(solution)/shard_map/pallas_call | solution.py:555
  2.1 2.5 %collective-permute-start = (bf16[784,128]{1,0:T(8,128)(2,1)S(1)}, bf16[784,128]{1,0:T(8,128)(2,1)S(1)}, u32[]{:S(2)}, u32[]{:S(2)}) collective-permute-start(bf16[784,128]{1,0:T(8,128)(2,1)S(1)} %get-tuple-element.28), channel_id=1, source_target_pairs={{0,5},{1,4},{2,7},{3,6},{4,1},{5,0},{6,3},{7,2},{8,13},{9,12},{10,... | collective-permute-start | bytes 602120 | tf_op jit(solution)/shard_map/ppermute | solution.py:468
  4.6 0.7 %collective-permute-start.3 = (bf16[784,128]{1,0:T(8,128)(2,1)S(1)}, bf16[784,128]{1,0:T(8,128)(2,1)S(1)}, u32[]{:S(2)}, u32[]{:S(2)}) collective-permute-start(bf16[784,128]{1,0:T(8,128)(2,1)S(1)} %get-tuple-element.31), channel_id=1, source_target_pairs={{0,1},{1,0},{2,3},{3,2},{4,5},{5,4},{6,7},{7,6},{8,9},{9,8},{10,11... | collective-permute-start | bytes 602120 | tf_op jit(solution)/shard_map/ppermute | solution.py:468
  5.3 0.0 collective-permute-start.1
  5.3 1.6 %collective-permute-start.2 = (bf16[256,128]{1,0:T(8,128)(2,1)S(1)}, bf16[256,128]{1,0:T(8,128)(2,1)S(1)}, u32[]{:S(2)}, u32[]{:S(2)}) collective-permute-start(bf16[256,128]{1,0:T(8,128)(2,1)S(1)} %get-tuple-element.30), channel_id=1, source_target_pairs={{0,3},{1,2},{2,1},{3,0},{4,7},{5,6},{6,5},{7,4},{8,11},{9,10},{10,... | collective-permute-start | bytes 196616 | tf_op jit(solution)/shard_map/ppermute | solution.py:468
  7.6 2.5 %shard_map.120.store = bf16[3392,512]{1,0:T(8,128)(2,1)S(1)} custom-call(s32[1]{0:T(128)S(6)} %copy.13.counts, bf16[512,512]{1,0:T(8,128)(2,1)} %bitcast.5, bf16[64,448]{1,0:T(8,128)(2,1)} %conv_ref.3, bf16[128,512]{1,0:T(8,128)(2,1)} %down_hbm.1, bf16[128,128]{1,0:T(8,128)(2,1)} %head_hbm.1), custom_call_target="tpu_custom_call" | custom-call | flops 1500000000 | bytes 4500000 | tf_op jit(solution)/shard_map/pallas_call | solution.py:555
  10.1 0.0 collective-permute-done.1.got_xb
  10.1 1.3 %collective-permute-done.got_xy = bf16[784,128]{1,0:T(8,128)(2,1)S(1)} collective-permute-done((bf16[784,128]{1,0:T(8,128)(2,1)S(1)}, bf16[784,128]{1,0:T(8,128)(2,1)S(1)}, u32[]{:S(2)}, u32[]{:S(2)}) %collective-permute-start) | collective-permute-done | bytes 200736 | tf_op jit(solution)/shard_map/ppermute | solution.py:468
  11.4 0.1 collective-permute-start.4
  11.5 1.4 %collective-permute-done.4.got_xa = bf16[784,128]{1,0:T(8,128)(2,1)S(1)} collective-permute-done((bf16[784,128]{1,0:T(8,128)(2,1)S(1)}, bf16[784,128]{1,0:T(8,128)(2,1)S(1)}, u32[]{:S(2)}, u32[]{:S(2)}) %collective-permute-start.4) | collective-permute-done | bytes 200736 | tf_op jit(solution)/shard_map/ppermute | solution.py:468
  12.9 4.7 %shard_map.121 = (bf16[512,512]{1,0:T(8,128)(2,1)S(1)}, bf16[448,128]{1,0:T(8,128)(2,1)S(1)}, bf16[448,128]{1,0:T(8,128)(2,1)S(1)}, bf16[1536,128]{1,0:T(8,128)(2,1)S(1)}) custom-call(s32[8,6]{1,0:T(8,128)} %nb_hbm.3, s32[1,8]{1,0:T(1,128)} %cmap.1, bf16[512,128]{1,0:T(8,128)(2,1)} %bitcast.7, bf16[784,128]{1,0:T(8,128)(2,1)S(1)} %collective-permute-done.4.got_xa, ...), custom_call_target="tpu_custom_call" | custom-call | flops 6000000000 | bytes 18000000 | tf_op jit(solution)/shard_map/pallas_call | solution.py:555
  17.6 0.2 collective-permute-start.5
  17.8 1.2 %collective-permute-done.5 = bf16[448,128]{1,0:T(8,128)(2,1)S(1)} collective-permute-done((bf16[448,128]{1,0:T(8,128)(2,1)S(1)}, bf16[448,128]{1,0:T(8,128)(2,1)S(1)}, u32[]{:S(2)}, u32[]{:S(2)}) %collective-permute-start.5) | collective-permute-done | bytes 114720 | tf_op jit(solution)/shard_map/ppermute | solution.py:468
  19.0 1.3 %collective-permute-start.6 = (bf16[448,128]{1,0:T(8,128)(2,1)S(1)}, bf16[448,128]{1,0:T(8,128)(2,1)S(1)}, u32[]{:S(2)}, u32[]{:S(2)}) collective-permute-start(bf16[448,128]{1,0:T(8,128)(2,1)S(1)} %add_convert_fusion.4), channel_id=1, source_target_pairs={{0,3},{1,8},{2,11},{3,0},{4,13},{5,6},{6,5},{7,14},{8,1},{9,10},{1... | collective-permute-start | bytes 344072 | tf_op jit(solution)/shard_map/ppermute | solution.py:468
  20.4 1.4 %collective-permute-start.7 = (bf16[256,128]{1,0:T(8,128)(2,1)S(1)}, bf16[256,128]{1,0:T(8,128)(2,1)S(1)}, u32[]{:S(2)}, u32[]{:S(2)}) collective-permute-start(bf16[256,128]{1,0:T(8,128)(2,1)S(1)} %get-tuple-element.53), channel_id=1, source_target_pairs={{0,1},{1,0},{2,3},{3,2},{4,8},{5,9},{6,10},{7,11},{8,4},{9,5},{10,... | collective-permute-start | bytes 196616 | tf_op jit(solution)/shard_map/ppermute | solution.py:468
  21.7 1.4 %collective-permute-start.11 = (bf16[256,128]{1,0:T(8,128)(2,1)S(1)}, bf16[256,128]{1,0:T(8,128)(2,1)S(1)}, u32[]{:S(2)}, u32[]{:S(2)}) collective-permute-start(bf16[256,128]{1,0:T(8,128)(2,1)S(1)} %get-tuple-element.41), channel_id=1, source_target_pairs={{0,4},{1,5},{2,6},{3,7},{4,0},{5,1},{6,2},{7,3},{8,12},{9,13},{10,... | collective-permute-start | bytes 196616 | tf_op jit(solution)/shard_map/ppermute | solution.py:468
  23.1 1.1 %collective-permute-start.12 = (bf16[256,128]{1,0:T(8,128)(2,1)S(1)}, bf16[256,128]{1,0:T(8,128)(2,1)S(1)}, u32[]{:S(2)}, u32[]{:S(2)}) collective-permute-start(bf16[256,128]{1,0:T(8,128)(2,1)S(1)} %get-tuple-element.42), channel_id=1, source_target_pairs={{0,3},{1,2},{2,1},{3,0},{4,7},{5,6},{6,5},{7,4},{8,11},{9,10},{10,... | collective-permute-start | bytes 196616 | tf_op jit(solution)/shard_map/ppermute | solution.py:468
  24.3 2.0 %collective-permute-start.8 = (bf16[448,128]{1,0:T(8,128)(2,1)S(1)}, bf16[448,128]{1,0:T(8,128)(2,1)S(1)}, u32[]{:S(2)}, u32[]{:S(2)}) collective-permute-start(bf16[448,128]{1,0:T(8,128)(2,1)S(1)} %add_convert_fusion.3), channel_id=1, source_target_pairs={{0,9},{1,2},{2,1},{3,10},{4,7},{5,12},{6,15},{7,4},{8,11},{9,0},{1... | collective-permute-start | bytes 344072 | tf_op jit(solution)/shard_map/ppermute | solution.py:468
  26.3 2.0 %shard_map.122.moved_ref = bf16[2048,512]{1,0:T(8,128)(2,1)S(1)} custom-call(s32[8,6]{1,0:T(8,128)} %nb_hbm.3, bf16[512,512]{1,0:T(8,128)(2,1)S(1)} %get-tuple-element.37.hg_ref), custom_call_target="tpu_custom_call" | custom-call | flops 2500000000 | bytes 7500000 | tf_op jit(solution)/shard_map/pallas_call | solution.py:555
  28.3 0.4 collective-permute-done.8
  28.8 1.7 %collective-permute-start.13 = (bf16[448,128]{1,0:T(8,128)(2,1)S(1)}, bf16[448,128]{1,0:T(8,128)(2,1)S(1)}, u32[]{:S(2)}, u32[]{:S(2)}) collective-permute-start(bf16[448,128]{1,0:T(8,128)(2,1)S(1)} %add_convert_fusion.2), channel_id=1, source_target_pairs={{0,5},{1,16},{2,19},{3,6},{4,21},{5,0},{6,3},{7,22},{8,25},{9,12},... | collective-permute-start | bytes 344072 | tf_op jit(solution)/shard_map/ppermute | solution.py:468
  30.6 1.1 %shard_map.123.near_ref = f32[512,512]{1,0:T(8,128)S(1)} custom-call(bf16[512,512]{1,0:T(8,128)(2,1)S(1)} %get-tuple-element.37.hg_ref, bf16[2048,512]{1,0:T(8,128)(2,1)S(1)} %shard_map.122.moved_ref, bf16[64,448]{1,0:T(8,128)(2,1)S(1)} %copy-done), custom_call_target="tpu_custom_call" | custom-call | flops 1000000000 | bytes 3000000 | tf_op jit(solution)/shard_map/pallas_call | solution.py:555
  31.7 0.1 collective-permute-start.9
  31.8 1.3 %collective-permute-done.13 = bf16[448,128]{1,0:T(8,128)(2,1)S(1)} collective-permute-done((bf16[448,128]{1,0:T(8,128)(2,1)S(1)}, bf16[448,128]{1,0:T(8,128)(2,1)S(1)}, u32[]{:S(2)}, u32[]{:S(2)}) %collective-permute-start.13) | collective-permute-done | bytes 114720 | tf_op jit(solution)/shard_map/ppermute | solution.py:468
  33.1 0.0 copy-start.1
  33.2 3.5 %collective-permute-start.15 = (bf16[448,128]{1,0:T(8,128)(2,1)S(1)}, bf16[448,128]{1,0:T(8,128)(2,1)S(1)}, u32[]{:S(2)}, u32[]{:S(2)}) collective-permute-start(bf16[448,128]{1,0:T(8,128)(2,1)S(1)} %add_convert_fusion.1), channel_id=1, source_target_pairs={{0,17},{1,4},{2,7},{3,18},{4,1},{5,20},{6,23},{7,2},{8,13},{9,24},... | collective-permute-start | bytes 344072 | tf_op jit(solution)/shard_map/ppermute | solution.py:468
  36.7 1.0 %collective-permute-start.14 = (bf16[512,128]{1,0:T(8,128)(2,1)S(1)}, bf16[512,128]{1,0:T(8,128)(2,1)S(1)}, u32[]{:S(2)}, u32[]{:S(2)}) collective-permute-start(bf16[512,128]{1,0:T(8,128)(2,1)S(1)} %collective-permute-done.9.got_xy), channel_id=1, source_target_pairs={{0,1},{1,0},{2,3},{3,2},{4,5},{5,4},{6,7},{7,6},{8,9},{9,8},{10,11... | collective-permute-start | bytes 393224 | tf_op jit(solution)/shard_map/ppermute | solution.py:468
  37.7 1.9 %shard_map.125 = bf16[512,512]{1,0:T(8,128)(2,1)} custom-call(s32[1]{0:T(128)S(6)} %copy.13.counts, f32[512,512]{1,0:T(8,128)S(1)} %shard_map.123.near_ref, bf16[256,128]{1,0:T(8,128)(2,1)S(1)} %collective-permute-done.11.got_xa, bf16[256,128]{1,0:T(8,128)(2,1)S(1)} %collective-permute-done.7.got_xb, bf16[768,128]{1,0:T(8,128)(2,1)S(1)} %collective-permute-done.10.got_ya, ...), custom_call_target="tpu_custom_call" | custom-call | flops 1800000000 | bytes 5400000 | tf_op jit(solution)/shard_map/pallas_call | solution.py:555
  39.6 0.1 collective-permute-start.16
  39.7 1.2 %shard_map.124 = bf16[512,128]{1,0:T(8,128)(2,1)} custom-call(s32[1,8]{1,0:T(1,128)S(1)} %copy-done.1, bf16[1536,128]{1,0:T(8,128)(2,1)S(1)} %get-tuple-element.33.own, bf16[512,128]{1,0:T(8,128)(2,1)S(1)} %collective-permute-done.14.got_x, bf16[768,128]{1,0:T(8,128)(2,1)S(1)} %collective-permute-done.10.got_ya, ...), custom_call_target="tpu_custom_call" | custom-call | flops 1200000000 | bytes 3600000 | tf_op jit(solution)/shard_map/pallas_call | solution.py:555
  40.9 0.1 collective-permute-done.16.refs_1_
  41.0 1.0 %shard_map.126 = (f32[64,448]{1,0:T(8,128)}, f32[128,512]{1,0:T(8,128)}, f32[128,128]{1,0:T(8,128)}) custom-call(bf16[448,128]{1,0:T(8,128)(2,1)S(1)} %add_convert_fusion.refs_0_, bf16[448,128]{1,0:T(8,128)(2,1)S(1)} %collective-permute-done.16.refs_1_), custom_call_target="tpu_custom_call" | custom-call | flops 1000000000 | bytes 3000000 | tf_op jit(solution)/shard_map/pallas_call | solution.py:555
  (22 shorter events, 0.2 us)
Async XLA Ops:
  2.1 9.3 %collective-permute-start = (bf16[784,128]{1,0:T(8,128)(2,1)S(1)}, bf16[784,128]{1,0:T(8,128)(2,1)S(1)}, u32[]{:S(2)}, u32[]{:S(2)}) collective-permute-start(bf16[784,128]{1,0:T(8,128)(2,1)S(1)} %get-tuple-element.28), channel_id=1, source_target_pairs={{0,5},{1,4},{2,7},{3,6},{4,1},{5,0},{6,3},{7,2},{8,13},{9,12},{10,... | collective-permute-start | bytes 602120 | tf_op jit(solution)/shard_map/ppermute | solution.py:468
  4.6 6.8 %collective-permute-start.3 = (bf16[784,128]{1,0:T(8,128)(2,1)S(1)}, bf16[784,128]{1,0:T(8,128)(2,1)S(1)}, u32[]{:S(2)}, u32[]{:S(2)}) collective-permute-start(bf16[784,128]{1,0:T(8,128)(2,1)S(1)} %get-tuple-element.31), channel_id=1, source_target_pairs={{0,1},{1,0},{2,3},{3,2},{4,5},{5,4},{6,7},{7,6},{8,9},{9,8},{10,11... | collective-permute-start | bytes 602120 | tf_op jit(solution)/shard_map/ppermute | solution.py:468
  5.3 4.8 %collective-permute-start.1 = (bf16[256,128]{1,0:T(8,128)(2,1)S(1)}, bf16[256,128]{1,0:T(8,128)(2,1)S(1)}, u32[]{:S(2)}, u32[]{:S(2)}) collective-permute-start(bf16[256,128]{1,0:T(8,128)(2,1)S(1)} %get-tuple-element.29), channel_id=1, source_target_pairs={{0,1},{1,0},{2,3},{3,2},{4,8},{5,9},{6,10},{7,11},{8,4},{9,5},{10,... | collective-permute-start | bytes 196616 | tf_op jit(solution)/shard_map/ppermute | solution.py:468
  5.3 4.8 %collective-permute-start.2 = (bf16[256,128]{1,0:T(8,128)(2,1)S(1)}, bf16[256,128]{1,0:T(8,128)(2,1)S(1)}, u32[]{:S(2)}, u32[]{:S(2)}) collective-permute-start(bf16[256,128]{1,0:T(8,128)(2,1)S(1)} %get-tuple-element.30), channel_id=1, source_target_pairs={{0,3},{1,2},{2,1},{3,0},{4,7},{5,6},{6,5},{7,4},{8,11},{9,10},{10,... | collective-permute-start | bytes 196616 | tf_op jit(solution)/shard_map/ppermute | solution.py:468
  11.4 1.4 %collective-permute-start.4 = (bf16[784,128]{1,0:T(8,128)(2,1)S(1)}, bf16[784,128]{1,0:T(8,128)(2,1)S(1)}, u32[]{:S(2)}, u32[]{:S(2)}) collective-permute-start(bf16[784,128]{1,0:T(8,128)(2,1)S(1)} %collective-permute-done.got_xy), channel_id=1, source_target_pairs={{0,1},{1,0},{2,3},{3,2},{4,5},{5,4},{6,7},{7,6},{8,9},{9,8},{10,11... | collective-permute-start | bytes 602120 | tf_op jit(solution)/shard_map/ppermute | solution.py:468
  17.6 1.4 %collective-permute-start.5 = (bf16[448,128]{1,0:T(8,128)(2,1)S(1)}, bf16[448,128]{1,0:T(8,128)(2,1)S(1)}, u32[]{:S(2)}, u32[]{:S(2)}) collective-permute-start(bf16[448,128]{1,0:T(8,128)(2,1)S(1)} %get-tuple-element.36), channel_id=1, source_target_pairs={{0,1},{1,0},{2,3},{3,2},{4,5},{5,4},{6,7},{7,6},{8,9},{9,8},{10,11... | collective-permute-start | bytes 344072 | tf_op jit(solution)/shard_map/ppermute | solution.py:468
  19.0 5.2 %collective-permute-start.6 = (bf16[448,128]{1,0:T(8,128)(2,1)S(1)}, bf16[448,128]{1,0:T(8,128)(2,1)S(1)}, u32[]{:S(2)}, u32[]{:S(2)}) collective-permute-start(bf16[448,128]{1,0:T(8,128)(2,1)S(1)} %add_convert_fusion.4), channel_id=1, source_target_pairs={{0,3},{1,8},{2,11},{3,0},{4,13},{5,6},{6,5},{7,14},{8,1},{9,10},{1... | collective-permute-start | bytes 344072 | tf_op jit(solution)/shard_map/ppermute | solution.py:468
  20.4 5.9 %collective-permute-start.7 = (bf16[256,128]{1,0:T(8,128)(2,1)S(1)}, bf16[256,128]{1,0:T(8,128)(2,1)S(1)}, u32[]{:S(2)}, u32[]{:S(2)}) collective-permute-start(bf16[256,128]{1,0:T(8,128)(2,1)S(1)} %get-tuple-element.53), channel_id=1, source_target_pairs={{0,1},{1,0},{2,3},{3,2},{4,8},{5,9},{6,10},{7,11},{8,4},{9,5},{10,... | collective-permute-start | bytes 196616 | tf_op jit(solution)/shard_map/ppermute | solution.py:468
  21.7 7.1 %collective-permute-start.11 = (bf16[256,128]{1,0:T(8,128)(2,1)S(1)}, bf16[256,128]{1,0:T(8,128)(2,1)S(1)}, u32[]{:S(2)}, u32[]{:S(2)}) collective-permute-start(bf16[256,128]{1,0:T(8,128)(2,1)S(1)} %get-tuple-element.41), channel_id=1, source_target_pairs={{0,4},{1,5},{2,6},{3,7},{4,0},{5,1},{6,2},{7,3},{8,12},{9,13},{10,... | collective-permute-start | bytes 196616 | tf_op jit(solution)/shard_map/ppermute | solution.py:468
  23.1 5.7 %collective-permute-start.12 = (bf16[256,128]{1,0:T(8,128)(2,1)S(1)}, bf16[256,128]{1,0:T(8,128)(2,1)S(1)}, u32[]{:S(2)}, u32[]{:S(2)}) collective-permute-start(bf16[256,128]{1,0:T(8,128)(2,1)S(1)} %get-tuple-element.42), channel_id=1, source_target_pairs={{0,3},{1,2},{2,1},{3,0},{4,7},{5,6},{6,5},{7,4},{8,11},{9,10},{10,... | collective-permute-start | bytes 196616 | tf_op jit(solution)/shard_map/ppermute | solution.py:468
  24.3 4.5 %collective-permute-start.8 = (bf16[448,128]{1,0:T(8,128)(2,1)S(1)}, bf16[448,128]{1,0:T(8,128)(2,1)S(1)}, u32[]{:S(2)}, u32[]{:S(2)}) collective-permute-start(bf16[448,128]{1,0:T(8,128)(2,1)S(1)} %add_convert_fusion.3), channel_id=1, source_target_pairs={{0,9},{1,2},{2,1},{3,10},{4,7},{5,12},{6,15},{7,4},{8,11},{9,0},{1... | collective-permute-start | bytes 344072 | tf_op jit(solution)/shard_map/ppermute | solution.py:468
  26.3 4.3 %copy-start = (bf16[64,448]{1,0:T(8,128)(2,1)S(1)}, bf16[64,448]{1,0:T(8,128)(2,1)}, u32[]{:S(2)}) copy-start(bf16[64,448]{1,0:T(8,128)(2,1)} %conv_ref.3) | copy-start | bytes 172036
  26.3 2.5 %collective-permute-start.10 = (bf16[768,128]{1,0:T(8,128)(2,1)S(1)}, bf16[768,128]{1,0:T(8,128)(2,1)S(1)}, u32[]{:S(2)}, u32[]{:S(2)}) collective-permute-start(bf16[768,128]{1,0:T(8,128)(2,1)S(1)} %slice.17), channel_id=1, source_target_pairs={{0,1},{1,0},{2,3},{3,2},{4,5},{5,4},{6,7},{7,6},{8,9},{9,8},{10,11... | collective-permute-start | bytes 589832 | tf_op jit(solution)/shard_map/ppermute | solution.py:468
  28.8 4.3 %collective-permute-start.13 = (bf16[448,128]{1,0:T(8,128)(2,1)S(1)}, bf16[448,128]{1,0:T(8,128)(2,1)S(1)}, u32[]{:S(2)}, u32[]{:S(2)}) collective-permute-start(bf16[448,128]{1,0:T(8,128)(2,1)S(1)} %add_convert_fusion.2), channel_id=1, source_target_pairs={{0,5},{1,16},{2,19},{3,6},{4,21},{5,0},{6,3},{7,22},{8,25},{9,12},... | collective-permute-start | bytes 344072 | tf_op jit(solution)/shard_map/ppermute | solution.py:468
  31.7 5.0 %collective-permute-start.9 = (bf16[512,128]{1,0:T(8,128)(2,1)S(1)}, bf16[512,128]{1,0:T(8,128)(2,1)S(1)}, u32[]{:S(2)}, u32[]{:S(2)}) collective-permute-start(bf16[512,128]{1,0:T(8,128)(2,1)S(1)} %slice.15), channel_id=1, source_target_pairs={{0,5},{1,4},{2,7},{3,6},{4,1},{5,0},{6,3},{7,2},{8,13},{9,12},{10,... | collective-permute-start | bytes 393224 | tf_op jit(solution)/shard_map/ppermute | solution.py:468
  33.1 6.5 %copy-start.1 = (s32[1,8]{1,0:T(1,128)S(1)}, s32[1,8]{1,0:T(1,128)}, u32[]{:S(2)}) copy-start(s32[1,8]{1,0:T(1,128)} %cmap.1) | copy-start | bytes 100
  33.2 6.4 %collective-permute-start.15 = (bf16[448,128]{1,0:T(8,128)(2,1)S(1)}, bf16[448,128]{1,0:T(8,128)(2,1)S(1)}, u32[]{:S(2)}, u32[]{:S(2)}) collective-permute-start(bf16[448,128]{1,0:T(8,128)(2,1)S(1)} %add_convert_fusion.1), channel_id=1, source_target_pairs={{0,17},{1,4},{2,7},{3,18},{4,1},{5,20},{6,23},{7,2},{8,13},{9,24},... | collective-permute-start | bytes 344072 | tf_op jit(solution)/shard_map/ppermute | solution.py:468
  36.7 2.9 %collective-permute-start.14 = (bf16[512,128]{1,0:T(8,128)(2,1)S(1)}, bf16[512,128]{1,0:T(8,128)(2,1)S(1)}, u32[]{:S(2)}, u32[]{:S(2)}) collective-permute-start(bf16[512,128]{1,0:T(8,128)(2,1)S(1)} %collective-permute-done.9.got_xy), channel_id=1, source_target_pairs={{0,1},{1,0},{2,3},{3,2},{4,5},{5,4},{6,7},{7,6},{8,9},{9,8},{10,11... | collective-permute-start | bytes 393224 | tf_op jit(solution)/shard_map/ppermute | solution.py:468
  39.6 1.4 %collective-permute-start.16 = (bf16[448,128]{1,0:T(8,128)(2,1)S(1)}, bf16[448,128]{1,0:T(8,128)(2,1)S(1)}, u32[]{:S(2)}, u32[]{:S(2)}) collective-permute-start(bf16[448,128]{1,0:T(8,128)(2,1)S(1)} %add_convert_fusion.refs_0_), channel_id=1, source_target_pairs={{0,1},{1,0},{2,3},{3,2},{4,5},{5,4},{6,7},{7,6},{8,9},{9,8},{10,11... | collective-permute-start | bytes 344072 | tf_op jit(solution)/shard_map/ppermute | solution.py:468
